TPU v7x, 32 devices: a whole 2x2x4 slice. The times are simulated.
32 devices in a mesh: tm: 2 (over x), space: 16 (over z, y, core).
Axes of the slice: x: 2, y: 2, z: 4, core: 2. Of those that a mesh axis runs over, the one named last changes fastest.
Arguments:
- flux: float32 [2, 65536], P('tm', 'space'), may hold values from -6 to 6
- noise: float32 [2, 65536], P('tm', 'space'), may hold values from -6 to 6
- prior_scale: float32 [65536], P('space'), may hold values from 0.3 to 3
- footprints: bfloat16 [2, 512, 32, 4096], P('tm', 'space'), may hold values from -0.09375 to 0.09375
- soundings: bfloat16 [2, 512, 32], P('tm', 'space'), may hold values from -6 to 6
- targets: int32 [2, 512, 1], P('tm', 'space'), may hold values from 0 to 15; in each aligned block of 32 rows (0 to 31, 32 to 63, ..., all dimensions but the last counted through in order) at most 4 rows name the same one
- basis: bfloat16 [65536, 256], P('space'), may hold values from -68 to 68
Outputs:
- proposal: float32 [2, 65536], P('tm', 'space')
- predicted: float32 [2, 512, 32], P('tm', 'space')
- info_factor: float32 [256, 256], replicated
- whitened_rhs: float32 [256], replicated
Inputs may be any that keep to these rules, and one draw needn't show every extreme that they name: `targets`: in the rows of one device no tile is named more than 4 times, and in every draw some device names some tile exactly 4 times.
All inputs are finite; a program needn't handle non-finite values.
Results may differ from a plain program's by a relative error of at most 0.0047.
Values may be sent and summed in bfloat16 or wider, within the bound.
No kernel may reach another device: no remote copies, remote signals or barrier semaphores. Data moves between devices by JAX's collectives and lax.ppermute only.
A program may use at most 128 MiB of HBM per device.

v0:
```python
import jax
import jax.numpy as jnp
from jax import lax
from jax.sharding import PartitionSpec as P

PATCH = 64
REACH = 8


BETA = 0.6
KEEP = 0.8


def padded(shard, sides, width):
    for axis, dim in sides:
        devices, length = (lax.axis_size(axis), shard.shape[dim])
        up = [(i, (i + 1) % devices) for i in range(devices - 1)]
        down = [(j, i) for i, j in up]
        last = lax.slice_in_dim(shard, length - width, length, axis=dim)
        leading = lax.slice_in_dim(shard, 0, width, axis=dim)
        before = lax.ppermute(last, axis, up)
        after = lax.ppermute(leading, axis, down)
        shard = jnp.concatenate([before, shard, after], axis=dim)
    return shard


def kernel_weights(reach):
    offsets = jnp.abs(jnp.arange(-reach, reach + 1).astype(jnp.float32))
    profile = (1.0 + 2.0 * offsets / reach) * jnp.exp(-2.0 * offsets / reach)
    return profile / jnp.sqrt(jnp.sum(profile * profile))


def finish_factor(gram_sum, projected):
    information = jnp.eye(gram_sum.shape[0], dtype=jnp.float32) + gram_sum
    factor_low = jnp.linalg.cholesky(information)
    rhs_value = jax.scipy.linalg.solve_triangular(factor_low, projected, lower=True)
    return (factor_low.T, rhs_value)


def per_device(flux, noise, prior_scale, footprints, soundings, targets, basis):
    tile_count = lax.axis_size("space")
    step_count = lax.axis_size("tm")
    block_count = footprints.shape[1]
    obs_count = footprints.shape[2]
    cell_count = footprints.shape[3]
    patch_edge = PATCH
    capacity = max(2, (2 * block_count + tile_count - 1) // tile_count)
    slot_count = tile_count * capacity
    weights = kernel_weights(REACH)
    extended = padded(noise, (("space", 1),), REACH * patch_edge)
    extended_grid = extended.reshape(patch_edge + 2 * REACH, patch_edge)
    row_offset = jnp.arange(patch_edge + 2 * REACH)[None, :] - jnp.arange(patch_edge)[:, None]
    col_offset = (
        jnp.arange(patch_edge)[:, None] - jnp.arange(patch_edge)[None, :] + REACH
    ) % patch_edge
    row_band = jnp.zeros((patch_edge, patch_edge + 2 * REACH), jnp.float32)
    col_circulant = jnp.zeros((patch_edge, patch_edge), jnp.float32)
    for position in range(2 * REACH + 1):
        row_band = row_band + weights[position] * (row_offset == position).astype(jnp.float32)
        col_circulant = col_circulant + weights[position] * (col_offset == position).astype(
            jnp.float32
        )
    along_rows = jnp.dot(row_band, extended_grid, precision=lax.Precision.HIGHEST)
    smooth = jnp.dot(along_rows, col_circulant, precision=lax.Precision.HIGHEST)
    proposal = KEEP * flux + BETA * prior_scale[None, :] * smooth.reshape(1, cell_count)
    destination = targets[0, :, 0]
    dest_onehot = (destination[:, None] == jnp.arange(tile_count)[None, :]).astype(jnp.int32)
    earlier = jnp.cumsum(dest_onehot, axis=0) - dest_onehot
    slot_rank = jnp.sum(earlier * dest_onehot, axis=1)
    slot_of = destination * capacity + slot_rank
    slot_match = slot_of[None, :] == jnp.arange(slot_count)[:, None]
    source_of = jnp.sum(jnp.where(slot_match, jnp.arange(block_count)[None, :] + 1, 0), axis=1) - 1
    source_of = jnp.where(source_of < 0, block_count, source_of)
    outgoing = jnp.take(footprints[0], source_of, axis=0, mode="fill", fill_value=0)
    sent_obs = jnp.take(soundings[0], source_of, axis=0, mode="fill", fill_value=0)
    outgoing = outgoing.reshape(tile_count, capacity, obs_count, cell_count)
    sent_obs = sent_obs.reshape(tile_count, capacity, obs_count)
    tile_half = proposal[0].astype(jnp.bfloat16)
    jac_scale = float(step_count * tile_count * block_count * obs_count) ** (-0.5)
    arrived, arrived_obs = (
        lax.all_to_all(outgoing, "space", split_axis=0, concat_axis=0, tiled=True),
        lax.all_to_all(sent_obs, "space", split_axis=0, concat_axis=0, tiled=True),
    )
    block_rows = arrived.reshape(slot_count * obs_count, cell_count)
    predicted_rows = jnp.dot(block_rows, tile_half, preferred_element_type=jnp.float32)
    jacobian = (jnp.dot(block_rows, basis, preferred_element_type=jnp.float32) * jac_scale).astype(
        jnp.bfloat16
    )
    misfit = arrived_obs.reshape(-1).astype(jnp.float32) - predicted_rows
    gram_sum = jnp.einsum("ra,rb->ab", jacobian, jacobian, preferred_element_type=jnp.float32)
    projected = jnp.dot(jacobian.astype(jnp.float32).T, misfit, precision=lax.Precision.HIGHEST)
    returned = lax.all_to_all(
        predicted_rows.reshape(tile_count, capacity, obs_count),
        "space",
        split_axis=0,
        concat_axis=0,
        tiled=True,
    )
    own_predicted = jnp.take(returned.reshape(slot_count, obs_count), slot_of, axis=0)
    tile_gram, tile_proj = lax.psum((gram_sum, projected), "space")
    window_gram, window_proj = lax.psum((tile_gram, tile_proj), "tm")
    factor_up, rhs_value = finish_factor(window_gram, window_proj)
    return (proposal, own_predicted[None], factor_up, rhs_value)


def solution(mesh):
    return jax.shard_map(
        per_device,
        mesh=mesh,
        in_specs=(
            P("tm", "space"),
            P("tm", "space"),
            P("space"),
            P("tm", "space", None, None),
            P("tm", "space", None),
            P("tm", "space", None),
            P("space", None),
        ),
        out_specs=(P("tm", "space"), P("tm", "space", None), P(), P()),
        check_vma=False,
    )
```

profile of v0, /device:TPU:0, one launch (start us, length us, event | category | flops | bytes accessed | tf_op | source)
XLA Modules:
  0.0 642.6 jit_solution(14513302548699186011)
XLA Ops:
  7.2 0.9 fusion.138
  8.1 0.8 select_reduce_fusion.3
  9.9 1.3 gather_fusion.2
  11.2 0.7 broadcast_select_fusion.1
  11.8 7.4 %all-to-all-start.2 = ((bf16[16,4,32]{2,1,0:T(4,128)(2,1)}), bf16[16,4,32]{2,1,0:T(4,128)(2,1)S(1)}, u32[]{:S(2)}, u32[]{:S(2)}) async-start(bf16[16,4,32]{2,1,0:T(4,128)(2,1)} %broadcast_select_fusion.1), calls=%async_computation.2 | async-start | bytes 32768 | tf_op jit(solution)/shard_map/all_to_all | solution.py:82
  19.2 10.8 %gather_fusion = bf16[64,32,4096]{2,1,0:T(8,128)(2,1)} fusion(bf16[32,32,4096]{2,1,0:T(8,128)(2,1)} %bitcast.111, s32[1024]{0:T(1024)S(1)} %pad_clamp_fusion.1), kind=kCustom, calls=%fused_computation | custom fusion | bytes 33554688 | tf_op jit(solution)/shard_map/jit(_take)/gather | solution.py:74
  30.0 14.0 %broadcast_select_fusion = bf16[16,4,32,4096]{3,2,1,0:T(8,128)(2,1)} fusion(bf16[16,4,32,4096]{3,2,1,0:T(8,128)(2,1)} %bitcast.110, pred[16,4]{1,0:T(8,128)(4,1)S(1)} %compare_and_fusion), kind=kLoop, calls=%fused_computation.5 | loop fusion | flops 8388608 | bytes 33554496 | tf_op jit(solution)/shard_map/jit(_take)/select_n | solution.py:74
  44.1 6.2 all-to-all-start
  50.3 2.3 collective-permute-start
  52.6 1.3 collective-permute-start.1
  55.3 0.7 fusion.255
  56.0 0.8 collective-permute-done.1
  56.9 10.6 %fusion.47 = f32[64,64]{1,0:T(8,128)S(1)} fusion(f32[80,64]{1,0:T(8,128)S(1)} %reshape.174, f32[]{:T(128)} %bitcast.16, f32[]{:T(128)} %bitcast.15, f32[]{:T(128)} %bitcast.14, f32[]{:T(128)} %bitcast.13, f32[]{:T(128)} %bitcast.12, f32[]{:T(128)} %bitcast.11, f32[]{:T(128)} %bitcast.10, f32[]{:T(128)} %bitcast.9, f32[]{:T(128)} %bitcast.8, f32[]{:T(128)} %bitcast.7, ...), kind=kOutput, calls=%fused_computation.73 | convolution fusion | flops 4193280 | bytes 36932 | tf_op jit(solution)/shard_map/dot_general | solution.py:63
  67.5 10.6 %fusion.13 = f32[64,64]{1,0:T(8,128)S(1)} fusion(f32[64,64]{1,0:T(8,128)S(1)} %fusion.47, f32[]{:T(128)} %bitcast.16, f32[]{:T(128)} %bitcast.15, f32[]{:T(128)} %bitcast.14, f32[]{:T(128)} %bitcast.13, f32[]{:T(128)} %bitcast.12, f32[]{:T(128)} %bitcast.11, f32[]{:T(128)} %bitcast.10, f32[]{:T(128)} %bitcast.9, f32[]{:T(128)} %bitcast.8, f32[]{:T(128)} %bitcast.7, ...), kind=kOutput, calls=%fused_computation.39 | convolution fusion | flops 3403776 | bytes 32836 | tf_op jit(solution)/shard_map/dot_general | solution.py:64
  78.4 268.6 %all-to-all-done = bf16[16,4,32,4096]{3,2,1,0:T(8,128)(2,1)} async-done(((bf16[16,4,32,4096]{3,2,1,0:T(8,128)(2,1)}), bf16[16,4,32,4096]{3,2,1,0:T(8,128)(2,1)}, u32[]{:S(2)}, u32[]{:S(2)}) %all-to-all-start) | async-done | bytes 16777248 | tf_op jit(solution)/shard_map/all_to_all | solution.py:81
  347.0 8.3 %fusion = bf16[2048,256]{1,0:T(8,128)(2,1)S(1)} fusion(bf16[2048,4096]{1,0:T(8,128)(2,1)} %bitcast.23, bf16[4096,256]{1,0:T(8,128)(2,1)S(1)} %copy-done), kind=kOutput, calls=%fused_computation.7 | convolution fusion | flops 4296015872 | bytes 19922944 | tf_op jit(solution)/shard_map/dot_general | solution.py:86
  355.3 1.2 fusion.256
  356.6 10.2 %fusion.135 = f32[1,2048]{1,0:T(1,128)S(1)} fusion(bf16[2048,4096]{1,0:T(8,128)(2,1)} %bitcast.23, f32[1,4096]{1,0:T(1,128)S(1)} %multiply_add_fusion), kind=kOutput, calls=%fused_computation.148 | convolution fusion | flops 16781312 | bytes 16801792 | tf_op jit(solution)/shard_map/dot_general | solution.py:85
  367.6 90.9 %all-to-all-start.1 = ((f32[16,1,128]{2,1,0:T(1,128)}), f32[16,1,128]{2,1,0:T(1,128)S(1)}, u32[]{:S(2)}, u32[]{:S(2)}) async-start(f32[16,1,128]{2,1,0:T(1,128)} %reshape.241), calls=%async_computation.1 | async-start | bytes 16384 | tf_op jit(solution)/shard_map/all_to_all | solution.py:92
  458.6 73.2 %all-reduce.4.cloned.1.call-done = f32[256,256]{0,1:T(8,128)} async-done(((f32[256,256]{0,1:T(8,128)}), f32[256,256]{0,1:T(8,128)}) %all-reduce.4.cloned.1.call-update) | async-done | bytes 262160 | tf_op jit(solution)/shard_map/psum | solution.py:100
  532.3 32.0 %psum.30 = f32[256]{0:T(256)S(1)} all-reduce(f32[256]{0:T(256)S(1)} %bitcast.121), channel_id=1, replica_groups=mesh['tm'=2,'space'=16] {'space'}, use_global_device_ids=true, to_apply=%region_10.11 | all-reduce | flops 256 | bytes 2048 | tf_op jit(solution)/shard_map/psum | solution.py:100
  564.3 5.1 psum.31
  571.9 1.0 convert_add_fusion
  573.0 1.0 fusion.5
  574.1 11.7 %cholesky.50 = f32[128,128]{1,0:T(8,128)S(1)} custom-call(f32[128,128]{1,0:T(8,128)S(1)} %cholesky.118), custom_call_target="Cholesky" | custom-call | tf_op jit(solution)/shard_map/jit(cholesky)/cholesky | solution.py:35
  585.8 9.8 %custom-call.15 = f32[1,128,128]{1,2,0:T(8,128)S(1)} custom-call(f32[1,128,128]{2,1,0:T(8,128)S(1)} %get-tuple-element.41), custom_call_target="InvertDiagBlocksLowerTriangular" | custom-call | tf_op jit(solution)/shard_map/jit(cholesky)/cholesky | solution.py:35
  596.1 11.7 %cholesky.105 = f32[128,128]{1,0:T(8,128)S(1)} custom-call(f32[128,128]{1,0:T(8,128)S(1)} %convolution_subtract_fusion), custom_call_target="Cholesky" | custom-call | tf_op jit(solution)/shard_map/jit(cholesky)/cholesky | solution.py:35
  609.9 4.2 while.1
  610.7 1.4 bitcast_dynamic-update-slice_fusion.2
  612.7 1.4 bitcast_dynamic-update-slice_fusion.2
  614.1 19.7 %custom-call.16 = f32[2,128,128]{1,2,0:T(8,128)S(1)} custom-call(f32[2,128,128]{2,1,0:T(8,128)S(1)} %get-tuple-element.11), custom_call_target="InvertDiagBlocksLowerTriangular" | custom-call | tf_op jit(solution)/shard_map/jit(_solve_triangular)/triangular_solve | solution.py:36
  634.9 0.8 copy.19
  (69 shorter events, 9.6 us)
Async XLA Ops:
  7.2 339.9 %copy-start = (bf16[4096,256]{1,0:T(8,128)(2,1)S(1)}, bf16[4096,256]{1,0:T(8,128)(2,1)}, u32[]{:S(2)}) copy-start(bf16[4096,256]{1,0:T(8,128)(2,1)} %param.13) | copy-start | bytes 6291460
  11.8 32.2 %all-to-all-start.2 = ((bf16[16,4,32]{2,1,0:T(4,128)(2,1)}), bf16[16,4,32]{2,1,0:T(4,128)(2,1)S(1)}, u32[]{:S(2)}, u32[]{:S(2)}) async-start(bf16[16,4,32]{2,1,0:T(4,128)(2,1)} %broadcast_select_fusion.1), calls=%async_computation.2 | async-start | bytes 32768 | tf_op jit(solution)/shard_map/all_to_all | solution.py:82
  44.0 6.3 copy-start.2
  44.0 11.2 %copy-start.5 = (s32[1,32,1]{1,2,0:T(1,128)S(1)}, s32[1,32,1]{1,2,0:T(1,128)}, u32[]{:S(2)}) copy-start(s32[1,32,1]{1,2,0:T(1,128)} %param.12) | copy-start | bytes 388
  44.0 34.2 %copy-start.3 = (f32[4096]{0:T(1024)S(1)}, f32[4096]{0:T(1024)}, u32[]{:S(2)}) copy-start(f32[4096]{0:T(1024)} %param.9) | copy-start | bytes 49156
  44.0 34.2 %copy-start.4 = (f32[1,4096]{1,0:T(1,128)S(1)}, f32[1,4096]{1,0:T(1,128)}, u32[]{:S(2)}) copy-start(f32[1,4096]{1,0:T(1,128)} %param.7) | copy-start | bytes 49156
  44.1 303.0 %all-to-all-start = ((bf16[16,4,32,4096]{3,2,1,0:T(8,128)(2,1)}), bf16[16,4,32,4096]{3,2,1,0:T(8,128)(2,1)}, u32[]{:S(2)}, u32[]{:S(2)}) async-start(bf16[16,4,32,4096]{3,2,1,0:T(8,128)(2,1)} %broadcast_select_fusion), calls=%async_computation | async-start | bytes 33554432 | tf_op jit(solution)/shard_map/all_to_all | solution.py:81
  50.3 481.5 %all-reduce.4.cloned.1.call-start = ((), (), s32[]{:S(2)}) async-start(), calls=%async_computation.3 | async-start | bytes 524288 | tf_op jit(solution)/shard_map/psum | solution.py:100
  50.3 5.7 collective-permute-start
  52.6 4.2 collective-permute-start.1
  78.3 288.5 %copy-start.1 = (f32[1,4096]{1,0:T(1,128)}, f32[1,4096]{1,0:T(1,128)S(1)}, u32[]{:S(2)}) copy-start(f32[1,4096]{1,0:T(1,128)S(1)} %multiply_add_fusion) | copy-start | bytes 49156
  367.6 201.8 %all-to-all-start.1 = ((f32[16,1,128]{2,1,0:T(1,128)}), f32[16,1,128]{2,1,0:T(1,128)S(1)}, u32[]{:S(2)}, u32[]{:S(2)}) async-start(f32[16,1,128]{2,1,0:T(1,128)} %reshape.241), calls=%async_computation.1 | async-start | bytes 16384 | tf_op jit(solution)/shard_map/all_to_all | solution.py:92
  458.5 113.4 %all-reduce.6.cloned.1.call-start = ((), (), s32[]{:S(2)}) async-start(), calls=%async_computation.4 | async-start | bytes 524288 | tf_op jit(solution)/shard_map/psum | solution.py:101
Sparse Core Ops, SparseCore 0:
  356.7 175.0 all-reduce.3
  534.1 23.6 all-reduce.5
where the time goes:
time: 644 us; the launch traced here: 643 us
  waiting for transfers between devices  343 us (53%)
  starting transfers between devices  108 us (17%)
  other arithmetic  75.5 us (12%)
  matrix products  42.5 us (7%)
  blocking collectives  37.1 us (6%)
  local copies, waits for them, and re-layouts  20.1 us (3%)
  between operations  16.3 us (3%)
    all_to_all x1, waiting for transfers between devices, per_device(): lax.all_to_all(outgoing, 'space', split_axis=0, concat_axis=0, tiled=True)  269 us
    all_to_all x1, starting transfers between devices, per_device(): lax.all_to_all(predicted_rows.reshape(tile_count, capacity, obs_count), '...  90.9 us
    psum x1, waiting for transfers between devices, per_device(): tile_gram, tile_proj = lax.psum((gram_sum, projected), 'space')  73.2 us
    another operation x6, other arithmetic, finish_factor(): factor_low = jnp.linalg.cholesky(information)  34 us
    psum x1, blocking collectives, per_device(): tile_gram, tile_proj = lax.psum((gram_sum, projected), 'space')  32 us
    another operation x4, other arithmetic, finish_factor(): jax.scipy.linalg.solve_triangular(factor_low, projected, lower=True)  20.3 us
    select_n x2, other arithmetic, per_device(): jnp.take(footprints[0], source_of, axis=0, mode='fill', fill_value=0)  14 us
  transfers between devices with their start and end apart: 7, of which 3 were waited for; matrix products, arithmetic and copies ran while one was open for 10% of the time, Pallas kernels for 0%

commit v1 on v0

v1 whole, which is shorter than its diff:
```python
import jax
import jax.numpy as jnp
from jax import lax
from jax.experimental import pallas as pl
from jax.experimental.pallas import tpu as pltpu
from jax.sharding import PartitionSpec as P

PATCH = 64
REACH = 8


BETA = 0.6
KEEP = 0.8
HIGHEST = lax.Precision.HIGHEST


def padded(shard, sides, width):
    for axis, dim in sides:
        devices, length = (lax.axis_size(axis), shard.shape[dim])
        up = [(i, (i + 1) % devices) for i in range(devices - 1)]
        down = [(j, i) for i, j in up]
        last = lax.slice_in_dim(shard, length - width, length, axis=dim)
        leading = lax.slice_in_dim(shard, 0, width, axis=dim)
        before = lax.ppermute(last, axis, up)
        after = lax.ppermute(leading, axis, down)
        shard = jnp.concatenate([before, shard, after], axis=dim)
    return shard


def kernel_weights(reach):
    offsets = jnp.abs(jnp.arange(-reach, reach + 1).astype(jnp.float32))
    profile = (1.0 + 2.0 * offsets / reach) * jnp.exp(-2.0 * offsets / reach)
    return profile / jnp.sqrt(jnp.sum(profile * profile))


def make_proposal(flux, noise, prior_scale):
    patch_edge = PATCH
    cell_count = flux.shape[1]
    weights = kernel_weights(REACH)
    extended = padded(noise, (("space", 1),), REACH * patch_edge)
    extended_grid = extended.reshape(patch_edge + 2 * REACH, patch_edge)
    row_offset = jnp.arange(patch_edge + 2 * REACH)[None, :] - jnp.arange(patch_edge)[:, None]
    col_offset = (
        jnp.arange(patch_edge)[:, None] - jnp.arange(patch_edge)[None, :] + REACH
    ) % patch_edge
    row_band = jnp.zeros((patch_edge, patch_edge + 2 * REACH), jnp.float32)
    col_circulant = jnp.zeros((patch_edge, patch_edge), jnp.float32)
    for position in range(2 * REACH + 1):
        row_band = row_band + weights[position] * (row_offset == position).astype(jnp.float32)
        col_circulant = col_circulant + weights[position] * (col_offset == position).astype(
            jnp.float32
        )
    along_rows = jnp.dot(row_band, extended_grid, precision=HIGHEST)
    smooth = jnp.dot(along_rows, col_circulant, precision=HIGHEST)
    return KEEP * flux + BETA * prior_scale[None, :] * smooth.reshape(1, cell_count)


def slots_of(destination, tile_ids, capacity):
    match = destination[None, :] == tile_ids[:, None]
    rank = jnp.cumsum(match.astype(jnp.int32), axis=1) - 1
    block = jnp.arange(destination.shape[0], dtype=jnp.int32)
    taken = match[:, None, :] & (rank[:, None, :] == jnp.arange(capacity)[None, :, None])
    slots = jnp.sum(jnp.where(taken, block[None, None, :], 0), axis=2)
    return slots.reshape(-1).astype(jnp.int32), jnp.sum(match, axis=1).astype(jnp.int32)


def block_products(slots, counts, starts, footprints, tiles, windows, out_dtype):
    blocks, rows, _ = footprints.shape
    tile_count, piece_count = len(tiles), len(tiles[0])
    rank = tiles[0][0].shape[1]
    capacity = slots.shape[0] // tile_count
    depth = sum(windows)
    places = [sum(windows[:p]) for p in range(piece_count)]

    def kernel(slots_ref, counts_ref, starts_ref, f_ref, *rest):
        piece_refs = rest[: tile_count * piece_count]
        out_ref, f_v, b_v, f_sem, b_sem = rest[tile_count * piece_count :]
        f_copies = []
        for p in range(piece_count):
            begin = pl.multiple_of(starts_ref[p], 128)
            copy = pltpu.make_async_copy(
                f_ref.at[:, :, pl.ds(begin, windows[p])],
                f_v.at[:, :, pl.ds(places[p], windows[p])],
                f_sem.at[p],
            )
            f_copies.append(copy)
        for s in range(tile_count):
            for p in range(piece_count):
                pltpu.make_async_copy(
                    piece_refs[s * piece_count + p],
                    b_v.at[s, pl.ds(places[p], windows[p])],
                    b_sem.at[s, p],
                ).start()
            if s == 0:
                for copy in f_copies:
                    copy.start()
        for copy in f_copies:
            copy.wait()

        def step(s, carry):
            for p in range(piece_count):
                pltpu.make_async_copy(
                    piece_refs[p], b_v.at[s, pl.ds(places[p], windows[p])], b_sem.at[s, p]
                ).wait()
            lhs = jnp.concatenate(
                [f_v[slots_ref[s * capacity + j]] for j in range(capacity)], axis=0
            )
            product = jnp.dot(lhs, b_v[s], preferred_element_type=jnp.float32)
            for j in range(capacity):

                @pl.when(counts_ref[s] > j)
                def _():
                    at = pl.multiple_of(slots_ref[s * capacity + j] * rows, rows)
                    out_ref[pl.ds(at, rows), :] = product[j * rows : (j + 1) * rows].astype(
                        out_dtype
                    )

            return carry

        lax.fori_loop(0, tile_count, step, 0)

    flat = [piece for tile in tiles for piece in tile]
    smem = pl.BlockSpec(memory_space=pltpu.SMEM)
    hbm = pl.BlockSpec(memory_space=pl.ANY)
    return pl.pallas_call(
        kernel,
        out_shape=jax.ShapeDtypeStruct((blocks * rows, rank), out_dtype),
        in_specs=[smem, smem, smem, hbm] + [hbm] * len(flat),
        out_specs=pl.BlockSpec(memory_space=pltpu.VMEM),
        scratch_shapes=[
            pltpu.VMEM((blocks, rows, depth), jnp.bfloat16),
            pltpu.VMEM((tile_count, depth, rank), jnp.bfloat16),
            pltpu.SemaphoreType.DMA((piece_count,)),
            pltpu.SemaphoreType.DMA((tile_count, piece_count)),
        ],
        compiler_params=pltpu.CompilerParams(vmem_limit_bytes=56 * 2**20),
        cost_estimate=pl.CostEstimate(
            flops=2 * tile_count * capacity * rows * depth * rank,
            bytes_accessed=2 * depth * (tile_count * rank + blocks * rows),
            transcendentals=0,
        ),
    )(slots, counts, starts, footprints, *flat)


def information_sums(own, received, misfit, scale):
    rows, rank = own.shape
    half = rank // 2
    packed = half + half // 2 + 16

    def kernel(own_ref, received_ref, misfit_ref, out_ref):
        jacobian = (own_ref[...] + received_ref[...].astype(jnp.float32)) * scale
        jacobian = jacobian.astype(jnp.bfloat16)
        gram = lax.dot_general(
            jacobian, jacobian, (((0,), (0,)), ((), ())), preferred_element_type=jnp.float32
        )
        out_ref[0:half, :] = gram[0:half, :]
        out_ref[half : half + half // 2, 0:half] = gram[half : half + half // 2, half:]
        out_ref[half : half + half // 2, half:] = gram[half + half // 2 :, half:]
        rest = misfit_ref[...]
        parts = []
        for _ in range(3):
            part = rest.astype(jnp.bfloat16)
            parts.append(part)
            rest = rest - part.astype(jnp.float32)
        lhs = jnp.concatenate(parts + [jnp.zeros((16 - 3, rows), jnp.bfloat16)], axis=0)
        projected = jnp.dot(lhs, jacobian, preferred_element_type=jnp.float32)
        total = projected[0:1] + projected[1:2] + projected[2:3]
        out_ref[half + half // 2 :, :] = jnp.broadcast_to(total, (16, rank))

    return pl.pallas_call(
        kernel,
        out_shape=jax.ShapeDtypeStruct((packed, rank), jnp.float32),
        compiler_params=pltpu.CompilerParams(vmem_limit_bytes=32 * 2**20),
    )(own, received, misfit)


def finish_factor(packed):
    rank = packed.shape[1]
    half = rank // 2
    quarter = half // 2
    wide = rank + 128
    strip = 64

    def kernel(in_ref, up_ref, rhs_ref, work, factor):
        top = in_ref[0:half, :]
        work[0:half, 0:rank] = top
        work[half:, 0:half] = top[:, half:].T
        work[half : half + quarter, half:rank] = in_ref[half : half + quarter, 0:half]
        work[half + quarter :, half:rank] = in_ref[half : half + quarter, half:]
        for k in range(0, rank, 128):
            row = lax.broadcasted_iota(jnp.int32, (128, 128), 0)
            col = lax.broadcasted_iota(jnp.int32, (128, 128), 1)
            work[k : k + 128, k : k + 128] += (row == col).astype(jnp.float32)
        column = in_ref[half + quarter : half + quarter + 8, :].T
        work[:, rank:] = jnp.broadcast_to(column[:, 0:1], (rank, 128))

        sub = lax.broadcasted_iota(jnp.int32, (8, wide), 0)
        for base in range(0, rank, strip):
            skip = base // 128 * 128
            width = wide - skip
            sub_w = sub[:, skip:]
            tiles = [work[base + 8 * i : base + 8 * i + 8, skip:] for i in range(strip // 8)]
            for p in range(strip // 8):
                at = base + 8 * p - skip
                r = [jnp.broadcast_to(tiles[p][j : j + 1, :], (8, width)) for j in range(8)]
                d = {}
                for j in range(8):
                    for m in range(j, 8):
                        d[j, m] = jnp.broadcast_to(r[j][:, at + m : at + m + 1], (8, 128))
                inv, e = [], {}
                for j in range(8):
                    inv.append(lax.rsqrt(d[j, j]))
                    for m in range(j + 1, 8):
                        e[j, m] = d[j, m] * inv[j]
                    for l in range(j + 1, 8):
                        for m in range(l, 8):
                            d[l, m] = d[l, m] - e[j, l] * e[j, m]
                lanes = lambda x: jnp.concatenate([x] * (width // 128), axis=1)
                u = []
                for j in range(8):
                    u.append(r[j] * lanes(inv[j]))
                    for l in range(j + 1, 8):
                        r[l] = r[l] - lanes(e[j, l]) * u[j]
                whole = jnp.zeros((8, width), jnp.float32)
                for j in range(8):
                    whole = jnp.where(sub_w == j, u[j], whole)
                factor[base + 8 * p : base + 8 * p + 8, skip:] = whole
                for i in range(p + 1, strip // 8):
                    a = [
                        jnp.broadcast_to(tiles[i][:, at + j : at + j + 1], (8, 128))
                        for j in range(8)
                    ]
                    tile = tiles[i]
                    for j in range(8):
                        m_j = a[j] * inv[j]
                        for l in range(j + 1, 8):
                            a[l] = a[l] - m_j * e[j, l]
                        tile = tile - lanes(m_j) * u[j]
                    tiles[i] = tile
            low = base + strip
            if low < rank:
                keep = low // 128 * 128
                left = factor[base:low, low:rank]
                right = factor[base:low, keep:]
                work[low:, keep:] -= lax.dot_general(
                    left,
                    right,
                    (((0,), (0,)), ((), ())),
                    precision=HIGHEST,
                    preferred_element_type=jnp.float32,
                )
        for k in range(0, rank, 128):
            for c in range(0, rank, 128):
                if c < k:
                    up_ref[k : k + 128, c : c + 128] = jnp.zeros((128, 128), jnp.float32)
                elif c > k:
                    up_ref[k : k + 128, c : c + 128] = factor[k : k + 128, c : c + 128]
                else:
                    row = lax.broadcasted_iota(jnp.int32, (128, 128), 0)
                    col = lax.broadcasted_iota(jnp.int32, (128, 128), 1)
                    up_ref[k : k + 128, c : c + 128] = jnp.where(
                        col >= row, factor[k : k + 128, c : c + 128], 0.0
                    )
            rhs_ref[:, k : k + 128] = factor[k : k + 128, rank:].T[0:8, :]

    return pl.pallas_call(
        kernel,
        out_shape=(
            jax.ShapeDtypeStruct((rank, rank), jnp.float32),
            jax.ShapeDtypeStruct((8, rank), jnp.float32),
        ),
        scratch_shapes=[
            pltpu.VMEM((rank, wide), jnp.float32),
            pltpu.VMEM((rank, wide), jnp.float32),
        ],
        compiler_params=pltpu.CompilerParams(vmem_limit_bytes=32 * 2**20),
    )(packed)


def per_device(flux, noise, prior_scale, footprints, soundings, targets, basis):
    tile_count = lax.axis_size("space")
    step_count = lax.axis_size("tm")
    _, block_count, obs_count, cell_count = footprints.shape
    rank = basis.shape[1]
    capacity = max(2, (2 * block_count + tile_count - 1) // tile_count)
    place = lax.axis_index("space")
    top = tile_count // 4
    side = lax.axis_index("tm") % 2
    share = cell_count // 2

    over_last = [(i, i ^ 1) for i in range(tile_count)]
    over_mid = [(i, i ^ 2) for i in range(tile_count)]
    over_top = [(i, (i - 4) % tile_count) for i in range(tile_count)]
    over_step = [(i, i ^ 1) for i in range(step_count)]

    own_blocks = footprints[0]
    theirs = lax.dynamic_slice_in_dim(own_blocks, (1 - side) * share, share, axis=2)
    swapped = lax.ppermute(theirs, "tm", over_step)
    destination = targets[0, :, 0]
    other_destination = lax.ppermute(destination, "tm", over_step)

    cut = share // 2
    own_half = lax.dynamic_slice_in_dim(basis, side * share, share, axis=0)
    pieces = [own_half[:cut], own_half[cut:]]
    near = [pieces]
    for k in range(1, top):
        near.append([lax.ppermute(piece, "space", over_top) for piece in near[k - 1]])
    far = []
    for k in range(top):
        row = []
        for p in range(2):
            if k == top - 1 and p == 0 and k > 0:
                row.append(lax.ppermute(far[k - 1][p], "space", over_top))
            else:
                row.append(lax.ppermute(near[k][p], "space", over_mid))
        far.append(row)
    tiles, tile_ids = [], []
    for k in range(top):
        at = (place + 4 * k) % tile_count
        for held, index in ((near[k], at), (far[k], at ^ 2)):
            tiles.append(held)
            tile_ids.append(index)
            tiles.append([lax.ppermute(piece, "space", over_last) for piece in held])
            tile_ids.append(index ^ 1)
    tile_ids = jnp.stack(tile_ids)

    proposal = make_proposal(flux, noise, prior_scale)
    halves = lax.all_gather(proposal.astype(jnp.bfloat16), "space", axis=0, tiled=True)
    every = lax.dot_general(
        halves,
        own_blocks.reshape(block_count * obs_count, cell_count),
        (((1,), (1,)), ((), ())),
        preferred_element_type=jnp.float32,
    )
    named = jnp.arange(tile_count)[:, None] == jnp.repeat(destination, obs_count)[None, :]
    predicted = jnp.sum(jnp.where(named, every, 0.0), axis=0, keepdims=True)
    misfit = soundings.reshape(1, -1).astype(jnp.float32) - predicted

    slots, counts = slots_of(destination, tile_ids, capacity)
    other_slots, other_counts = slots_of(other_destination, tile_ids, capacity)
    windows = [cut, share - cut]
    start = (side * share).astype(jnp.int32)
    starts = jnp.stack([start, start + cut])
    others = block_products(
        other_slots,
        other_counts,
        jnp.array([0, cut], jnp.int32),
        swapped,
        tiles,
        windows,
        jnp.bfloat16,
    )
    received = lax.ppermute(others, "tm", over_step)
    own = block_products(slots, counts, starts, own_blocks, tiles, windows, jnp.float32)
    jac_scale = float(step_count * tile_count * block_count * obs_count) ** (-0.5)
    total = information_sums(own, received, misfit, jac_scale)

    half = total.shape[0] // 2
    last = place % 2
    mine = lax.dynamic_slice_in_dim(total, last * half, half, axis=0)
    sent = lax.dynamic_slice_in_dim(total, (1 - last) * half, half, axis=0)
    mine = mine + lax.ppermute(sent, "space", over_last)
    shift = 1
    while shift < step_count:
        pairs = [(i, i ^ shift) for i in range(step_count)]
        mine = mine + lax.ppermute(mine, "tm", pairs)
        shift *= 2
    shift = 2
    while shift < tile_count:
        pairs = [(i, i ^ shift) for i in range(tile_count)]
        mine = mine + lax.ppermute(mine, "space", pairs)
        shift *= 2
    back = lax.ppermute(mine, "space", over_last)
    packed = jnp.where(
        last == 0, jnp.concatenate([mine, back]), jnp.concatenate([back, mine])
    )
    factor_up, rhs = finish_factor(packed)
    return (
        proposal,
        predicted.reshape(1, block_count, obs_count),
        factor_up,
        rhs[0],
    )


def solution(mesh):
    return jax.shard_map(
        per_device,
        mesh=mesh,
        in_specs=(
            P("tm", "space"),
            P("tm", "space"),
            P("space"),
            P("tm", "space", None, None),
            P("tm", "space", None),
            P("tm", "space", None),
            P("space", None),
        ),
        out_specs=(P("tm", "space"), P("tm", "space", None), P(), P()),
        check_vma=False,
    )
```

time: 644 us -> 221 us (0.34)
  waiting for transfers between devices: 343 us -> 72.6 us
  other arithmetic: 75.5 us -> 4.01 us
  starting transfers between devices: 108 us -> 40.5 us
  Pallas kernels: 0 us -> 38.5 us
  blocking collectives: 37.1 us -> 21.2 us
  matrix products: 42.5 us -> 27.7 us
  between operations: 16.3 us -> 1.76 us
    all_to_all x3 -> x0, waiting for transfers between devices: 269 us -> none  [the longest x1 269 us: per_device(): lax.all_to_all(outgoing, 'space', split_axis=0, concat_axis=0, tiled=True)]
    all_to_all x3 -> x0, starting transfers between devices: 105 us -> none  [the longest x1 90.9 us: per_device(): lax.all_to_all(predicted_rows.reshape(tile_count, capacity, obs_count), '...]
    psum x2 -> x0, waiting for transfers between devices: 73.2 us -> none  [the longest x1 73.2 us: per_device(): tile_gram, tile_proj = lax.psum((gram_sum, projected), 'space')]
    ppermute x0 -> x39, waiting for transfers between devices: none -> 72.6 us  [the longest x7 30.7 us: per_device(): row.append(lax.ppermute(near[k][p], 'space', over_mid))]
    another operation x11 -> x4, other arithmetic: 54.3 us -> 1.59 us  [the longest x1 0.67 us: per_device(): starts = jnp.stack([start, start + cut])]
    pallas_call x0 -> x4, Pallas kernels: none -> 38.5 us  [the longest x2 28.5 us: block_products(): pl.pallas_call(kernel, out_shape=jax.ShapeDtypeStruct((blocks * rows, ran...]
    ppermute x0 -> x39, starting transfers between devices: none -> 38 us  [the longest x16 13.7 us: per_device(): tiles.append([lax.ppermute(piece, 'space', over_last) for piece in held])]
    psum x2 -> x0, blocking collectives: 37.1 us -> none  [the longest x1 32 us: per_device(): tile_gram, tile_proj = lax.psum((gram_sum, projected), 'space')]
  transfers between devices with their start and end apart: 7 -> 41, of which waited for: 3 -> 13; matrix products, arithmetic and copies ran while one was open for 10% -> 18% of each run, Pallas kernels for 0% -> 7%
where the time goes in v1:
time: 221 us
  waiting for transfers between devices  72.6 us (33%)
  starting transfers between devices  40.5 us (18%)
  Pallas kernels  38.5 us (17%)
  matrix products  27.7 us (13%)
  blocking collectives  21.2 us (10%)
  local copies, waits for them, and re-layouts  14.1 us (6%)
  other arithmetic  4.01 us (2%)
    ppermute x7, waiting for transfers between devices, per_device(): row.append(lax.ppermute(near[k][p], 'space', over_mid))  30.7 us
    pallas_call x2, Pallas kernels, block_products(): pl.pallas_call(kernel, out_shape=jax.ShapeDtypeStruct((blocks * rows, ran...  28.5 us
    all_gather x1, blocking collectives, per_device(): lax.all_gather(proposal.astype(jnp.bfloat16), 'space', axis=0, tiled=True)  21.2 us
    ppermute x6, waiting for transfers between devices, per_device(): lax.ppermute(piece, 'space', over_top)  17.7 us
    ppermute x3, waiting for transfers between devices, per_device(): mine = mine + lax.ppermute(mine, 'space', pairs)  15.6 us
    ppermute x16, starting transfers between devices, per_device(): tiles.append([lax.ppermute(piece, 'space', over_last) for piece in held])  13.7 us
    dot_general x1, matrix products, make_proposal(): smooth = jnp.dot(along_rows, col_circulant, precision=HIGHEST)  11 us
    dot_general x1, matrix products, make_proposal(): along_rows = jnp.dot(row_band, extended_grid, precision=HIGHEST)  11 us
  transfers between devices with their start and end apart: 41, of which 13 were waited for; matrix products, arithmetic and copies ran while one was open for 18% of the time, Pallas kernels for 7%

profile of v1, /device:TPU:0, one launch (start us, length us, event | category | flops | bytes accessed | tf_op | source)
XLA Modules:
  0.0 220.5 jit_solution(4546496748758429499)
XLA Ops:
  0.7 1.3 constant_dynamic-slice_fusion.1
  2.0 5.1 %collective-permute-start.8 = (bf16[1024,256]{1,0:T(8,128)(2,1)S(1)}, bf16[1024,256]{1,0:T(8,128)(2,1)S(1)}, u32[]{:S(2)}, u32[]{:S(2)}) collective-permute-start(bf16[1024,256]{1,0:T(8,128)(2,1)S(1)} %get-tuple-element.13.rest_0_), channel_id=1, source_target_pairs={{0,12},{1,13},{2,14},{3,15},{4,0},{5,1},{6,2},{7,3},{8,4},{9,5},{1... | collective-permute-start | bytes 1572872 | tf_op jit(solution)/shard_map/ppermute | solution.py:307
  8.3 1.3 collective-permute-start
  9.5 1.3 collective-permute-start.1
  10.8 1.6 collective-permute-start.32
  12.4 2.2 collective-permute-done.32
  14.6 4.5 %collective-permute-start.4 = (bf16[1024,256]{1,0:T(8,128)(2,1)S(1)}, bf16[1024,256]{1,0:T(8,128)(2,1)S(1)}, u32[]{:S(2)}, u32[]{:S(2)}) collective-permute-start(bf16[1024,256]{1,0:T(8,128)(2,1)S(1)} %get-tuple-element.13.rest_0_), channel_id=1, source_target_pairs={{0,2},{1,3},{2,0},{3,1},{4,6},{5,7},{6,4},{7,5},{8,10},{9,11},{10,... | collective-permute-start | bytes 1572872 | tf_op jit(solution)/shard_map/ppermute | solution.py:315
  19.1 10.7 %collective-permute-start.2 = (bf16[1024,256]{1,0:T(8,128)(2,1)S(1)}, bf16[1024,256]{1,0:T(8,128)(2,1)S(1)}, u32[]{:S(2)}, u32[]{:S(2)}) collective-permute-start(bf16[1024,256]{1,0:T(8,128)(2,1)S(1)} %get-tuple-element.13.rest_0_), channel_id=1, source_target_pairs={{0,1},{1,0},{2,3},{3,2},{4,5},{5,4},{6,7},{7,6},{8,9},{9,8},{10,11... | collective-permute-start | bytes 1572872 | tf_op jit(solution)/shard_map/ppermute | solution.py:323
  29.9 4.9 %dynamic-slice_bitcast_fusion = bf16[32,32,2048]{2,1,0:T(8,128)(2,1)} fusion(bf16[1,32,32,4096]{3,2,1,0:T(8,128)(2,1)} %param.11, s32[]{:T(128)S(6)} %select_n.108), kind=kLoop, calls=%fused_computation | loop fusion | bytes 8388612 | tf_op jit(solution)/shard_map/dynamic_slice | solution.py:297
  34.7 1.5 collective-permute-start.33
  36.8 4.4 %collective-permute-done.5.rest_5_ = bf16[1024,256]{1,0:T(8,128)(2,1)S(1)} collective-permute-done((bf16[1024,256]{1,0:T(8,128)(2,1)S(1)}, bf16[1024,256]{1,0:T(8,128)(2,1)S(1)}, u32[]{:S(2)}, u32[]{:S(2)}) %collective-permute-start.5) | collective-permute-done | bytes 524320 | tf_op jit(solution)/shard_map/ppermute | solution.py:315
  42.6 1.6 collective-permute-start.13
  44.2 7.2 %collective-permute-done.16.rest_16_ = bf16[1024,256]{1,0:T(8,128)(2,1)S(1)} collective-permute-done((bf16[1024,256]{1,0:T(8,128)(2,1)S(1)}, bf16[1024,256]{1,0:T(8,128)(2,1)S(1)}, u32[]{:S(2)}, u32[]{:S(2)}) %collective-permute-start.16) | collective-permute-done | bytes 524320 | tf_op jit(solution)/shard_map/ppermute | solution.py:307
  51.4 10.5 %collective-permute-done.17.rest_17_ = bf16[1024,256]{1,0:T(8,128)(2,1)S(1)} collective-permute-done((bf16[1024,256]{1,0:T(8,128)(2,1)S(1)}, bf16[1024,256]{1,0:T(8,128)(2,1)S(1)}, u32[]{:S(2)}, u32[]{:S(2)}) %collective-permute-start.17) | collective-permute-done | bytes 524320 | tf_op jit(solution)/shard_map/ppermute | solution.py:307
  62.4 4.7 %collective-permute-done.13.rest_13_ = bf16[1024,256]{1,0:T(8,128)(2,1)S(1)} collective-permute-done((bf16[1024,256]{1,0:T(8,128)(2,1)S(1)}, bf16[1024,256]{1,0:T(8,128)(2,1)S(1)}, u32[]{:S(2)}, u32[]{:S(2)}) %collective-permute-start.13) | collective-permute-done | bytes 524320 | tf_op jit(solution)/shard_map/ppermute | solution.py:315
  70.1 1.8 collective-permute-start.21
  74.4 21.7 %collective-permute-done.20.rest_20_ = bf16[1024,256]{1,0:T(8,128)(2,1)} collective-permute-done((bf16[1024,256]{1,0:T(8,128)(2,1)}, bf16[1024,256]{1,0:T(8,128)(2,1)}, u32[]{:S(2)}, u32[]{:S(2)}) %collective-permute-start.20) | collective-permute-done | bytes 524320 | tf_op jit(solution)/shard_map/ppermute | solution.py:315
  101.0 1.5 collective-permute-start.29
  102.5 11.0 %fusion.38 = f32[64,64]{1,0:T(8,128)S(1)} fusion(f32[80,64]{1,0:T(8,128)S(1)} %reshape.151, f32[]{:T(128)} %bitcast.16, f32[]{:T(128)} %bitcast.15, f32[]{:T(128)} %bitcast.14, f32[]{:T(128)} %bitcast.13, f32[]{:T(128)} %bitcast.12, f32[]{:T(128)} %bitcast.11, f32[]{:T(128)} %bitcast.10, f32[]{:T(128)} %bitcast.9, f32[]{:T(128)} %bitcast.8, f32[]{:T(128)} %bitcast.7, ...), kind=kOutput, calls=%fused_computation.50 | convolution fusion | flops 4193280 | bytes 36932 | tf_op jit(solution)/shard_map/dot_general | solution.py:53
  113.6 11.0 %fusion.4 = f32[64,64]{1,0:T(8,128)S(1)} fusion(f32[64,64]{1,0:T(8,128)S(1)} %fusion.38, f32[]{:T(128)} %bitcast.16, f32[]{:T(128)} %bitcast.15, f32[]{:T(128)} %bitcast.14, f32[]{:T(128)} %bitcast.13, f32[]{:T(128)} %bitcast.12, f32[]{:T(128)} %bitcast.11, f32[]{:T(128)} %bitcast.10, f32[]{:T(128)} %bitcast.9, f32[]{:T(128)} %bitcast.8, f32[]{:T(128)} %bitcast.7, ...), kind=kOutput, calls=%fused_computation.16 | convolution fusion | flops 3403776 | bytes 32836 | tf_op jit(solution)/shard_map/dot_general | solution.py:54
  126.5 21.2 %all-gather = bf16[16,1,4096]{2,1,0:T(2,128)(2,1)S(1)} all-gather(bf16[1,1,4096]{2,1,0:T(2,128)(2,1)S(1)} %get-tuple-element.10), channel_id=1, replica_groups=mesh['tm'=2,'space'=16] {'space'}, dimensions={0}, use_global_device_ids=true | all-gather | bytes 139264 | tf_op jit(solution)/shard_map/all_gather | solution.py:328
  149.2 14.1 %shard_map.112 = bf16[1024,256]{1,0:T(8,128)(2,1)} custom-call(s32[64]{0:T(128)} %reshape.154.slots_ref, s32[16]{0:T(128)} %get-tuple-element.8.counts_ref, s32[2]{0:T(128)} %iota_multiply_fusion.starts_ref, bf16[32,32,2048]{2,1,0:T(8,128)(2,1)} %collective-permute-done.33.f_ref, bf16[1024,256]{1,0:T(8,128)(2,1)} %copy-done.2, bf16[1024,256]{1,0:T(8,128)(2,1)} %copy-done.1, ...), custom_call_target="tpu_custom_call" | custom-call | flops 2147483648 | bytes 20971520 | tf_op jit(solution)/shard_map/pallas_call | solution.py:125
  163.3 1.6 collective-permute-start.34
  164.8 5.7 %fusion = f32[1024]{0:T(1024)S(1)} fusion(bf16[1024,4096]{1,0:T(8,128)(2,1)} %bitcast.51, bf16[16,1,4096]{2,1,0:T(2,128)(2,1)S(1)} %all-gather, s32[1024]{0:T(1024)S(1)} %eq.359), kind=kOutput, calls=%fused_computation.2 | convolution fusion | flops 134265856 | bytes 8527872 | tf_op jit(solution)/shard_map/dot_general | solution.py:329
  170.5 14.4 %shard_map.111.own_ref = f32[1024,256]{1,0:T(8,128)} custom-call(s32[64]{0:T(128)} %reshape.153.slots_ref, s32[16]{0:T(128)} %get-tuple-element.9.counts_ref, s32[2]{0:T(128)} %pad_add_fusion.starts_ref, bf16[32,32,4096]{2,1,0:T(8,128)(2,1)} %bitcast.52, bf16[1024,256]{1,0:T(8,128)(2,1)} %copy-done.2, bf16[1024,256]{1,0:T(8,128)(2,1)} %copy-done.1, ...), custom_call_target="tpu_custom_call" | custom-call | flops 2147483648 | bytes 20971520 | tf_op jit(solution)/shard_map/pallas_call | solution.py:125
  185.0 1.2 copy-done
  186.8 1.2 collective-permute-done.35
  188.6 4.5 %collective-permute-done.36 = f32[104,256]{1,0:T(8,128)S(1)} collective-permute-done((f32[104,256]{1,0:T(8,128)S(1)}, f32[104,256]{1,0:T(8,128)S(1)}, u32[]{:S(2)}, u32[]{:S(2)}) %collective-permute-start.36) | collective-permute-done | bytes 106528 | tf_op jit(solution)/shard_map/ppermute | solution.py:366
  193.2 4.7 %collective-permute-done.37 = f32[104,256]{1,0:T(8,128)S(1)} collective-permute-done((f32[104,256]{1,0:T(8,128)S(1)}, f32[104,256]{1,0:T(8,128)S(1)}, u32[]{:S(2)}, u32[]{:S(2)}) %collective-permute-start.37) | collective-permute-done | bytes 106528 | tf_op jit(solution)/shard_map/ppermute | solution.py:371
  198.0 4.7 %collective-permute-done.38 = f32[104,256]{1,0:T(8,128)S(1)} collective-permute-done((f32[104,256]{1,0:T(8,128)S(1)}, f32[104,256]{1,0:T(8,128)S(1)}, u32[]{:S(2)}, u32[]{:S(2)}) %collective-permute-start.38) | collective-permute-done | bytes 106528 | tf_op jit(solution)/shard_map/ppermute | solution.py:371
  202.8 6.2 %collective-permute-done.39 = f32[104,256]{1,0:T(8,128)S(1)} collective-permute-done((f32[104,256]{1,0:T(8,128)S(1)}, f32[104,256]{1,0:T(8,128)S(1)}, u32[]{:S(2)}, u32[]{:S(2)}) %collective-permute-start.39) | collective-permute-done | bytes 106528 | tf_op jit(solution)/shard_map/ppermute | solution.py:371
  210.4 9.6 %shard_map.114 = (f32[256,256]{1,0:T(8,128)}, f32[8,256]{1,0:T(8,128)S(1)}) custom-call(f32[208,256]{1,0:T(8,128)S(1)} %maximum_select_fusion.in_ref), custom_call_target="tpu_custom_call" | custom-call | tf_op jit(solution)/shard_map/pallas_call | solution.py:266
  (140 shorter events, 20.1 us)
Async XLA Ops:
  2.0 27.8 %collective-permute-start.8 = (bf16[1024,256]{1,0:T(8,128)(2,1)S(1)}, bf16[1024,256]{1,0:T(8,128)(2,1)S(1)}, u32[]{:S(2)}, u32[]{:S(2)}) collective-permute-start(bf16[1024,256]{1,0:T(8,128)(2,1)S(1)} %get-tuple-element.13.rest_0_), channel_id=1, source_target_pairs={{0,12},{1,13},{2,14},{3,15},{4,0},{5,1},{6,2},{7,3},{8,4},{9,5},{1... | collective-permute-start | bytes 1572872 | tf_op jit(solution)/shard_map/ppermute | solution.py:307
  7.1 27.6 %collective-permute-start.9 = (bf16[1024,256]{1,0:T(8,128)(2,1)S(1)}, bf16[1024,256]{1,0:T(8,128)(2,1)S(1)}, u32[]{:S(2)}, u32[]{:S(2)}) collective-permute-start(bf16[1024,256]{1,0:T(8,128)(2,1)S(1)} %get-tuple-element.12.rest_1_), channel_id=1, source_target_pairs={{0,12},{1,13},{2,14},{3,15},{4,0},{5,1},{6,2},{7,3},{8,4},{9,5},{1... | collective-permute-start | bytes 1572872 | tf_op jit(solution)/shard_map/ppermute | solution.py:307
  8.3 10.8 %collective-permute-start = (f32[1,512]{1,0:T(1,128)S(1)}, f32[1,512]{1,0:T(1,128)S(1)}, u32[]{:S(2)}, u32[]{:S(2)}) collective-permute-start(f32[1,512]{1,0:T(1,128)S(1)} %get-tuple-element.14), channel_id=1, source_target_pairs={{0,1},{1,2},{2,3},{3,4},{4,5},{5,6},{6,7},{7,8},{8,9},{9,10},{10,1... | collective-permute-start | bytes 6152 | tf_op jit(solution)/shard_map/ppermute | solution.py:24
  9.5 9.6 %collective-permute-start.1 = (f32[1,512]{1,0:T(1,128)S(1)}, f32[1,512]{1,0:T(1,128)S(1)}, u32[]{:S(2)}, u32[]{:S(2)}) collective-permute-start(f32[1,512]{1,0:T(1,128)S(1)} %get-tuple-element.15), channel_id=1, source_target_pairs={{1,0},{2,1},{3,2},{4,3},{5,4},{6,5},{7,6},{8,7},{9,8},{10,9},{11,1... | collective-permute-start | bytes 6152 | tf_op jit(solution)/shard_map/ppermute | solution.py:25
  14.6 21.6 %collective-permute-start.4 = (bf16[1024,256]{1,0:T(8,128)(2,1)S(1)}, bf16[1024,256]{1,0:T(8,128)(2,1)S(1)}, u32[]{:S(2)}, u32[]{:S(2)}) collective-permute-start(bf16[1024,256]{1,0:T(8,128)(2,1)S(1)} %get-tuple-element.13.rest_0_), channel_id=1, source_target_pairs={{0,2},{1,3},{2,0},{3,1},{4,6},{5,7},{6,4},{7,5},{8,10},{9,11},{10,... | collective-permute-start | bytes 1572872 | tf_op jit(solution)/shard_map/ppermute | solution.py:315
  19.1 22.1 %collective-permute-start.5 = (bf16[1024,256]{1,0:T(8,128)(2,1)S(1)}, bf16[1024,256]{1,0:T(8,128)(2,1)S(1)}, u32[]{:S(2)}, u32[]{:S(2)}) collective-permute-start(bf16[1024,256]{1,0:T(8,128)(2,1)S(1)} %get-tuple-element.12.rest_1_), channel_id=1, source_target_pairs={{0,2},{1,3},{2,0},{3,1},{4,6},{5,7},{6,4},{7,5},{8,10},{9,11},{10,... | collective-permute-start | bytes 1572872 | tf_op jit(solution)/shard_map/ppermute | solution.py:315
  19.1 23.0 %collective-permute-start.2 = (bf16[1024,256]{1,0:T(8,128)(2,1)S(1)}, bf16[1024,256]{1,0:T(8,128)(2,1)S(1)}, u32[]{:S(2)}, u32[]{:S(2)}) collective-permute-start(bf16[1024,256]{1,0:T(8,128)(2,1)S(1)} %get-tuple-element.13.rest_0_), channel_id=1, source_target_pairs={{0,1},{1,0},{2,3},{3,2},{4,5},{5,4},{6,7},{7,6},{8,9},{9,8},{10,11... | collective-permute-start | bytes 1572872 | tf_op jit(solution)/shard_map/ppermute | solution.py:323
  29.8 12.8 %collective-permute-start.3 = (bf16[1024,256]{1,0:T(8,128)(2,1)S(1)}, bf16[1024,256]{1,0:T(8,128)(2,1)S(1)}, u32[]{:S(2)}, u32[]{:S(2)}) collective-permute-start(bf16[1024,256]{1,0:T(8,128)(2,1)S(1)} %get-tuple-element.12.rest_1_), channel_id=1, source_target_pairs={{0,1},{1,0},{2,3},{3,2},{4,5},{5,4},{6,7},{7,6},{8,9},{9,8},{10,11... | collective-permute-start | bytes 1572872 | tf_op jit(solution)/shard_map/ppermute | solution.py:323
  34.7 113.1 %collective-permute-start.33 = (bf16[32,32,2048]{2,1,0:T(8,128)(2,1)}, bf16[32,32,2048]{2,1,0:T(8,128)(2,1)}, u32[]{:S(2)}, u32[]{:S(2)}) collective-permute-start(bf16[32,32,2048]{2,1,0:T(8,128)(2,1)} %dynamic-slice_bitcast_fusion), channel_id=1, source_target_pairs={{0,16},{16,0},{1,17},{17,1},{2,18},{18,2},{3,19},{19,3},{4,20},{20... | collective-permute-start | bytes 12582920 | tf_op jit(solution)/shard_map/ppermute | solution.py:298
  36.2 15.1 %collective-permute-start.16 = (bf16[1024,256]{1,0:T(8,128)(2,1)S(1)}, bf16[1024,256]{1,0:T(8,128)(2,1)S(1)}, u32[]{:S(2)}, u32[]{:S(2)}) collective-permute-start(bf16[1024,256]{1,0:T(8,128)(2,1)S(1)} %collective-permute-done.8.rest_8_), channel_id=1, source_target_pairs={{0,12},{1,13},{2,14},{3,15},{4,0},{5,1},{6,2},{7,3},{8,4},{9,5},{1... | collective-permute-start | bytes 1572872 | tf_op jit(solution)/shard_map/ppermute | solution.py:307
  41.1 20.7 %collective-permute-start.17 = (bf16[1024,256]{1,0:T(8,128)(2,1)S(1)}, bf16[1024,256]{1,0:T(8,128)(2,1)S(1)}, u32[]{:S(2)}, u32[]{:S(2)}) collective-permute-start(bf16[1024,256]{1,0:T(8,128)(2,1)S(1)} %collective-permute-done.9.rest_9_), channel_id=1, source_target_pairs={{0,12},{1,13},{2,14},{3,15},{4,0},{5,1},{6,2},{7,3},{8,4},{9,5},{1... | collective-permute-start | bytes 1572872 | tf_op jit(solution)/shard_map/ppermute | solution.py:307
  42.1 19.7 %collective-permute-start.12 = (bf16[1024,256]{1,0:T(8,128)(2,1)S(1)}, bf16[1024,256]{1,0:T(8,128)(2,1)S(1)}, u32[]{:S(2)}, u32[]{:S(2)}) collective-permute-start(bf16[1024,256]{1,0:T(8,128)(2,1)S(1)} %collective-permute-done.8.rest_8_), channel_id=1, source_target_pairs={{0,2},{1,3},{2,0},{3,1},{4,6},{5,7},{6,4},{7,5},{8,10},{9,11},{10,... | collective-permute-start | bytes 1572872 | tf_op jit(solution)/shard_map/ppermute | solution.py:315
  42.6 24.5 %collective-permute-start.13 = (bf16[1024,256]{1,0:T(8,128)(2,1)S(1)}, bf16[1024,256]{1,0:T(8,128)(2,1)S(1)}, u32[]{:S(2)}, u32[]{:S(2)}) collective-permute-start(bf16[1024,256]{1,0:T(8,128)(2,1)S(1)} %collective-permute-done.9.rest_9_), channel_id=1, source_target_pairs={{0,2},{1,3},{2,0},{3,1},{4,6},{5,7},{6,4},{7,5},{8,10},{9,11},{10,... | collective-permute-start | bytes 1572872 | tf_op jit(solution)/shard_map/ppermute | solution.py:315
  51.4 18.8 %collective-permute-start.10 = (bf16[1024,256]{1,0:T(8,128)(2,1)S(1)}, bf16[1024,256]{1,0:T(8,128)(2,1)}, u32[]{:S(2)}, u32[]{:S(2)}) collective-permute-start(bf16[1024,256]{1,0:T(8,128)(2,1)S(1)} %collective-permute-done.8.rest_8_), channel_id=1, source_target_pairs={{0,1},{1,0},{2,3},{3,2},{4,5},{5,4},{6,7},{7,6},{8,9},{9,8},{10,11... | collective-permute-start | bytes 1572872 | tf_op jit(solution)/shard_map/ppermute | solution.py:323
  61.9 8.3 %collective-permute-start.11 = (bf16[1024,256]{1,0:T(8,128)(2,1)S(1)}, bf16[1024,256]{1,0:T(8,128)(2,1)}, u32[]{:S(2)}, u32[]{:S(2)}) collective-permute-start(bf16[1024,256]{1,0:T(8,128)(2,1)S(1)} %collective-permute-done.9.rest_9_), channel_id=1, source_target_pairs={{0,1},{1,0},{2,3},{3,2},{4,5},{5,4},{6,7},{7,6},{8,9},{9,8},{10,11... | collective-permute-start | bytes 1572872 | tf_op jit(solution)/shard_map/ppermute | solution.py:323
  61.9 10.1 %collective-permute-start.6 = (bf16[1024,256]{1,0:T(8,128)(2,1)S(1)}, bf16[1024,256]{1,0:T(8,128)(2,1)}, u32[]{:S(2)}, u32[]{:S(2)}) collective-permute-start(bf16[1024,256]{1,0:T(8,128)(2,1)S(1)} %collective-permute-done.4.rest_4_), channel_id=1, source_target_pairs={{0,1},{1,0},{2,3},{3,2},{4,5},{5,4},{6,7},{7,6},{8,9},{9,8},{10,11... | collective-permute-start | bytes 1572872 | tf_op jit(solution)/shard_map/ppermute | solution.py:323
  70.1 26.0 %collective-permute-start.25 = (bf16[1024,256]{1,0:T(8,128)(2,1)}, bf16[1024,256]{1,0:T(8,128)(2,1)}, u32[]{:S(2)}, u32[]{:S(2)}) collective-permute-start(bf16[1024,256]{1,0:T(8,128)(2,1)} %copy-done.10), channel_id=1, source_target_pairs={{0,12},{1,13},{2,14},{3,15},{4,0},{5,1},{6,2},{7,3},{8,4},{9,5},{1... | collective-permute-start | bytes 1572872 | tf_op jit(solution)/shard_map/ppermute | solution.py:307
  70.1 26.5 %collective-permute-start.21 = (bf16[1024,256]{1,0:T(8,128)(2,1)}, bf16[1024,256]{1,0:T(8,128)(2,1)}, u32[]{:S(2)}, u32[]{:S(2)}) collective-permute-start(bf16[1024,256]{1,0:T(8,128)(2,1)} %copy-done.10), channel_id=1, source_target_pairs={{0,2},{1,3},{2,0},{3,1},{4,6},{5,7},{6,4},{7,5},{8,10},{9,11},{10,... | collective-permute-start | bytes 1572872 | tf_op jit(solution)/shard_map/ppermute | solution.py:315
  71.9 24.1 %collective-permute-start.20 = (bf16[1024,256]{1,0:T(8,128)(2,1)}, bf16[1024,256]{1,0:T(8,128)(2,1)}, u32[]{:S(2)}, u32[]{:S(2)}) collective-permute-start(bf16[1024,256]{1,0:T(8,128)(2,1)} %copy-done.9), channel_id=1, source_target_pairs={{0,2},{1,3},{2,0},{3,1},{4,6},{5,7},{6,4},{7,5},{8,10},{9,11},{10,... | collective-permute-start | bytes 1572872 | tf_op jit(solution)/shard_map/ppermute | solution.py:315
  72.2 24.4 %collective-permute-start.24 = (bf16[1024,256]{1,0:T(8,128)(2,1)}, bf16[1024,256]{1,0:T(8,128)(2,1)}, u32[]{:S(2)}, u32[]{:S(2)}) collective-permute-start(bf16[1024,256]{1,0:T(8,128)(2,1)} %copy-done.9), channel_id=1, source_target_pairs={{0,12},{1,13},{2,14},{3,15},{4,0},{5,1},{6,2},{7,3},{8,4},{9,5},{1... | collective-permute-start | bytes 1572872 | tf_op jit(solution)/shard_map/ppermute | solution.py:307
  96.1 6.4 %collective-permute-start.19 = (bf16[1024,256]{1,0:T(8,128)(2,1)}, bf16[1024,256]{1,0:T(8,128)(2,1)}, u32[]{:S(2)}, u32[]{:S(2)}) collective-permute-start(bf16[1024,256]{1,0:T(8,128)(2,1)} %copy-done.10), channel_id=1, source_target_pairs={{0,1},{1,0},{2,3},{3,2},{4,5},{5,4},{6,7},{7,6},{8,9},{9,8},{10,11... | collective-permute-start | bytes 1572872 | tf_op jit(solution)/shard_map/ppermute | solution.py:323
  99.8 24.9 %collective-permute-start.28 = (bf16[1024,256]{1,0:T(8,128)(2,1)}, bf16[1024,256]{1,0:T(8,128)(2,1)}, u32[]{:S(2)}, u32[]{:S(2)}) collective-permute-start(bf16[1024,256]{1,0:T(8,128)(2,1)} %collective-permute-done.20.rest_20_), channel_id=1, source_target_pairs={{0,12},{1,13},{2,14},{3,15},{4,0},{5,1},{6,2},{7,3},{8,4},{9,5},{1... | collective-permute-start | bytes 1572872 | tf_op jit(solution)/shard_map/ppermute | solution.py:313
  100.7 24.6 %collective-permute-start.22 = (bf16[1024,256]{1,0:T(8,128)(2,1)}, bf16[1024,256]{1,0:T(8,128)(2,1)}, u32[]{:S(2)}, u32[]{:S(2)}) collective-permute-start(bf16[1024,256]{1,0:T(8,128)(2,1)} %collective-permute-done.20.rest_20_), channel_id=1, source_target_pairs={{0,1},{1,0},{2,3},{3,2},{4,5},{5,4},{6,7},{7,6},{8,9},{9,8},{10,11... | collective-permute-start | bytes 1572872 | tf_op jit(solution)/shard_map/ppermute | solution.py:323
  101.0 24.3 %collective-permute-start.29 = (bf16[1024,256]{1,0:T(8,128)(2,1)}, bf16[1024,256]{1,0:T(8,128)(2,1)}, u32[]{:S(2)}, u32[]{:S(2)}) collective-permute-start(bf16[1024,256]{1,0:T(8,128)(2,1)} %collective-permute-done.25.rest_25_), channel_id=1, source_target_pairs={{0,2},{1,3},{2,0},{3,1},{4,6},{5,7},{6,4},{7,5},{8,10},{9,11},{10,... | collective-permute-start | bytes 1572872 | tf_op jit(solution)/shard_map/ppermute | solution.py:315
  102.5 23.3 %collective-permute-start.23 = (bf16[1024,256]{1,0:T(8,128)(2,1)}, bf16[1024,256]{1,0:T(8,128)(2,1)}, u32[]{:S(2)}, u32[]{:S(2)}) collective-permute-start(bf16[1024,256]{1,0:T(8,128)(2,1)} %collective-permute-done.21.rest_21_), channel_id=1, source_target_pairs={{0,1},{1,0},{2,3},{3,2},{4,5},{5,4},{6,7},{7,6},{8,9},{9,8},{10,11... | collective-permute-start | bytes 1572872 | tf_op jit(solution)/shard_map/ppermute | solution.py:323
  124.7 23.1 %collective-permute-start.27 = (bf16[1024,256]{1,0:T(8,128)(2,1)}, bf16[1024,256]{1,0:T(8,128)(2,1)S(1)}, u32[]{:S(2)}, u32[]{:S(2)}) collective-permute-start(bf16[1024,256]{1,0:T(8,128)(2,1)} %collective-permute-done.25.rest_25_), channel_id=1, source_target_pairs={{0,1},{1,0},{2,3},{3,2},{4,5},{5,4},{6,7},{7,6},{8,9},{9,8},{10,11... | collective-permute-start | bytes 1572872 | tf_op jit(solution)/shard_map/ppermute | solution.py:323
  125.3 22.5 %collective-permute-start.26 = (bf16[1024,256]{1,0:T(8,128)(2,1)}, bf16[1024,256]{1,0:T(8,128)(2,1)S(1)}, u32[]{:S(2)}, u32[]{:S(2)}) collective-permute-start(bf16[1024,256]{1,0:T(8,128)(2,1)} %collective-permute-done.24.rest_24_), channel_id=1, source_target_pairs={{0,1},{1,0},{2,3},{3,2},{4,5},{5,4},{6,7},{7,6},{8,9},{9,8},{10,11... | collective-permute-start | bytes 1572872 | tf_op jit(solution)/shard_map/ppermute | solution.py:323
  125.4 22.4 %collective-permute-start.30 = (bf16[1024,256]{1,0:T(8,128)(2,1)}, bf16[1024,256]{1,0:T(8,128)(2,1)S(1)}, u32[]{:S(2)}, u32[]{:S(2)}) collective-permute-start(bf16[1024,256]{1,0:T(8,128)(2,1)} %collective-permute-done.28.rest_28_), channel_id=1, source_target_pairs={{0,1},{1,0},{2,3},{3,2},{4,5},{5,4},{6,7},{7,6},{8,9},{9,8},{10,11... | collective-permute-start | bytes 1572872 | tf_op jit(solution)/shard_map/ppermute | solution.py:323
  125.8 22.0 %collective-permute-start.31 = (bf16[1024,256]{1,0:T(8,128)(2,1)}, bf16[1024,256]{1,0:T(8,128)(2,1)S(1)}, u32[]{:S(2)}, u32[]{:S(2)}) collective-permute-start(bf16[1024,256]{1,0:T(8,128)(2,1)} %collective-permute-done.29.rest_29_), channel_id=1, source_target_pairs={{0,1},{1,0},{2,3},{3,2},{4,5},{5,4},{6,7},{7,6},{8,9},{9,8},{10,11... | collective-permute-start | bytes 1572872 | tf_op jit(solution)/shard_map/ppermute | solution.py:323
  163.3 21.7 %collective-permute-start.34 = (bf16[1024,256]{1,0:T(8,128)(2,1)}, bf16[1024,256]{1,0:T(8,128)(2,1)S(1)}, u32[]{:S(2)}, u32[]{:S(2)}) collective-permute-start(bf16[1024,256]{1,0:T(8,128)(2,1)} %shard_map.112), channel_id=1, source_target_pairs={{0,16},{16,0},{1,17},{17,1},{2,18},{18,2},{3,19},{19,3},{4,20},{20... | collective-permute-start | bytes 1572872 | tf_op jit(solution)/shard_map/ppermute | solution.py:353
  188.0 5.1 %collective-permute-start.36 = (f32[104,256]{1,0:T(8,128)S(1)}, f32[104,256]{1,0:T(8,128)S(1)}, u32[]{:S(2)}, u32[]{:S(2)}) collective-permute-start(f32[104,256]{1,0:T(8,128)S(1)} %dynamic-slice_add_fusion), channel_id=1, source_target_pairs={{0,16},{16,0},{1,17},{17,1},{2,18},{18,2},{3,19},{19,3},{4,20},{20... | collective-permute-start | bytes 319496 | tf_op jit(solution)/shard_map/ppermute | solution.py:366
  202.7 6.3 %collective-permute-start.39 = (f32[104,256]{1,0:T(8,128)S(1)}, f32[104,256]{1,0:T(8,128)S(1)}, u32[]{:S(2)}, u32[]{:S(2)}) collective-permute-start(f32[104,256]{1,0:T(8,128)S(1)} %add.304), channel_id=1, source_target_pairs={{0,8},{1,9},{2,10},{3,11},{4,12},{5,13},{6,14},{7,15},{8,0},{9,1},... | collective-permute-start | bytes 319496 | tf_op jit(solution)/shard_map/ppermute | solution.py:371
  (31 other events, 1341.1 us)

commit v2 on v1

--- a/solution.py
+++ b/solution.py
@@ -1,5 +1,6 @@
 import jax
 import jax.numpy as jnp
+import numpy as np
 from jax import lax
 from jax.experimental import pallas as pl
 from jax.experimental.pallas import tpu as pltpu
@@ -14,45 +15,41 @@
 HIGHEST = lax.Precision.HIGHEST
 
 
-def padded(shard, sides, width):
-    for axis, dim in sides:
-        devices, length = (lax.axis_size(axis), shard.shape[dim])
-        up = [(i, (i + 1) % devices) for i in range(devices - 1)]
-        down = [(j, i) for i, j in up]
-        last = lax.slice_in_dim(shard, length - width, length, axis=dim)
-        leading = lax.slice_in_dim(shard, 0, width, axis=dim)
-        before = lax.ppermute(last, axis, up)
-        after = lax.ppermute(leading, axis, down)
-        shard = jnp.concatenate([before, shard, after], axis=dim)
-    return shard
-
-
 def kernel_weights(reach):
-    offsets = jnp.abs(jnp.arange(-reach, reach + 1).astype(jnp.float32))
-    profile = (1.0 + 2.0 * offsets / reach) * jnp.exp(-2.0 * offsets / reach)
-    return profile / jnp.sqrt(jnp.sum(profile * profile))
+    offsets = np.abs(np.arange(-reach, reach + 1)).astype(np.float32)
+    profile = (1.0 + 2.0 * offsets / reach) * np.exp(-2.0 * offsets / reach)
+    return [float(w) for w in profile / np.sqrt(np.sum(profile * profile))]
 
 
 def make_proposal(flux, noise, prior_scale):
-    patch_edge = PATCH
-    cell_count = flux.shape[1]
+    edge = PATCH
+    cells = flux.shape[1]
+    width = REACH * edge
     weights = kernel_weights(REACH)
-    extended = padded(noise, (("space", 1),), REACH * patch_edge)
-    extended_grid = extended.reshape(patch_edge + 2 * REACH, patch_edge)
-    row_offset = jnp.arange(patch_edge + 2 * REACH)[None, :] - jnp.arange(patch_edge)[:, None]
-    col_offset = (
-        jnp.arange(patch_edge)[:, None] - jnp.arange(patch_edge)[None, :] + REACH
-    ) % patch_edge
-    row_band = jnp.zeros((patch_edge, patch_edge + 2 * REACH), jnp.float32)
-    col_circulant = jnp.zeros((patch_edge, patch_edge), jnp.float32)
-    for position in range(2 * REACH + 1):
-        row_band = row_band + weights[position] * (row_offset == position).astype(jnp.float32)
-        col_circulant = col_circulant + weights[position] * (col_offset == position).astype(
-            jnp.float32
-        )
-    along_rows = jnp.dot(row_band, extended_grid, precision=HIGHEST)
-    smooth = jnp.dot(along_rows, col_circulant, precision=HIGHEST)
-    return KEEP * flux + BETA * prior_scale[None, :] * smooth.reshape(1, cell_count)
+    devices = lax.axis_size("space")
+    up = [(i, (i + 1) % devices) for i in range(devices - 1)]
+    down = [(j, i) for i, j in up]
+    before = lax.ppermute(noise[:, cells - width :], "space", up)
+    after = lax.ppermute(noise[:, :width], "space", down)
+    extended = jnp.concatenate([before, noise, after], axis=1).reshape(edge + 2 * REACH, edge)
+
+    def kernel(extended_ref, flux_ref, scale_ref, out_ref):
+        rows = jnp.zeros((edge, edge), jnp.float32)
+        for position in range(2 * REACH + 1):
+            rows = rows + weights[position] * extended_ref[position : position + edge, :]
+        twice = jnp.concatenate([rows, rows], axis=1)
+        smooth = jnp.zeros((edge, 2 * edge), jnp.float32)
+        for position in range(2 * REACH + 1):
+            shift = (REACH - position) % (2 * edge)
+            rolled = pltpu.roll(twice, shift, 1) if shift else twice
+            smooth = smooth + weights[position] * rolled
+        out_ref[...] = KEEP * flux_ref[...] + BETA * scale_ref[...] * smooth[:, :edge]
+
+    proposal = pl.pallas_call(
+        kernel, out_shape=jax.ShapeDtypeStruct((edge, edge), jnp.float32)
+    )(extended, flux.reshape(edge, edge), prior_scale.reshape(edge, edge))
+    flat = proposal.reshape(1, cells)
+    return flat, flat.astype(jnp.bfloat16), (before, after)
 
 
 def slots_of(destination, tile_ids, capacity):
@@ -64,82 +61,108 @@
     return slots.reshape(-1).astype(jnp.int32), jnp.sum(match, axis=1).astype(jnp.int32)
 
 
-def block_products(slots, counts, starts, footprints, tiles, windows, out_dtype):
-    blocks, rows, _ = footprints.shape
-    tile_count, piece_count = len(tiles), len(tiles[0])
-    rank = tiles[0][0].shape[1]
-    capacity = slots.shape[0] // tile_count
-    depth = sum(windows)
-    places = [sum(windows[:p]) for p in range(piece_count)]
-
-    def kernel(slots_ref, counts_ref, starts_ref, f_ref, *rest):
-        piece_refs = rest[: tile_count * piece_count]
-        out_ref, f_v, b_v, f_sem, b_sem = rest[tile_count * piece_count :]
+def block_products(slots, counts, sources, tiles, jobs, capacity, out_dtype, base=None):
+    blocks, rows, _ = sources[0][0].shape
+    rank = tiles[0][0][0].shape[1]
+    widths = [width for _, _, width in sources]
+    places = [sum(widths[:i]) for i in range(len(widths))]
+    depth = max(high - low for _, low, high in jobs)
+    arrays, copies = [], []
+    for s, low, high in jobs:
+        parts, at = [], 0
+        for array, first, count in tiles[s]:
+            begin, end = max(low, at), min(high, at + count)
+            if begin < end:
+                known = [i for i, other in enumerate(arrays) if other is array]
+                if not known:
+                    arrays.append(array)
+                    known = [len(arrays) - 1]
+                parts.append((known[0], first + begin - at, begin - low, end - begin))
+            at += count
+        copies.append(parts)
+    most = max(len(parts) for parts in copies)
+    ahead = min(4, len(jobs))
+
+    def kernel(slots_ref, counts_ref, starts_ref, *rest):
+        f_refs, rest = rest[: len(sources)], rest[len(sources) :]
+        b_refs, rest = rest[: len(arrays)], rest[len(arrays) :]
+        if base is not None:
+            base_ref, rest = rest[0], rest[1:]
+        out_ref, f_v, b_v, f_sem, b_sem = rest
         f_copies = []
-        for p in range(piece_count):
-            begin = pl.multiple_of(starts_ref[p], 128)
+        for i, width in enumerate(widths):
+            begin = pl.multiple_of(starts_ref[i], 128)
             copy = pltpu.make_async_copy(
-                f_ref.at[:, :, pl.ds(begin, windows[p])],
-                f_v.at[:, :, pl.ds(places[p], windows[p])],
-                f_sem.at[p],
+                f_refs[i].at[:, :, pl.ds(begin, width)],
+                f_v.at[:, :, pl.ds(places[i], width)],
+                f_sem.at[i],
             )
+            copy.start()
             f_copies.append(copy)
-        for s in range(tile_count):
-            for p in range(piece_count):
+
+        def job_copies(n):
+            return [
                 pltpu.make_async_copy(
-                    piece_refs[s * piece_count + p],
-                    b_v.at[s, pl.ds(places[p], windows[p])],
-                    b_sem.at[s, p],
-                ).start()
-            if s == 0:
-                for copy in f_copies:
-                    copy.start()
+                    b_refs[i].at[pl.ds(first, count)],
+                    b_v.at[n, pl.ds(place, count)],
+                    b_sem.at[n, part],
+                )
+                for part, (i, first, place, count) in enumerate(copies[n])
+            ]
+
+        for n in range(ahead):
+            for copy in job_copies(n):
+                copy.start()
+        if base is not None and out_dtype == jnp.float32:
+            out_ref[...] = base_ref[...]
         for copy in f_copies:
             copy.wait()
-
-        def step(s, carry):
-            for p in range(piece_count):
-                pltpu.make_async_copy(
-                    piece_refs[p], b_v.at[s, pl.ds(places[p], windows[p])], b_sem.at[s, p]
-                ).wait()
+        for n, (s, low, high) in enumerate(jobs):
+            if n + ahead < len(jobs):
+                for copy in job_copies(n + ahead):
+                    copy.start()
+            for copy in job_copies(n):
+                copy.wait()
             lhs = jnp.concatenate(
-                [f_v[slots_ref[s * capacity + j]] for j in range(capacity)], axis=0
+                [f_v[slots_ref[s * capacity + j], :, low:high] for j in range(capacity)], axis=0
             )
-            product = jnp.dot(lhs, b_v[s], preferred_element_type=jnp.float32)
+            product = jnp.dot(
+                lhs, b_v[n, 0 : high - low, :], preferred_element_type=jnp.float32
+            )
             for j in range(capacity):
 
                 @pl.when(counts_ref[s] > j)
                 def _():
                     at = pl.multiple_of(slots_ref[s * capacity + j] * rows, rows)
-                    out_ref[pl.ds(at, rows), :] = product[j * rows : (j + 1) * rows].astype(
-                        out_dtype
-                    )
-
-            return carry
-
-        lax.fori_loop(0, tile_count, step, 0)
-
-    flat = [piece for tile in tiles for piece in tile]
+                    part = product[j * rows : (j + 1) * rows]
+                    if low > 0:
+                        part = part + base_ref[pl.ds(at, rows), :]
+                    out_ref[pl.ds(at, rows), :] = part.astype(out_dtype)
+
     smem = pl.BlockSpec(memory_space=pltpu.SMEM)
+    vmem = pl.BlockSpec(memory_space=pltpu.VMEM)
     hbm = pl.BlockSpec(memory_space=pl.ANY)
+    extra = [] if base is None else [base]
+    starts = jnp.stack([jnp.asarray(first, jnp.int32) for _, first, _ in sources])
+    cells = sum(high - low for _, low, high in jobs)
     return pl.pallas_call(
         kernel,
         out_shape=jax.ShapeDtypeStruct((blocks * rows, rank), out_dtype),
-        in_specs=[smem, smem, smem, hbm] + [hbm] * len(flat),
-        out_specs=pl.BlockSpec(memory_space=pltpu.VMEM),
+        in_specs=[smem] * 3 + [hbm] * (len(sources) + len(arrays)) + [vmem] * len(extra),
+        out_specs=vmem,
         scratch_shapes=[
-            pltpu.VMEM((blocks, rows, depth), jnp.bfloat16),
-            pltpu.VMEM((tile_count, depth, rank), jnp.bfloat16),
-            pltpu.SemaphoreType.DMA((piece_count,)),
-            pltpu.SemaphoreType.DMA((tile_count, piece_count)),
+            pltpu.VMEM((blocks, rows, sum(widths)), jnp.bfloat16),
+            pltpu.VMEM((len(jobs), depth, rank), jnp.bfloat16),
+            pltpu.SemaphoreType.DMA((len(sources),)),
+            pltpu.SemaphoreType.DMA((len(jobs), most)),
         ],
         compiler_params=pltpu.CompilerParams(vmem_limit_bytes=56 * 2**20),
         cost_estimate=pl.CostEstimate(
-            flops=2 * tile_count * capacity * rows * depth * rank,
-            bytes_accessed=2 * depth * (tile_count * rank + blocks * rows),
+            flops=2 * cells * capacity * rows * rank,
+            bytes_accessed=2 * cells * rank + 2 * blocks * rows * sum(widths),
             transcendentals=0,
         ),
-    )(slots, counts, starts, footprints, *flat)
+    )(slots, counts, starts, *[f for f, _, _ in sources], *arrays, *extra)
 
 
 def information_sums(own, received, misfit, scale):
@@ -293,65 +316,100 @@
     over_top = [(i, (i - 4) % tile_count) for i in range(tile_count)]
     over_step = [(i, i ^ 1) for i in range(step_count)]
 
-    own_blocks = footprints[0]
-    theirs = lax.dynamic_slice_in_dim(own_blocks, (1 - side) * share, share, axis=2)
-    swapped = lax.ppermute(theirs, "tm", over_step)
     destination = targets[0, :, 0]
     other_destination = lax.ppermute(destination, "tm", over_step)
-
+    proposal, rounded, rims = make_proposal(flux, noise, prior_scale)
+
+    own_blocks = footprints[0]
+    begin = (1 - side) * share
+    to_send = lax.dynamic_slice_in_dim(own_blocks, begin, share, axis=2)
+    to_send, other_destination = lax.optimization_barrier((to_send, other_destination))
+    swapped = lax.ppermute(to_send, "tm", over_step)
+
+    basis, _, _ = lax.optimization_barrier((basis, rims, to_send))
+    own_half = lax.dynamic_slice_in_dim(basis, side * share, share, axis=0)
     cut = share // 2
-    own_half = lax.dynamic_slice_in_dim(basis, side * share, share, axis=0)
-    pieces = [own_half[:cut], own_half[cut:]]
-    near = [pieces]
+    first = own_half[:cut]
+    second = jnp.concatenate([own_half[cut:], rounded.reshape(-1, rank)], axis=0)
+
+    def forward(x):
+        return lax.ppermute(x, "space", over_last)
+
+    def both(way):
+        return jnp.concatenate([lax.ppermute(x, "space", way) for x in (first, second)], axis=0)
+
+    whole = [(0, share)]
+    near = [[(first, 0, cut), (second, 0, share - cut)]]
+    near_array, far_array = both(over_top), both(over_mid)
+    far = [[(far_array, 0, share)]]
+    tail = share + cell_count // rank
     for k in range(1, top):
-        near.append([lax.ppermute(piece, "space", over_top) for piece in near[k - 1]])
-    far = []
-    for k in range(top):
-        row = []
-        for p in range(2):
-            if k == top - 1 and p == 0 and k > 0:
-                row.append(lax.ppermute(far[k - 1][p], "space", over_top))
-            else:
-                row.append(lax.ppermute(near[k][p], "space", over_mid))
-        far.append(row)
-    tiles, tile_ids = [], []
+        if k > 1:
+            near_array = lax.ppermute(near_array, "space", over_top)
+        near.append([(near_array, 0, share)])
+        if k < top - 1:
+            far_array = lax.ppermute(near_array, "space", over_mid)
+            far.append([(far_array, 0, share)])
+        else:
+            cut = share // 2
+            upper = lax.ppermute(far_array[:cut], "space", over_top)
+            lower = lax.ppermute(near_array[cut:], "space", over_mid)
+            upper, lower, swapped = lax.optimization_barrier((upper, lower, swapped))
+            far.append([(upper, 0, cut), (lower, 0, share - cut)])
+
+    tiles, tile_ids, proposals = [], [], []
+
+    def proposal_of(pieces):
+        array, at, count = pieces[-1]
+        return array[at + count :].reshape(cell_count)
+
     for k in range(top):
         at = (place + 4 * k) % tile_count
         for held, index in ((near[k], at), (far[k], at ^ 2)):
-            tiles.append(held)
-            tile_ids.append(index)
-            tiles.append([lax.ppermute(piece, "space", over_last) for piece in held])
-            tile_ids.append(index ^ 1)
+            sibling = [(forward(array), first_row, count) for array, first_row, count in held]
+            for pieces, name in ((held, index), (sibling, index ^ 1)):
+                tiles.append(pieces)
+                tile_ids.append(name)
+                proposals.append(proposal_of(pieces))
     tile_ids = jnp.stack(tile_ids)
 
-    proposal = make_proposal(flux, noise, prior_scale)
-    halves = lax.all_gather(proposal.astype(jnp.bfloat16), "space", axis=0, tiled=True)
     every = lax.dot_general(
-        halves,
+        jnp.stack(proposals),
         own_blocks.reshape(block_count * obs_count, cell_count),
         (((1,), (1,)), ((), ())),
         preferred_element_type=jnp.float32,
     )
-    named = jnp.arange(tile_count)[:, None] == jnp.repeat(destination, obs_count)[None, :]
+    named = tile_ids[:, None] == jnp.repeat(destination, obs_count)[None, :]
     predicted = jnp.sum(jnp.where(named, every, 0.0), axis=0, keepdims=True)
     misfit = soundings.reshape(1, -1).astype(jnp.float32) - predicted
 
     slots, counts = slots_of(destination, tile_ids, capacity)
     other_slots, other_counts = slots_of(other_destination, tile_ids, capacity)
-    windows = [cut, share - cut]
-    start = (side * share).astype(jnp.int32)
-    starts = jnp.stack([start, start + cut])
+    mine = [(own_blocks, side * share, share)]
+    early = tile_count // 2
+    own = block_products(
+        slots, counts, mine, tiles, [(s, 0, share) for s in range(early)], capacity, jnp.float32
+    )
     others = block_products(
         other_slots,
         other_counts,
-        jnp.array([0, cut], jnp.int32),
-        swapped,
+        [(swapped, 0, share)],
         tiles,
-        windows,
+        [(s, 0, share) for s in range(tile_count)],
+        capacity,
         jnp.bfloat16,
     )
     received = lax.ppermute(others, "tm", over_step)
-    own = block_products(slots, counts, starts, own_blocks, tiles, windows, jnp.float32)
+    own = block_products(
+        slots,
+        counts,
+        mine,
+        tiles,
+        [(s, 0, share) for s in range(early, tile_count)],
+        capacity,
+        jnp.float32,
+        own,
+    )
     jac_scale = float(step_count * tile_count * block_count * obs_count) ** (-0.5)
     total = information_sums(own, received, misfit, jac_scale)
 

time: 221 us -> 186 us (0.84)
  matrix products: 27.7 us -> 5.67 us
  blocking collectives: 21.2 us -> 0 us
  local copies, waits for them, and re-layouts: 14.1 us -> 23.9 us
  starting transfers between devices: 40.5 us -> 35.2 us
  Pallas kernels: 38.5 us -> 41.2 us
  waiting for transfers between devices: 72.6 us -> 74.9 us
    dot_general x3 -> x1, matrix products: 27.7 us -> 5.67 us  [per_device(): lax.dot_general(jnp.stack(proposals), own_blocks.reshape(block_count * ob...]
    all_gather x1 -> x0, blocking collectives: 21.2 us -> none  [per_device(): lax.all_gather(proposal.astype(jnp.bfloat16), 'space', axis=0, tiled=True)]
    ppermute x33 -> x23, starting transfers between devices: 36.4 us -> 27.3 us  [the longest x4 9.96 us: both(): lax.ppermute(x, 'space', way)]
    ppermute x33 -> x23, waiting for transfers between devices: 48.5 us -> 56.8 us  [the longest x2 31.8 us: per_device(): near_array = lax.ppermute(near_array, 'space', over_top)]
    unnamed x44 -> x79, local copies, waits for them, and re-layouts: 3.4 us -> 9.21 us
    ppermute x3, waiting for transfers between devices: 15.6 us -> 12.6 us  [per_device(): mine = mine + lax.ppermute(mine, 'space', pairs)]
    ppermute x3, starting transfers between devices: 0.21 us -> 2.61 us  [per_device(): mine = mine + lax.ppermute(mine, 'space', pairs)]
    pallas_call x2 -> x3, Pallas kernels: 28.5 us -> 29.6 us  [block_products(): pl.pallas_call(kernel, out_shape=jax.ShapeDtypeStruct((blocks * rows, ran...]
  transfers between devices with their start and end apart: 41 -> 31, of which waited for: 13 -> 15; matrix products, arithmetic and copies ran while one was open for 18% -> 16% of each run, Pallas kernels for 7% -> 10%
where the time goes in v2:
time: 186 us; the launch traced here: 185 us
  waiting for transfers between devices  74.9 us (40%)
  Pallas kernels  41.2 us (22%)
  starting transfers between devices  35.2 us (19%)
  local copies, waits for them, and re-layouts  23.9 us (13%)
  matrix products  5.67 us (3%)
  other arithmetic  3.07 us (2%)
    ppermute x2, waiting for transfers between devices, per_device(): near_array = lax.ppermute(near_array, 'space', over_top)  31.8 us
    pallas_call x3, Pallas kernels, block_products(): pl.pallas_call(kernel, out_shape=jax.ShapeDtypeStruct((blocks * rows, ran...  29.6 us
    ppermute x4, waiting for transfers between devices, both(): lax.ppermute(x, 'space', way)  14 us
    ppermute x3, waiting for transfers between devices, per_device(): mine = mine + lax.ppermute(mine, 'space', pairs)  12.6 us
    ppermute x4, starting transfers between devices, both(): lax.ppermute(x, 'space', way)  9.96 us
    pallas_call x1, Pallas kernels, finish_factor(): pl.pallas_call(kernel, out_shape=(jax.ShapeDtypeStruct((rank, rank), jnp....  9.56 us
    unnamed x79, local copies, waits for them, and re-layouts  9.21 us
    ppermute x2, starting transfers between devices, per_device(): near_array = lax.ppermute(near_array, 'space', over_top)  8.56 us
  transfers between devices with their start and end apart: 31, of which 15 were waited for; matrix products, arithmetic and copies ran while one was open for 16% of the time, Pallas kernels for 10%

profile of v2, /device:TPU:0, one launch (start us, length us, event | category | flops | bytes accessed | tf_op | source)
XLA Modules:
  0.0 185.1 jit_solution(12138941162535726148)
XLA Ops:
  0.6 3.0 %collective-permute-start.2 = (s32[32]{0:T(128)}, s32[32]{0:T(128)S(1)}, u32[]{:S(2)}, u32[]{:S(2)}) collective-permute-start(s32[32]{0:T(128)} %bitcast.105), channel_id=1, source_target_pairs={{0,16},{16,0},{1,17},{17,1},{2,18},{18,2},{3,19},{19,3},{4,20},{20... | collective-permute-start | bytes 392 | tf_op jit(solution)/shard_map/ppermute | solution.py:320
  4.3 1.4 collective-permute-start
  5.8 1.3 collective-permute-start.1
  7.1 4.9 %dynamic-slice_bitcast_fusion = bf16[32,32,2048]{2,1,0:T(8,128)(2,1)} fusion(bf16[1,32,32,4096]{3,2,1,0:T(8,128)(2,1)} %param.10, s32[]{:T(128)S(6)} %select_n.63), kind=kLoop, calls=%fused_computation | loop fusion | bytes 8388612 | tf_op jit(solution)/shard_map/dynamic_slice | solution.py:325
  14.7 7.4 %collective-permute-start.8 = (bf16[1024,256]{1,0:T(8,128)(2,1)S(1)}, bf16[1024,256]{1,0:T(8,128)(2,1)S(1)}, u32[]{:S(2)}, u32[]{:S(2)}) collective-permute-start(bf16[1024,256]{1,0:T(8,128)(2,1)S(1)} %get-tuple-element.22.rest_1_), channel_id=1, source_target_pairs={{0,12},{1,13},{2,14},{3,15},{4,0},{5,1},{6,2},{7,3},{8,4},{9,5},{1... | collective-permute-start | bytes 1572872 | tf_op jit(solution)/shard_map/ppermute | solution.py:339
  22.9 1.7 shard_map.102
  27.8 1.4 collective-permute-start.4
  29.2 5.2 %collective-permute-done.8 = bf16[1024,256]{1,0:T(8,128)(2,1)S(1)} collective-permute-done((bf16[1024,256]{1,0:T(8,128)(2,1)S(1)}, bf16[1024,256]{1,0:T(8,128)(2,1)S(1)}, u32[]{:S(2)}, u32[]{:S(2)}) %collective-permute-start.8) | collective-permute-done | bytes 524320 | tf_op jit(solution)/shard_map/ppermute | solution.py:339
  35.3 8.6 %collective-permute-done.7 = bf16[1040,256]{1,0:T(8,128)(2,1)S(1)} collective-permute-done((bf16[1040,256]{1,0:T(8,128)(2,1)S(1)}, bf16[1040,256]{1,0:T(8,128)(2,1)S(1)}, u32[]{:S(2)}, u32[]{:S(2)}) %collective-permute-start.7) | collective-permute-done | bytes 532512 | tf_op jit(solution)/shard_map/ppermute | solution.py:339
  44.7 4.3 %collective-permute-start.12 = (bf16[2064,256]{1,0:T(8,128)(2,1)}, bf16[2064,256]{1,0:T(8,128)(2,1)}, u32[]{:S(2)}, u32[]{:S(2)}) collective-permute-start(bf16[2064,256]{1,0:T(8,128)(2,1)} %constant_dynamic-update-slice_fusion.2.rest_7_), channel_id=1, source_target_pairs={{0,12},{1,13},{2,14},{3,15},{4,0},{5,1},{6,2},{7,3},{8,4},{9,5},{1... | collective-permute-start | bytes 3170312 | tf_op jit(solution)/shard_map/ppermute | solution.py:348
  49.6 1.9 %constant_dynamic-update-slice_fusion.1 = bf16[2064,256]{1,0:T(8,128)(2,1)} fusion(bf16[1024,256]{1,0:T(8,128)(2,1)} %collective-permute-done.5), kind=kLoop, calls=%fused_computation.14 | loop fusion | bytes 1048576
  55.6 14.6 %collective-permute-done.12.rest_1_.rest_11_ = bf16[2064,256]{1,0:T(8,128)(2,1)} collective-permute-done((bf16[2064,256]{1,0:T(8,128)(2,1)}, bf16[2064,256]{1,0:T(8,128)(2,1)}, u32[]{:S(2)}, u32[]{:S(2)}) %collective-permute-start.12) | collective-permute-done | bytes 1056800 | tf_op jit(solution)/shard_map/ppermute | solution.py:348
  70.1 4.3 %collective-permute-start.16 = (bf16[2064,256]{1,0:T(8,128)(2,1)}, bf16[2064,256]{1,0:T(8,128)(2,1)S(1)}, u32[]{:S(2)}, u32[]{:S(2)}) collective-permute-start(bf16[2064,256]{1,0:T(8,128)(2,1)} %collective-permute-done.12.rest_1_.rest_11_), channel_id=1, source_target_pairs={{0,12},{1,13},{2,14},{3,15},{4,0},{5,1},{6,2},{7,3},{8,4},{9,5},{1... | collective-permute-start | bytes 3170312 | tf_op jit(solution)/shard_map/ppermute | solution.py:348
  77.4 17.3 %collective-permute-done.16.rest_5_.rest_15_ = bf16[2064,256]{1,0:T(8,128)(2,1)S(1)} collective-permute-done((bf16[2064,256]{1,0:T(8,128)(2,1)}, bf16[2064,256]{1,0:T(8,128)(2,1)S(1)}, u32[]{:S(2)}, u32[]{:S(2)}) %collective-permute-start.16) | collective-permute-done | bytes 1056800 | tf_op jit(solution)/shard_map/ppermute | solution.py:348
  94.6 2.1 %collective-permute-done.14.rest_3_.rest_13_ = bf16[2064,256]{1,0:T(8,128)(2,1)S(1)} collective-permute-done((bf16[2064,256]{1,0:T(8,128)(2,1)}, bf16[2064,256]{1,0:T(8,128)(2,1)S(1)}, u32[]{:S(2)}, u32[]{:S(2)}) %collective-permute-start.14) | collective-permute-done | bytes 1056800 | tf_op jit(solution)/shard_map/ppermute | solution.py:351
  99.0 1.5 collective-permute-start.19
  102.7 8.5 %shard_map.103.rest_11_ = f32[1024,256]{1,0:T(8,128)} custom-call(s32[64]{0:T(128)} %reshape.172.slots_ref, s32[16]{0:T(128)} %get-tuple-element.21.counts_ref, s32[1]{0:T(128)} %bitcast.19.starts_ref, bf16[32,32,4096]{2,1,0:T(8,128)(2,1)} %bitcast.86, bf16[1024,256]{1,0:T(8,128)(2,1)} %copy-done.4, bf16[1040,256]{1,0:T(8,128)(2,1)} %copy-done.3, ...), custom_call_target="tpu_custom_call" | custom-call | flops 1073741824 | bytes 12582912 | tf_op jit(solution)/shard_map/pallas_call | solution.py:148
  111.1 4.2 %collective-permute-done.18.rest_7_.rest_17_ = bf16[1024,256]{1,0:T(8,128)(2,1)S(1)} collective-permute-done((bf16[1024,256]{1,0:T(8,128)(2,1)}, bf16[1024,256]{1,0:T(8,128)(2,1)S(1)}, u32[]{:S(2)}, u32[]{:S(2)}) %collective-permute-start.18) | collective-permute-done | bytes 524320 | tf_op jit(solution)/shard_map/ppermute | solution.py:355
  115.4 2.6 %collective-permute-done.20.rest_0_ = bf16[32,32,2048]{2,1,0:T(8,128)(2,1)} collective-permute-done((bf16[32,32,2048]{2,1,0:T(8,128)(2,1)}, bf16[32,32,2048]{2,1,0:T(8,128)(2,1)}, u32[]{:S(2)}, u32[]{:S(2)}) %collective-permute-start.20) | collective-permute-done | bytes 4194336 | tf_op jit(solution)/shard_map/ppermute | solution.py:327
  118.6 2.0 %collective-permute-done.22.rest_9_.rest_19_ = bf16[1024,256]{1,0:T(8,128)(2,1)S(1)} collective-permute-done((bf16[1024,256]{1,0:T(8,128)(2,1)S(1)}, bf16[1024,256]{1,0:T(8,128)(2,1)S(1)}, u32[]{:S(2)}, u32[]{:S(2)}) %collective-permute-start.22) | collective-permute-done | bytes 524320 | tf_op jit(solution)/shard_map/ppermute | solution.py:336
  121.6 12.1 %shard_map.105 = bf16[1024,256]{1,0:T(8,128)(2,1)} custom-call(s32[64]{0:T(128)} %reshape.173.slots_ref, s32[16]{0:T(128)} %get-tuple-element.20.counts_ref, s32[1]{0:T(128)} %constant.74.clone.1.starts_ref, bf16[32,32,2048]{2,1,0:T(8,128)(2,1)} %collective-permute-done.20.rest_0_, bf16[1024,256]{1,0:T(8,128)(2,1)} %copy-done.4, ...), custom_call_target="tpu_custom_call" | custom-call | flops 2147483648 | bytes 20971520 | tf_op jit(solution)/shard_map/pallas_call | solution.py:148
  135.4 5.7 %fusion = f32[1024]{0:T(1024)S(1)} fusion(bf16[16,4096]{1,0:T(8,128)(2,1)S(1)} %stack.75, bf16[1024,4096]{1,0:T(8,128)(2,1)} %bitcast.87, s32[1024]{0:T(1024)S(1)} %eq.92, s32[16]{0:T(128)S(1)} %stack.74), kind=kOutput, calls=%fused_computation.2 | convolution fusion | flops 134265856 | bytes 8527936 | tf_op jit(solution)/shard_map/dot_general | solution.py:376
  141.1 9.0 %shard_map.104.own_ref = f32[1024,256]{1,0:T(8,128)} custom-call(s32[64]{0:T(128)} %reshape.172.slots_ref, s32[16]{0:T(128)} %get-tuple-element.21.counts_ref, s32[1]{0:T(128)} %bitcast.19.starts_ref, bf16[32,32,4096]{2,1,0:T(8,128)(2,1)} %bitcast.88, bf16[2064,256]{1,0:T(8,128)(2,1)} %collective-permute-done.12.rest_1_.rest_11_, ...), custom_call_target="tpu_custom_call" | custom-call | flops 1073741824 | bytes 12582912 | tf_op jit(solution)/shard_map/pallas_call | solution.py:148
  151.9 1.3 collective-permute-done.25
  153.2 1.6 collective-permute-start.26
  154.8 3.5 %collective-permute-done.26 = f32[104,256]{1,0:T(8,128)S(1)} collective-permute-done((f32[104,256]{1,0:T(8,128)S(1)}, f32[104,256]{1,0:T(8,128)S(1)}, u32[]{:S(2)}, u32[]{:S(2)}) %collective-permute-start.26) | collective-permute-done | bytes 106528 | tf_op jit(solution)/shard_map/ppermute | solution.py:424
  158.3 1.2 collective-permute-start.27
  159.5 3.5 %collective-permute-done.27 = f32[104,256]{1,0:T(8,128)S(1)} collective-permute-done((f32[104,256]{1,0:T(8,128)S(1)}, f32[104,256]{1,0:T(8,128)S(1)}, u32[]{:S(2)}, u32[]{:S(2)}) %collective-permute-start.27) | collective-permute-done | bytes 106528 | tf_op jit(solution)/shard_map/ppermute | solution.py:429
  163.1 1.3 collective-permute-start.28
  164.4 3.5 %collective-permute-done.28 = f32[104,256]{1,0:T(8,128)S(1)} collective-permute-done((f32[104,256]{1,0:T(8,128)S(1)}, f32[104,256]{1,0:T(8,128)S(1)}, u32[]{:S(2)}, u32[]{:S(2)}) %collective-permute-start.28) | collective-permute-done | bytes 106528 | tf_op jit(solution)/shard_map/ppermute | solution.py:429
  168.0 5.6 %collective-permute-done.29 = f32[104,256]{1,0:T(8,128)S(1)} collective-permute-done((f32[104,256]{1,0:T(8,128)S(1)}, f32[104,256]{1,0:T(8,128)S(1)}, u32[]{:S(2)}, u32[]{:S(2)}) %collective-permute-start.29) | collective-permute-done | bytes 106528 | tf_op jit(solution)/shard_map/ppermute | solution.py:429
  175.0 9.6 %shard_map.107 = (f32[256,256]{1,0:T(8,128)}, f32[8,256]{1,0:T(8,128)S(1)}) custom-call(f32[208,256]{1,0:T(8,128)S(1)} %maximum_select_fusion.in_ref), custom_call_target="tpu_custom_call" | custom-call | tf_op jit(solution)/shard_map/pallas_call | solution.py:289
  (159 shorter events, 28.0 us)
Async XLA Ops:
  0.6 14.0 %collective-permute-start.2 = (s32[32]{0:T(128)}, s32[32]{0:T(128)S(1)}, u32[]{:S(2)}, u32[]{:S(2)}) collective-permute-start(s32[32]{0:T(128)} %bitcast.105), channel_id=1, source_target_pairs={{0,16},{16,0},{1,17},{17,1},{2,18},{18,2},{3,19},{19,3},{4,20},{20... | collective-permute-start | bytes 392 | tf_op jit(solution)/shard_map/ppermute | solution.py:320
  4.3 10.3 %collective-permute-start = (f32[1,512]{1,0:T(1,128)S(1)}, f32[1,512]{1,0:T(1,128)S(1)}, u32[]{:S(2)}, u32[]{:S(2)}) collective-permute-start(f32[1,512]{1,0:T(1,128)S(1)} %get-tuple-element.24), channel_id=1, source_target_pairs={{0,1},{1,2},{2,3},{3,4},{4,5},{5,6},{6,7},{7,8},{8,9},{9,10},{10,1... | collective-permute-start | bytes 6152 | tf_op jit(solution)/shard_map/ppermute | solution.py:32
  5.8 8.8 %collective-permute-start.1 = (f32[1,512]{1,0:T(1,128)S(1)}, f32[1,512]{1,0:T(1,128)S(1)}, u32[]{:S(2)}, u32[]{:S(2)}) collective-permute-start(f32[1,512]{1,0:T(1,128)S(1)} %get-tuple-element.25), channel_id=1, source_target_pairs={{1,0},{2,1},{3,2},{4,3},{5,4},{6,5},{7,6},{8,7},{9,8},{10,9},{11,1... | collective-permute-start | bytes 6152 | tf_op jit(solution)/shard_map/ppermute | solution.py:33
  14.7 79.9 %copy-start.4 = (bf16[1024,256]{1,0:T(8,128)(2,1)}, bf16[1024,256]{1,0:T(8,128)(2,1)S(1)}, u32[]{:S(2)}) copy-start(bf16[1024,256]{1,0:T(8,128)(2,1)S(1)} %get-tuple-element.22.rest_1_) | copy-start | bytes 1572868
  14.7 19.7 %collective-permute-start.8 = (bf16[1024,256]{1,0:T(8,128)(2,1)S(1)}, bf16[1024,256]{1,0:T(8,128)(2,1)S(1)}, u32[]{:S(2)}, u32[]{:S(2)}) collective-permute-start(bf16[1024,256]{1,0:T(8,128)(2,1)S(1)} %get-tuple-element.22.rest_1_), channel_id=1, source_target_pairs={{0,12},{1,13},{2,14},{3,15},{4,0},{5,1},{6,2},{7,3},{8,4},{9,5},{1... | collective-permute-start | bytes 1572872 | tf_op jit(solution)/shard_map/ppermute | solution.py:339
  25.5 18.4 %collective-permute-start.7 = (bf16[1040,256]{1,0:T(8,128)(2,1)S(1)}, bf16[1040,256]{1,0:T(8,128)(2,1)S(1)}, u32[]{:S(2)}, u32[]{:S(2)}) collective-permute-start(bf16[1040,256]{1,0:T(8,128)(2,1)S(1)} %pad_maximum_fusion.rest_2_), channel_id=1, source_target_pairs={{0,12},{1,13},{2,14},{3,15},{4,0},{5,1},{6,2},{7,3},{8,4},{9,5},{1... | collective-permute-start | bytes 1597448 | tf_op jit(solution)/shard_map/ppermute | solution.py:339
  26.4 91.6 %collective-permute-start.20 = (bf16[32,32,2048]{2,1,0:T(8,128)(2,1)}, bf16[32,32,2048]{2,1,0:T(8,128)(2,1)}, u32[]{:S(2)}, u32[]{:S(2)}) collective-permute-start(bf16[32,32,2048]{2,1,0:T(8,128)(2,1)} %dynamic-slice_bitcast_fusion), channel_id=1, source_target_pairs={{0,16},{16,0},{1,17},{17,1},{2,18},{18,2},{3,19},{19,3},{4,20},{20... | collective-permute-start | bytes 12582920 | tf_op jit(solution)/shard_map/ppermute | solution.py:327
  27.0 22.0 %collective-permute-start.5 = (bf16[1024,256]{1,0:T(8,128)(2,1)S(1)}, bf16[1024,256]{1,0:T(8,128)(2,1)}, u32[]{:S(2)}, u32[]{:S(2)}) collective-permute-start(bf16[1024,256]{1,0:T(8,128)(2,1)S(1)} %get-tuple-element.22.rest_1_), channel_id=1, source_target_pairs={{0,2},{1,3},{2,0},{3,1},{4,6},{5,7},{6,4},{7,5},{8,10},{9,11},{10,... | collective-permute-start | bytes 1572872 | tf_op jit(solution)/shard_map/ppermute | solution.py:339
  27.8 23.8 %collective-permute-start.4 = (bf16[1040,256]{1,0:T(8,128)(2,1)S(1)}, bf16[1040,256]{1,0:T(8,128)(2,1)S(1)}, u32[]{:S(2)}, u32[]{:S(2)}) collective-permute-start(bf16[1040,256]{1,0:T(8,128)(2,1)S(1)} %pad_maximum_fusion.rest_2_), channel_id=1, source_target_pairs={{0,2},{1,3},{2,0},{3,1},{4,6},{5,7},{6,4},{7,5},{8,10},{9,11},{10,... | collective-permute-start | bytes 1597448 | tf_op jit(solution)/shard_map/ppermute | solution.py:339
  34.5 18.0 %collective-permute-start.3 = (bf16[1040,256]{1,0:T(8,128)(2,1)S(1)}, bf16[1040,256]{1,0:T(8,128)(2,1)S(1)}, u32[]{:S(2)}, u32[]{:S(2)}) collective-permute-start(bf16[1040,256]{1,0:T(8,128)(2,1)S(1)} %pad_maximum_fusion.rest_2_), channel_id=1, source_target_pairs={{0,1},{1,0},{2,3},{3,2},{4,5},{5,4},{6,7},{7,6},{8,9},{9,8},{10,11... | collective-permute-start | bytes 1597448 | tf_op jit(solution)/shard_map/ppermute | solution.py:336
  44.7 25.4 %collective-permute-start.12 = (bf16[2064,256]{1,0:T(8,128)(2,1)}, bf16[2064,256]{1,0:T(8,128)(2,1)}, u32[]{:S(2)}, u32[]{:S(2)}) collective-permute-start(bf16[2064,256]{1,0:T(8,128)(2,1)} %constant_dynamic-update-slice_fusion.2.rest_7_), channel_id=1, source_target_pairs={{0,12},{1,13},{2,14},{3,15},{4,0},{5,1},{6,2},{7,3},{8,4},{9,5},{1... | collective-permute-start | bytes 3170312 | tf_op jit(solution)/shard_map/ppermute | solution.py:348
  49.0 25.4 %collective-permute-start.10 = (bf16[2064,256]{1,0:T(8,128)(2,1)}, bf16[2064,256]{1,0:T(8,128)(2,1)}, u32[]{:S(2)}, u32[]{:S(2)}) collective-permute-start(bf16[2064,256]{1,0:T(8,128)(2,1)} %constant_dynamic-update-slice_fusion.2.rest_7_), channel_id=1, source_target_pairs={{0,2},{1,3},{2,0},{3,1},{4,6},{5,7},{6,4},{7,5},{8,10},{9,11},{10,... | collective-permute-start | bytes 3170312 | tf_op jit(solution)/shard_map/ppermute | solution.py:351
  51.6 23.0 %collective-permute-start.9 = (bf16[2064,256]{1,0:T(8,128)(2,1)}, bf16[2064,256]{1,0:T(8,128)(2,1)}, u32[]{:S(2)}, u32[]{:S(2)}) collective-permute-start(bf16[2064,256]{1,0:T(8,128)(2,1)} %constant_dynamic-update-slice_fusion.2.rest_7_), channel_id=1, source_target_pairs={{0,1},{1,0},{2,3},{3,2},{4,5},{5,4},{6,7},{7,6},{8,9},{9,8},{10,11... | collective-permute-start | bytes 3170312 | tf_op jit(solution)/shard_map/ppermute | solution.py:336
  52.5 22.2 %collective-permute-start.6 = (bf16[2064,256]{1,0:T(8,128)(2,1)}, bf16[2064,256]{1,0:T(8,128)(2,1)}, u32[]{:S(2)}, u32[]{:S(2)}) collective-permute-start(bf16[2064,256]{1,0:T(8,128)(2,1)} %constant_dynamic-update-slice_fusion.rest_5_), channel_id=1, source_target_pairs={{0,1},{1,0},{2,3},{3,2},{4,5},{5,4},{6,7},{7,6},{8,9},{9,8},{10,11... | collective-permute-start | bytes 3170312 | tf_op jit(solution)/shard_map/ppermute | solution.py:336
  70.1 24.5 %collective-permute-start.16 = (bf16[2064,256]{1,0:T(8,128)(2,1)}, bf16[2064,256]{1,0:T(8,128)(2,1)S(1)}, u32[]{:S(2)}, u32[]{:S(2)}) collective-permute-start(bf16[2064,256]{1,0:T(8,128)(2,1)} %collective-permute-done.12.rest_1_.rest_11_), channel_id=1, source_target_pairs={{0,12},{1,13},{2,14},{3,15},{4,0},{5,1},{6,2},{7,3},{8,4},{9,5},{1... | collective-permute-start | bytes 3170312 | tf_op jit(solution)/shard_map/ppermute | solution.py:348
  74.4 22.4 %collective-permute-start.14 = (bf16[2064,256]{1,0:T(8,128)(2,1)}, bf16[2064,256]{1,0:T(8,128)(2,1)S(1)}, u32[]{:S(2)}, u32[]{:S(2)}) collective-permute-start(bf16[2064,256]{1,0:T(8,128)(2,1)} %collective-permute-done.12.rest_1_.rest_11_), channel_id=1, source_target_pairs={{0,2},{1,3},{2,0},{3,1},{4,6},{5,7},{6,4},{7,5},{8,10},{9,11},{10,... | collective-permute-start | bytes 3170312 | tf_op jit(solution)/shard_map/ppermute | solution.py:351
  74.6 23.0 %collective-permute-start.11 = (bf16[2064,256]{1,0:T(8,128)(2,1)}, bf16[2064,256]{1,0:T(8,128)(2,1)S(1)}, u32[]{:S(2)}, u32[]{:S(2)}) collective-permute-start(bf16[2064,256]{1,0:T(8,128)(2,1)} %collective-permute-done.10.rest_9_), channel_id=1, source_target_pairs={{0,1},{1,0},{2,3},{3,2},{4,5},{5,4},{6,7},{7,6},{8,9},{9,8},{10,11... | collective-permute-start | bytes 3170312 | tf_op jit(solution)/shard_map/ppermute | solution.py:336
  74.7 24.3 %collective-permute-start.13 = (bf16[2064,256]{1,0:T(8,128)(2,1)}, bf16[2064,256]{1,0:T(8,128)(2,1)S(1)}, u32[]{:S(2)}, u32[]{:S(2)}) collective-permute-start(bf16[2064,256]{1,0:T(8,128)(2,1)} %collective-permute-done.12.rest_1_.rest_11_), channel_id=1, source_target_pairs={{0,1},{1,0},{2,3},{3,2},{4,5},{5,4},{6,7},{7,6},{8,9},{9,8},{10,11... | collective-permute-start | bytes 3170312 | tf_op jit(solution)/shard_map/ppermute | solution.py:336
  94.6 6.8 %collective-permute-start.23 = (bf16[1024,256]{1,0:T(8,128)(2,1)S(1)}, bf16[1024,256]{1,0:T(8,128)(2,1)S(1)}, u32[]{:S(2)}, u32[]{:S(2)}) collective-permute-start(bf16[1024,256]{1,0:T(8,128)(2,1)S(1)} %get-tuple-element.22.rest_1_), channel_id=1, source_target_pairs={{0,1},{1,0},{2,3},{3,2},{4,5},{5,4},{6,7},{7,6},{8,9},{9,8},{10,11... | collective-permute-start | bytes 1572872 | tf_op jit(solution)/shard_map/ppermute | solution.py:336
  96.8 21.7 %collective-permute-start.15 = (bf16[2064,256]{1,0:T(8,128)(2,1)S(1)}, bf16[2064,256]{1,0:T(8,128)(2,1)S(1)}, u32[]{:S(2)}, u32[]{:S(2)}) collective-permute-start(bf16[2064,256]{1,0:T(8,128)(2,1)S(1)} %collective-permute-done.14.rest_3_.rest_13_), channel_id=1, source_target_pairs={{0,1},{1,0},{2,3},{3,2},{4,5},{5,4},{6,7},{7,6},{8,9},{9,8},{10,11... | collective-permute-start | bytes 3170312 | tf_op jit(solution)/shard_map/ppermute | solution.py:336
  97.6 20.9 %collective-permute-start.17 = (bf16[2064,256]{1,0:T(8,128)(2,1)S(1)}, bf16[2064,256]{1,0:T(8,128)(2,1)S(1)}, u32[]{:S(2)}, u32[]{:S(2)}) collective-permute-start(bf16[2064,256]{1,0:T(8,128)(2,1)S(1)} %collective-permute-done.16.rest_5_.rest_15_), channel_id=1, source_target_pairs={{0,1},{1,0},{2,3},{3,2},{4,5},{5,4},{6,7},{7,6},{8,9},{9,8},{10,11... | collective-permute-start | bytes 3170312 | tf_op jit(solution)/shard_map/ppermute | solution.py:336
  99.0 16.3 %collective-permute-start.19 = (bf16[1040,256]{1,0:T(8,128)(2,1)}, bf16[1040,256]{1,0:T(8,128)(2,1)S(1)}, u32[]{:S(2)}, u32[]{:S(2)}) collective-permute-start(bf16[1040,256]{1,0:T(8,128)(2,1)} %slice.102), channel_id=1, source_target_pairs={{0,2},{1,3},{2,0},{3,1},{4,6},{5,7},{6,4},{7,5},{8,10},{9,11},{10,... | collective-permute-start | bytes 1597448 | tf_op jit(solution)/shard_map/ppermute | solution.py:356
  101.4 14.0 %collective-permute-start.18 = (bf16[1024,256]{1,0:T(8,128)(2,1)}, bf16[1024,256]{1,0:T(8,128)(2,1)S(1)}, u32[]{:S(2)}, u32[]{:S(2)}) collective-permute-start(bf16[1024,256]{1,0:T(8,128)(2,1)} %slice.101), channel_id=1, source_target_pairs={{0,12},{1,13},{2,14},{3,15},{4,0},{5,1},{6,2},{7,3},{8,4},{9,5},{1... | collective-permute-start | bytes 1572872 | tf_op jit(solution)/shard_map/ppermute | solution.py:355
  117.9 2.7 %collective-permute-start.21 = (bf16[1040,256]{1,0:T(8,128)(2,1)S(1)}, bf16[1040,256]{1,0:T(8,128)(2,1)S(1)}, u32[]{:S(2)}, u32[]{:S(2)}) collective-permute-start(bf16[1040,256]{1,0:T(8,128)(2,1)S(1)} %collective-permute-done.19.rest_8_.rest_18_), channel_id=1, source_target_pairs={{0,1},{1,0},{2,3},{3,2},{4,5},{5,4},{6,7},{7,6},{8,9},{9,8},{10,11... | collective-permute-start | bytes 1597448 | tf_op jit(solution)/shard_map/ppermute | solution.py:336
  117.9 2.7 %collective-permute-start.22 = (bf16[1024,256]{1,0:T(8,128)(2,1)S(1)}, bf16[1024,256]{1,0:T(8,128)(2,1)S(1)}, u32[]{:S(2)}, u32[]{:S(2)}) collective-permute-start(bf16[1024,256]{1,0:T(8,128)(2,1)S(1)} %collective-permute-done.18.rest_7_.rest_17_), channel_id=1, source_target_pairs={{0,1},{1,0},{2,3},{3,2},{4,5},{5,4},{6,7},{7,6},{8,9},{9,8},{10,11... | collective-permute-start | bytes 1572872 | tf_op jit(solution)/shard_map/ppermute | solution.py:336
  133.7 16.4 %collective-permute-start.24 = (bf16[1024,256]{1,0:T(8,128)(2,1)}, bf16[1024,256]{1,0:T(8,128)(2,1)S(1)}, u32[]{:S(2)}, u32[]{:S(2)}) collective-permute-start(bf16[1024,256]{1,0:T(8,128)(2,1)} %shard_map.105), channel_id=1, source_target_pairs={{0,16},{16,0},{1,17},{17,1},{2,18},{18,2},{3,19},{19,3},{4,20},{20... | collective-permute-start | bytes 1572872 | tf_op jit(solution)/shard_map/ppermute | solution.py:402
  151.8 1.4 collective-permute-start.25
  153.2 5.1 %collective-permute-start.26 = (f32[104,256]{1,0:T(8,128)S(1)}, f32[104,256]{1,0:T(8,128)S(1)}, u32[]{:S(2)}, u32[]{:S(2)}) collective-permute-start(f32[104,256]{1,0:T(8,128)S(1)} %dynamic-slice_add_fusion), channel_id=1, source_target_pairs={{0,16},{16,0},{1,17},{17,1},{2,18},{18,2},{3,19},{19,3},{4,20},{20... | collective-permute-start | bytes 319496 | tf_op jit(solution)/shard_map/ppermute | solution.py:424
  158.3 4.8 %collective-permute-start.27 = (f32[104,256]{1,0:T(8,128)S(1)}, f32[104,256]{1,0:T(8,128)S(1)}, u32[]{:S(2)}, u32[]{:S(2)}) collective-permute-start(f32[104,256]{1,0:T(8,128)S(1)} %add.79), channel_id=1, source_target_pairs={{0,2},{1,3},{2,0},{3,1},{4,6},{5,7},{6,4},{7,5},{8,10},{9,11},{10,... | collective-permute-start | bytes 319496 | tf_op jit(solution)/shard_map/ppermute | solution.py:429
  163.1 4.8 %collective-permute-start.28 = (f32[104,256]{1,0:T(8,128)S(1)}, f32[104,256]{1,0:T(8,128)S(1)}, u32[]{:S(2)}, u32[]{:S(2)}) collective-permute-start(f32[104,256]{1,0:T(8,128)S(1)} %add.80), channel_id=1, source_target_pairs={{0,4},{1,5},{2,6},{3,7},{4,0},{5,1},{6,2},{7,3},{8,12},{9,13},{10,... | collective-permute-start | bytes 319496 | tf_op jit(solution)/shard_map/ppermute | solution.py:429
  167.9 5.7 %collective-permute-start.29 = (f32[104,256]{1,0:T(8,128)S(1)}, f32[104,256]{1,0:T(8,128)S(1)}, u32[]{:S(2)}, u32[]{:S(2)}) collective-permute-start(f32[104,256]{1,0:T(8,128)S(1)} %add.81), channel_id=1, source_target_pairs={{0,8},{1,9},{2,10},{3,11},{4,12},{5,13},{6,14},{7,15},{8,0},{9,1},... | collective-permute-start | bytes 319496 | tf_op jit(solution)/shard_map/ppermute | solution.py:429
  173.6 1.4 collective-permute-start.30
  (22 other events, 229.6 us)

commit v3 on v2

--- a/solution.py
+++ b/solution.py
@@ -49,7 +49,7 @@
         kernel, out_shape=jax.ShapeDtypeStruct((edge, edge), jnp.float32)
     )(extended, flux.reshape(edge, edge), prior_scale.reshape(edge, edge))
     flat = proposal.reshape(1, cells)
-    return flat, flat.astype(jnp.bfloat16), (before, after)
+    return flat, flat.astype(jnp.bfloat16)
 
 
 def slots_of(destination, tile_ids, capacity):
@@ -81,97 +81,71 @@
             at += count
         copies.append(parts)
     most = max(len(parts) for parts in copies)
-    ahead = min(4, len(jobs))
 
     def kernel(slots_ref, counts_ref, starts_ref, *rest):
         f_refs, rest = rest[: len(sources)], rest[len(sources) :]
         b_refs, rest = rest[: len(arrays)], rest[len(arrays) :]
         if base is not None:
             base_ref, rest = rest[0], rest[1:]
-        out_ref, f_v, b_v, f_sem, b_sem = rest
-        f_copies = []
-        for i, width in enumerate(widths):
-            begin = pl.multiple_of(starts_ref[i], 128)
-            copy = pltpu.make_async_copy(
-                f_refs[i].at[:, :, pl.ds(begin, width)],
-                f_v.at[:, :, pl.ds(places[i], width)],
-                f_sem.at[i],
-            )
-            copy.start()
-            f_copies.append(copy)
-
-        def job_copies(n):
-            return [
-                pltpu.make_async_copy(
-                    b_refs[i].at[pl.ds(first, count)],
-                    b_v.at[n, pl.ds(place, count)],
-                    b_sem.at[n, part],
-                )
-                for part, (i, first, place, count) in enumerate(copies[n])
-            ]
-
-        for n in range(ahead):
-            for copy in job_copies(n):
-                copy.start()
+        (out_ref,) = rest
+        begin = pl.multiple_of(starts_ref[0], 128)
         if base is not None and out_dtype == jnp.float32:
             out_ref[...] = base_ref[...]
-        for copy in f_copies:
-            copy.wait()
         for n, (s, low, high) in enumerate(jobs):
-            if n + ahead < len(jobs):
-                for copy in job_copies(n + ahead):
-                    copy.start()
-            for copy in job_copies(n):
-                copy.wait()
             lhs = jnp.concatenate(
-                [f_v[slots_ref[s * capacity + j], :, low:high] for j in range(capacity)], axis=0
+                [
+                    f_refs[0][slots_ref[s * capacity + j], :, pl.ds(begin + low, high - low)]
+                    for j in range(capacity)
+                ],
+                axis=0,
             )
-            product = jnp.dot(
-                lhs, b_v[n, 0 : high - low, :], preferred_element_type=jnp.float32
-            )
+            parts = [b_refs[i][first : first + count, :] for i, first, _, count in copies[n]]
+            rhs = parts[0] if len(parts) == 1 else jnp.concatenate(parts, axis=0)
+            product = jnp.dot(lhs, rhs, preferred_element_type=jnp.float32)
             for j in range(capacity):
-
-                @pl.when(counts_ref[s] > j)
-                def _():
-                    at = pl.multiple_of(slots_ref[s * capacity + j] * rows, rows)
-                    part = product[j * rows : (j + 1) * rows]
-                    if low > 0:
-                        part = part + base_ref[pl.ds(at, rows), :]
-                    out_ref[pl.ds(at, rows), :] = part.astype(out_dtype)
+                block = jnp.where(counts_ref[s] > j, slots_ref[s * capacity + j], blocks)
+                at = pl.multiple_of(block * rows, rows)
+                part = product[j * rows : (j + 1) * rows]
+                if low > 0:
+                    part = part + base_ref[pl.ds(at, rows), :]
+                out_ref[pl.ds(at, rows), :] = part.astype(out_dtype)
+        out_ref[blocks * rows :, :] = jnp.zeros((rows, rank), out_dtype)
 
     smem = pl.BlockSpec(memory_space=pltpu.SMEM)
     vmem = pl.BlockSpec(memory_space=pltpu.VMEM)
     hbm = pl.BlockSpec(memory_space=pl.ANY)
     extra = [] if base is None else [base]
     starts = jnp.stack([jnp.asarray(first, jnp.int32) for _, first, _ in sources])
-    cells = sum(high - low for _, low, high in jobs)
     return pl.pallas_call(
         kernel,
-        out_shape=jax.ShapeDtypeStruct((blocks * rows, rank), out_dtype),
-        in_specs=[smem] * 3 + [hbm] * (len(sources) + len(arrays)) + [vmem] * len(extra),
+        out_shape=jax.ShapeDtypeStruct(((blocks + 1) * rows, rank), out_dtype),
+        in_specs=[smem] * 3 + [vmem] * (len(sources) + len(arrays) + len(extra)),
         out_specs=vmem,
-        scratch_shapes=[
-            pltpu.VMEM((blocks, rows, sum(widths)), jnp.bfloat16),
-            pltpu.VMEM((len(jobs), depth, rank), jnp.bfloat16),
-            pltpu.SemaphoreType.DMA((len(sources),)),
-            pltpu.SemaphoreType.DMA((len(jobs), most)),
-        ],
-        compiler_params=pltpu.CompilerParams(vmem_limit_bytes=56 * 2**20),
-        cost_estimate=pl.CostEstimate(
-            flops=2 * cells * capacity * rows * rank,
-            bytes_accessed=2 * cells * rank + 2 * blocks * rows * sum(widths),
-            transcendentals=0,
-        ),
+        compiler_params=pltpu.CompilerParams(vmem_limit_bytes=60 * 2**20),
+        cost_estimate=pl.CostEstimate(flops=1, bytes_accessed=1, transcendentals=0),
     )(slots, counts, starts, *[f for f, _, _ in sources], *arrays, *extra)
 
 
+def arrival(array):
+    def kernel(_, out_ref):
+        out_ref[0] = 0
+
+    return pl.pallas_call(
+        kernel,
+        out_shape=jax.ShapeDtypeStruct((1,), jnp.int32),
+        in_specs=[pl.BlockSpec(memory_space=pl.ANY)],
+        out_specs=pl.BlockSpec(memory_space=pltpu.SMEM),
+        cost_estimate=pl.CostEstimate(flops=1, bytes_accessed=100 * 2**20, transcendentals=0),
+    )(array)
+
+
 def information_sums(own, received, misfit, scale):
-    rows, rank = own.shape
+    rows, rank = misfit.shape[1], own.shape[1]
     half = rank // 2
     packed = half + half // 2 + 16
 
     def kernel(own_ref, received_ref, misfit_ref, out_ref):
-        jacobian = (own_ref[...] + received_ref[...].astype(jnp.float32)) * scale
+        jacobian = (own_ref[0:rows] + received_ref[0:rows].astype(jnp.float32)) * scale
         jacobian = jacobian.astype(jnp.bfloat16)
         gram = lax.dot_general(
             jacobian, jacobian, (((0,), (0,)), ((), ())), preferred_element_type=jnp.float32
@@ -318,31 +292,30 @@
 
     destination = targets[0, :, 0]
     other_destination = lax.ppermute(destination, "tm", over_step)
-    proposal, rounded, rims = make_proposal(flux, noise, prior_scale)
 
     own_blocks = footprints[0]
     begin = (1 - side) * share
     to_send = lax.dynamic_slice_in_dim(own_blocks, begin, share, axis=2)
     to_send, other_destination = lax.optimization_barrier((to_send, other_destination))
     swapped = lax.ppermute(to_send, "tm", over_step)
-
-    basis, _, _ = lax.optimization_barrier((basis, rims, to_send))
+    zero = arrival(swapped)[0]
+
+    noise, _ = lax.optimization_barrier((noise, to_send))
+    proposal, rounded = make_proposal(flux, noise, prior_scale)
     own_half = lax.dynamic_slice_in_dim(basis, side * share, share, axis=0)
-    cut = share // 2
-    first = own_half[:cut]
-    second = jnp.concatenate([own_half[cut:], rounded.reshape(-1, rank)], axis=0)
+    rounded = rounded.reshape(-1, rank)
 
     def forward(x):
         return lax.ppermute(x, "space", over_last)
 
     def both(way):
-        return jnp.concatenate([lax.ppermute(x, "space", way) for x in (first, second)], axis=0)
-
-    whole = [(0, share)]
-    near = [[(first, 0, cut), (second, 0, share - cut)]]
+        return jnp.concatenate(
+            [lax.ppermute(x, "space", way) for x in (own_half, rounded)], axis=0
+        )
+
+    near = [[(own_half, 0, share), (rounded, 0, 0)]]
     near_array, far_array = both(over_top), both(over_mid)
     far = [[(far_array, 0, share)]]
-    tail = share + cell_count // rank
     for k in range(1, top):
         if k > 1:
             near_array = lax.ppermute(near_array, "space", over_top)
@@ -354,23 +327,31 @@
             cut = share // 2
             upper = lax.ppermute(far_array[:cut], "space", over_top)
             lower = lax.ppermute(near_array[cut:], "space", over_mid)
-            upper, lower, swapped = lax.optimization_barrier((upper, lower, swapped))
             far.append([(upper, 0, cut), (lower, 0, share - cut)])
 
     tiles, tile_ids, proposals = [], [], []
 
-    def proposal_of(pieces):
-        array, at, count = pieces[-1]
-        return array[at + count :].reshape(cell_count)
+    def add_tile(pieces, index):
+        sibling = [(forward(array), first_row, count) for array, first_row, count in pieces]
+        for parts, name in ((pieces, index), (sibling, index ^ 1)):
+            tiles.append(parts)
+            tile_ids.append(name)
+            array, at, count = parts[-1]
+            proposals.append(array[at + count :].reshape(cell_count))
 
     for k in range(top):
-        at = (place + 4 * k) % tile_count
-        for held, index in ((near[k], at), (far[k], at ^ 2)):
-            sibling = [(forward(array), first_row, count) for array, first_row, count in held]
-            for pieces, name in ((held, index), (sibling, index ^ 1)):
-                tiles.append(pieces)
-                tile_ids.append(name)
-                proposals.append(proposal_of(pieces))
+        add_tile(near[k], (place + 4 * k) % tile_count)
+        if k < top - 1:
+            add_tile(far[k], ((place + 4 * k) % tile_count) ^ 2)
+    early = len(tiles) - 4
+    slots, counts = slots_of(destination, jnp.stack(tile_ids), capacity)
+    mine = [(own_blocks, side * share, share)]
+    own = block_products(
+        slots, counts, mine, tiles, [(s, 0, share) for s in range(early)], capacity, jnp.float32
+    )
+    upper, lower, own, zero = lax.optimization_barrier((upper, lower, own, zero))
+    far[-1] = [(upper, 0, cut), (lower, 0, share - cut)]
+    add_tile(far[-1], ((place + 4 * (top - 1)) % tile_count) ^ 2)
     tile_ids = jnp.stack(tile_ids)
 
     every = lax.dot_general(
@@ -385,15 +366,10 @@
 
     slots, counts = slots_of(destination, tile_ids, capacity)
     other_slots, other_counts = slots_of(other_destination, tile_ids, capacity)
-    mine = [(own_blocks, side * share, share)]
-    early = tile_count // 2
-    own = block_products(
-        slots, counts, mine, tiles, [(s, 0, share) for s in range(early)], capacity, jnp.float32
-    )
     others = block_products(
         other_slots,
         other_counts,
-        [(swapped, 0, share)],
+        [(swapped, zero, share)],
         tiles,
         [(s, 0, share) for s in range(tile_count)],
         capacity,

time: 186 us -> 182 us (0.978)
  waiting for transfers between devices: 74.9 us -> 56.1 us
  starting transfers between devices: 35.2 us -> 42.8 us
  local copies, waits for them, and re-layouts: 23.9 us -> 31.3 us
    ppermute x4, waiting for transfers between devices: 14 us -> 2.11 us  [both(): lax.ppermute(x, 'space', way)]
    ppermute x4, starting transfers between devices: 9.96 us -> 18.5 us  [both(): lax.ppermute(x, 'space', way)]
    unnamed x79 -> x58, local copies, waits for them, and re-layouts: 9.21 us -> 14.6 us
    ppermute x1, waiting for transfers between devices: 4.23 us -> 0.01 us  [per_device(): upper = lax.ppermute(far_array[:cut], 'space', over_top)]
    ppermute x1, starting transfers between devices: 1.16 us -> 4.28 us  [per_device(): upper = lax.ppermute(far_array[:cut], 'space', over_top)]
    ppermute x2, waiting for transfers between devices: 31.8 us -> 34.6 us  [per_device(): near_array = lax.ppermute(near_array, 'space', over_top)]
    ppermute x2, starting transfers between devices: 8.56 us -> 5.97 us  [per_device(): near_array = lax.ppermute(near_array, 'space', over_top)]
    ppermute x1, waiting for transfers between devices: 2.55 us -> 0.01 us  [per_device(): swapped = lax.ppermute(to_send, 'tm', over_step)]
  transfers between devices with their start and end apart: 31 -> 31, of which waited for: 15 -> 10; matrix products, arithmetic and copies ran while one was open for 16% -> 20% of each run, Pallas kernels for 10% -> 10%
where the time goes in v3:
time: 182 us; the launch traced here: 181 us
  waiting for transfers between devices  56.1 us (31%)
  starting transfers between devices  42.8 us (24%)
  Pallas kernels  39.8 us (22%)
  local copies, waits for them, and re-layouts  31.3 us (17%)
  matrix products  5.75 us (3%)
  other arithmetic  4.41 us (2%)
    ppermute x2, waiting for transfers between devices, per_device(): near_array = lax.ppermute(near_array, 'space', over_top)  34.6 us
    pallas_call x3, Pallas kernels, block_products(): pl.pallas_call(kernel, out_shape=jax.ShapeDtypeStruct(((blocks + 1) * row...  27.4 us
    ppermute x4, starting transfers between devices, both(): lax.ppermute(x, 'space', way)  18.5 us
    unnamed x58, local copies, waits for them, and re-layouts  14.6 us
    ppermute x3, waiting for transfers between devices, per_device(): mine = mine + lax.ppermute(mine, 'space', pairs)  12 us
    pallas_call x1, Pallas kernels, finish_factor(): pl.pallas_call(kernel, out_shape=(jax.ShapeDtypeStruct((rank, rank), jnp....  9.76 us
    ppermute x2, starting transfers between devices, per_device(): near_array = lax.ppermute(near_array, 'space', over_top)  5.97 us
    dot_general x1, matrix products, per_device(): lax.dot_general(jnp.stack(proposals), own_blocks.reshape(block_count * ob...  5.75 us
  transfers between devices with their start and end apart: 31, of which 10 were waited for; matrix products, arithmetic and copies ran while one was open for 20% of the time, Pallas kernels for 10%

profile of v3, /device:TPU:0, one launch (start us, length us, event | category | flops | bytes accessed | tf_op | source)
XLA Modules:
  0.0 181.2 jit_solution(15121342881632087400)
XLA Ops:
  0.7 1.6 copy-done
  3.3 5.0 %collective-permute-start.8 = (bf16[2048,256]{1,0:T(8,128)(2,1)}, bf16[2048,256]{1,0:T(8,128)(2,1)}, u32[]{:S(2)}, u32[]{:S(2)}) collective-permute-start(bf16[2048,256]{1,0:T(8,128)(2,1)} %constant_dynamic-slice_fusion.1.rest_1_), channel_id=1, source_target_pairs={{0,12},{1,13},{2,14},{3,15},{4,0},{5,1},{6,2},{7,3},{8,4},{9,5},{1... | collective-permute-start | bytes 3145736 | tf_op jit(solution)/shard_map/ppermute | solution.py:313
  8.3 1.5 collective-permute-start.5
  9.8 1.5 collective-permute-start
  11.3 4.8 %dynamic-slice_bitcast_fusion = bf16[32,32,2048]{2,1,0:T(8,128)(2,1)} fusion(bf16[1,32,32,4096]{3,2,1,0:T(8,128)(2,1)} %param.10, s32[]{:T(128)S(6)} %select_n.71), kind=kLoop, calls=%fused_computation | loop fusion | bytes 8388612 | tf_op jit(solution)/shard_map/dynamic_slice | solution.py:298
  17.4 1.3 collective-permute-start.2
  22.6 1.7 shard_map.102
  25.1 9.7 %collective-permute-start.7 = (bf16[16,256]{1,0:T(8,128)(2,1)S(1)}, bf16[16,256]{1,0:T(8,128)(2,1)S(1)}, u32[]{:S(2)}, u32[]{:S(2)}) collective-permute-start(bf16[16,256]{1,0:T(8,128)(2,1)S(1)} %convert_element_type.57), channel_id=1, source_target_pairs={{0,12},{1,13},{2,14},{3,15},{4,0},{5,1},{6,2},{7,3},{8,4},{9,5},{1... | collective-permute-start | bytes 24584 | tf_op jit(solution)/shard_map/ppermute | solution.py:313
  34.8 1.3 constant_dynamic-update-slice_fusion.3
  36.1 2.1 %collective-permute-done.7 = bf16[16,256]{1,0:T(8,128)(2,1)S(1)} collective-permute-done((bf16[16,256]{1,0:T(8,128)(2,1)S(1)}, bf16[16,256]{1,0:T(8,128)(2,1)S(1)}, u32[]{:S(2)}, u32[]{:S(2)}) %collective-permute-start.7) | collective-permute-done | bytes 8224 | tf_op jit(solution)/shard_map/ppermute | solution.py:313
  38.2 2.0 %collective-permute-start.12 = (bf16[2064,256]{1,0:T(8,128)(2,1)S(1)}, bf16[2064,256]{1,0:T(8,128)(2,1)}, u32[]{:S(2)}, u32[]{:S(2)}) collective-permute-start(bf16[2064,256]{1,0:T(8,128)(2,1)S(1)} %constant_dynamic-update-slice_fusion.2.rest_5_), channel_id=1, source_target_pairs={{0,12},{1,13},{2,14},{3,15},{4,0},{5,1},{6,2},{7,3},{8,4},{9,5},{1... | collective-permute-start | bytes 3170312 | tf_op jit(solution)/shard_map/ppermute | solution.py:321
  40.6 2.2 %collective-permute-start.4 = (bf16[16,256]{1,0:T(8,128)(2,1)S(1)}, bf16[16,256]{1,0:T(8,128)(2,1)S(1)}, u32[]{:S(2)}, u32[]{:S(2)}) collective-permute-start(bf16[16,256]{1,0:T(8,128)(2,1)S(1)} %convert_element_type.57), channel_id=1, source_target_pairs={{0,2},{1,3},{2,0},{3,1},{4,6},{5,7},{6,4},{7,5},{8,10},{9,11},{10,... | collective-permute-start | bytes 24584 | tf_op jit(solution)/shard_map/ppermute | solution.py:313
  43.3 2.3 %constant_dynamic-update-slice_fusion.1 = bf16[2064,256]{1,0:T(8,128)(2,1)} fusion(bf16[2048,256]{1,0:T(8,128)(2,1)} %collective-permute-done.5), kind=kLoop, calls=%fused_computation.16 | loop fusion | bytes 2097152
  46.8 17.4 %collective-permute-done.12.rest_9_ = bf16[2064,256]{1,0:T(8,128)(2,1)} collective-permute-done((bf16[2064,256]{1,0:T(8,128)(2,1)S(1)}, bf16[2064,256]{1,0:T(8,128)(2,1)}, u32[]{:S(2)}, u32[]{:S(2)}) %collective-permute-start.12) | collective-permute-done | bytes 1056800 | tf_op jit(solution)/shard_map/ppermute | solution.py:321
  64.2 3.9 %collective-permute-start.16 = (bf16[2064,256]{1,0:T(8,128)(2,1)}, bf16[2064,256]{1,0:T(8,128)(2,1)}, u32[]{:S(2)}, u32[]{:S(2)}) collective-permute-start(bf16[2064,256]{1,0:T(8,128)(2,1)} %collective-permute-done.12.rest_9_), channel_id=1, source_target_pairs={{0,12},{1,13},{2,14},{3,15},{4,0},{5,1},{6,2},{7,3},{8,4},{9,5},{1... | collective-permute-start | bytes 3170312 | tf_op jit(solution)/shard_map/ppermute | solution.py:321
  74.1 17.3 %collective-permute-done.16.rest_3_.rest_13_ = bf16[2064,256]{1,0:T(8,128)(2,1)} collective-permute-done((bf16[2064,256]{1,0:T(8,128)(2,1)}, bf16[2064,256]{1,0:T(8,128)(2,1)}, u32[]{:S(2)}, u32[]{:S(2)}) %collective-permute-start.16) | collective-permute-done | bytes 1056800 | tf_op jit(solution)/shard_map/ppermute | solution.py:321
  94.2 1.9 %slice.79 = bf16[1040,256]{1,0:T(8,128)(2,1)} slice(bf16[2064,256]{1,0:T(8,128)(2,1)} %collective-permute-done.16.rest_3_.rest_13_), slice={[1024:2064], [0:256]} | slice | bytes 1064960 | tf_op jit(solution)/shard_map/slice | solution.py:329
  96.4 2.0 %slice.78 = bf16[1024,256]{1,0:T(8,128)(2,1)} slice(bf16[2064,256]{1,0:T(8,128)(2,1)} %collective-permute-done.14.rest_1_.rest_11_), slice={[0:1024], [0:256]} | slice | bytes 1048576 | tf_op jit(solution)/shard_map/slice | solution.py:328
  99.3 4.3 %collective-permute-start.18 = (bf16[1024,256]{1,0:T(8,128)(2,1)}, bf16[1024,256]{1,0:T(8,128)(2,1)}, u32[]{:S(2)}, u32[]{:S(2)}) collective-permute-start(bf16[1024,256]{1,0:T(8,128)(2,1)} %slice.78), channel_id=1, source_target_pairs={{0,12},{1,13},{2,14},{3,15},{4,0},{5,1},{6,2},{7,3},{8,4},{9,5},{1... | collective-permute-start | bytes 1572872 | tf_op jit(solution)/shard_map/ppermute | solution.py:328
  104.6 9.0 %shard_map.103.rest_9_ = f32[1056,256]{1,0:T(8,128)} custom-call(s32[56]{0:T(128)} %reshape.230.slots_ref, s32[14]{0:T(128)} %convert_reduce_fusion.2.counts_ref, s32[1]{0:T(128)} %bitcast.18.starts_ref, bf16[32,32,4096]{2,1,0:T(8,128)(2,1)} %bitcast.85, bf16[2048,256]{1,0:T(8,128)(2,1)} %constant_dynamic-slice_fusion.1.rest_1_, ...), custom_call_target="tpu_custom_call" | custom-call | flops 1 | bytes 1 | tf_op jit(solution)/shard_map/pallas_call | solution.py:119
  119.4 10.8 %shard_map.106 = bf16[1056,256]{1,0:T(8,128)(2,1)} custom-call(s32[64]{0:T(128)} %reshape.232.slots_ref, s32[16]{0:T(128)} %get-tuple-element.22.counts_ref, s32[1]{0:T(128)} %bitcast.22.starts_ref, bf16[32,32,2048]{2,1,0:T(8,128)(2,1)} %collective-permute-done.21._.rest_0_, bf16[2048,256]{1,0:T(8,128)(2,1)} %constant_dynamic-slice_fusion.1.rest_1_, ...), custom_call_target="tpu_custom_call" | custom-call | flops 1 | bytes 1 | tf_op jit(solution)/shard_map/pallas_call | solution.py:119
  130.2 1.5 collective-permute-start.24
  132.4 7.5 %shard_map.105.own_ref = f32[1056,256]{1,0:T(8,128)} custom-call(s32[64]{0:T(128)} %reshape.231.slots_ref, s32[16]{0:T(128)} %get-tuple-element.23.counts_ref, s32[1]{0:T(128)} %bitcast.18.starts_ref, bf16[32,32,4096]{2,1,0:T(8,128)(2,1)} %bitcast.86, bf16[2064,256]{1,0:T(8,128)(2,1)} %collective-permute-done.14.rest_1_.rest_11_, ...), custom_call_target="tpu_custom_call" | custom-call | flops 1 | bytes 1 | tf_op jit(solution)/shard_map/pallas_call | solution.py:119
  140.3 5.8 %fusion = f32[1024]{0:T(1024)S(1)} fusion(bf16[16,4096]{1,0:T(8,128)(2,1)S(1)} %stack.97, bf16[1024,4096]{1,0:T(8,128)(2,1)} %bitcast.87, s32[1024]{0:T(1024)S(1)} %eq.130, s32[16]{0:T(128)S(1)} %stack.94), kind=kOutput, calls=%fused_computation.2 | convolution fusion | flops 134265856 | bytes 8527936 | tf_op jit(solution)/shard_map/dot_general | solution.py:357
  146.7 1.3 collective-permute-done.25
  148.6 4.5 %collective-permute-done.26 = f32[104,256]{1,0:T(8,128)S(1)} collective-permute-done((f32[104,256]{1,0:T(8,128)S(1)}, f32[104,256]{1,0:T(8,128)S(1)}, u32[]{:S(2)}, u32[]{:S(2)}) %collective-permute-start.26) | collective-permute-done | bytes 106528 | tf_op jit(solution)/shard_map/ppermute | solution.py:400
  153.1 1.8 collective-permute-start.27
  154.9 3.0 %collective-permute-done.27 = f32[104,256]{1,0:T(8,128)S(1)} collective-permute-done((f32[104,256]{1,0:T(8,128)S(1)}, f32[104,256]{1,0:T(8,128)S(1)}, u32[]{:S(2)}, u32[]{:S(2)}) %collective-permute-start.27) | collective-permute-done | bytes 106528 | tf_op jit(solution)/shard_map/ppermute | solution.py:405
  157.9 4.7 %collective-permute-done.28 = f32[104,256]{1,0:T(8,128)S(1)} collective-permute-done((f32[104,256]{1,0:T(8,128)S(1)}, f32[104,256]{1,0:T(8,128)S(1)}, u32[]{:S(2)}, u32[]{:S(2)}) %collective-permute-start.28) | collective-permute-done | bytes 106528 | tf_op jit(solution)/shard_map/ppermute | solution.py:405
  162.7 2.5 %collective-permute-start.29 = (f32[104,256]{1,0:T(8,128)S(1)}, f32[104,256]{1,0:T(8,128)S(1)}, u32[]{:S(2)}, u32[]{:S(2)}) collective-permute-start(f32[104,256]{1,0:T(8,128)S(1)} %add.93), channel_id=1, source_target_pairs={{0,8},{1,9},{2,10},{3,11},{4,12},{5,13},{6,14},{7,15},{8,0},{9,1},... | collective-permute-start | bytes 319496 | tf_op jit(solution)/shard_map/ppermute | solution.py:405
  165.1 4.4 %collective-permute-done.29 = f32[104,256]{1,0:T(8,128)S(1)} collective-permute-done((f32[104,256]{1,0:T(8,128)S(1)}, f32[104,256]{1,0:T(8,128)S(1)}, u32[]{:S(2)}, u32[]{:S(2)}) %collective-permute-start.29) | collective-permute-done | bytes 106528 | tf_op jit(solution)/shard_map/ppermute | solution.py:405
  170.9 9.8 %shard_map.108 = (f32[256,256]{1,0:T(8,128)}, f32[8,256]{1,0:T(8,128)S(1)}) custom-call(f32[208,256]{1,0:T(8,128)S(1)} %maximum_select_fusion.in_ref), custom_call_target="tpu_custom_call" | custom-call | tf_op jit(solution)/shard_map/pallas_call | solution.py:263
  (145 shorter events, 30.0 us)
Async XLA Ops:
  3.3 31.5 %collective-permute-start.8 = (bf16[2048,256]{1,0:T(8,128)(2,1)}, bf16[2048,256]{1,0:T(8,128)(2,1)}, u32[]{:S(2)}, u32[]{:S(2)}) collective-permute-start(bf16[2048,256]{1,0:T(8,128)(2,1)} %constant_dynamic-slice_fusion.1.rest_1_), channel_id=1, source_target_pairs={{0,12},{1,13},{2,14},{3,15},{4,0},{5,1},{6,2},{7,3},{8,4},{9,5},{1... | collective-permute-start | bytes 3145736 | tf_op jit(solution)/shard_map/ppermute | solution.py:313
  8.3 34.5 %collective-permute-start.5 = (bf16[2048,256]{1,0:T(8,128)(2,1)}, bf16[2048,256]{1,0:T(8,128)(2,1)}, u32[]{:S(2)}, u32[]{:S(2)}) collective-permute-start(bf16[2048,256]{1,0:T(8,128)(2,1)} %constant_dynamic-slice_fusion.1.rest_1_), channel_id=1, source_target_pairs={{0,2},{1,3},{2,0},{3,1},{4,6},{5,7},{6,4},{7,5},{8,10},{9,11},{10,... | collective-permute-start | bytes 3145736 | tf_op jit(solution)/shard_map/ppermute | solution.py:313
  9.8 6.3 %collective-permute-start = (s32[32]{0:T(128)S(1)}, s32[32]{0:T(128)S(1)}, u32[]{:S(2)}, u32[]{:S(2)}) collective-permute-start(s32[32]{0:T(128)S(1)} %bitcast.107), channel_id=1, source_target_pairs={{0,16},{16,0},{1,17},{17,1},{2,18},{18,2},{3,19},{19,3},{4,20},{20... | collective-permute-start | bytes 392 | tf_op jit(solution)/shard_map/ppermute | solution.py:294
  16.1 5.7 %collective-permute-start.1 = (f32[1,512]{1,0:T(1,128)S(1)}, f32[1,512]{1,0:T(1,128)S(1)}, u32[]{:S(2)}, u32[]{:S(2)}) collective-permute-start(f32[1,512]{1,0:T(1,128)S(1)} %get-tuple-element.24), channel_id=1, source_target_pairs={{0,1},{1,2},{2,3},{3,4},{4,5},{5,6},{6,7},{7,8},{8,9},{9,10},{10,1... | collective-permute-start | bytes 6152 | tf_op jit(solution)/shard_map/ppermute | solution.py:32
  17.4 4.4 %collective-permute-start.2 = (f32[1,512]{1,0:T(1,128)S(1)}, f32[1,512]{1,0:T(1,128)S(1)}, u32[]{:S(2)}, u32[]{:S(2)}) collective-permute-start(f32[1,512]{1,0:T(1,128)S(1)} %get-tuple-element.25), channel_id=1, source_target_pairs={{1,0},{2,1},{3,2},{4,3},{5,4},{6,5},{7,6},{8,7},{9,8},{10,9},{11,1... | collective-permute-start | bytes 6152 | tf_op jit(solution)/shard_map/ppermute | solution.py:33
  21.3 93.8 %collective-permute-start.21 = (bf16[32,32,2048]{2,1,0:T(8,128)(2,1)}, bf16[32,32,2048]{2,1,0:T(8,128)(2,1)}, u32[]{:S(2)}, u32[]{:S(2)}) collective-permute-start(bf16[32,32,2048]{2,1,0:T(8,128)(2,1)} %dynamic-slice_bitcast_fusion), channel_id=1, source_target_pairs={{0,16},{16,0},{1,17},{17,1},{2,18},{18,2},{3,19},{19,3},{4,20},{20... | collective-permute-start | bytes 12582920 | tf_op jit(solution)/shard_map/ppermute | solution.py:300
  25.1 13.1 %collective-permute-start.7 = (bf16[16,256]{1,0:T(8,128)(2,1)S(1)}, bf16[16,256]{1,0:T(8,128)(2,1)S(1)}, u32[]{:S(2)}, u32[]{:S(2)}) collective-permute-start(bf16[16,256]{1,0:T(8,128)(2,1)S(1)} %convert_element_type.57), channel_id=1, source_target_pairs={{0,12},{1,13},{2,14},{3,15},{4,0},{5,1},{6,2},{7,3},{8,4},{9,5},{1... | collective-permute-start | bytes 24584 | tf_op jit(solution)/shard_map/ppermute | solution.py:313
  38.2 26.0 %collective-permute-start.12 = (bf16[2064,256]{1,0:T(8,128)(2,1)S(1)}, bf16[2064,256]{1,0:T(8,128)(2,1)}, u32[]{:S(2)}, u32[]{:S(2)}) collective-permute-start(bf16[2064,256]{1,0:T(8,128)(2,1)S(1)} %constant_dynamic-update-slice_fusion.2.rest_5_), channel_id=1, source_target_pairs={{0,12},{1,13},{2,14},{3,15},{4,0},{5,1},{6,2},{7,3},{8,4},{9,5},{1... | collective-permute-start | bytes 3170312 | tf_op jit(solution)/shard_map/ppermute | solution.py:321
  40.6 32.7 %copy-start.7 = (f32[64,64]{1,0:T(8,128)S(1)}, f32[64,64]{1,0:T(8,128)}, u32[]{:S(2)}) copy-start(f32[64,64]{1,0:T(8,128)} %shard_map.102) | copy-start | bytes 49156
  40.6 5.0 %collective-permute-start.4 = (bf16[16,256]{1,0:T(8,128)(2,1)S(1)}, bf16[16,256]{1,0:T(8,128)(2,1)S(1)}, u32[]{:S(2)}, u32[]{:S(2)}) collective-permute-start(bf16[16,256]{1,0:T(8,128)(2,1)S(1)} %convert_element_type.57), channel_id=1, source_target_pairs={{0,2},{1,3},{2,0},{3,1},{4,6},{5,7},{6,4},{7,5},{8,10},{9,11},{10,... | collective-permute-start | bytes 24584 | tf_op jit(solution)/shard_map/ppermute | solution.py:313
  42.8 3.4 %collective-permute-start.3 = (bf16[16,256]{1,0:T(8,128)(2,1)S(1)}, bf16[16,256]{1,0:T(8,128)(2,1)S(1)}, u32[]{:S(2)}, u32[]{:S(2)}) collective-permute-start(bf16[16,256]{1,0:T(8,128)(2,1)S(1)} %convert_element_type.57), channel_id=1, source_target_pairs={{0,1},{1,0},{2,3},{3,2},{4,5},{5,4},{6,7},{7,6},{8,9},{9,8},{10,11... | collective-permute-start | bytes 24584 | tf_op jit(solution)/shard_map/ppermute | solution.py:309
  42.9 27.8 %collective-permute-start.10 = (bf16[2064,256]{1,0:T(8,128)(2,1)S(1)}, bf16[2064,256]{1,0:T(8,128)(2,1)}, u32[]{:S(2)}, u32[]{:S(2)}) collective-permute-start(bf16[2064,256]{1,0:T(8,128)(2,1)S(1)} %constant_dynamic-update-slice_fusion.2.rest_5_), channel_id=1, source_target_pairs={{0,2},{1,3},{2,0},{3,1},{4,6},{5,7},{6,4},{7,5},{8,10},{9,11},{10,... | collective-permute-start | bytes 3170312 | tf_op jit(solution)/shard_map/ppermute | solution.py:324
  46.2 24.5 %collective-permute-start.6 = (bf16[2064,256]{1,0:T(8,128)(2,1)}, bf16[2064,256]{1,0:T(8,128)(2,1)}, u32[]{:S(2)}, u32[]{:S(2)}) collective-permute-start(bf16[2064,256]{1,0:T(8,128)(2,1)} %constant_dynamic-update-slice_fusion.rest_3_), channel_id=1, source_target_pairs={{0,1},{1,0},{2,3},{3,2},{4,5},{5,4},{6,7},{7,6},{8,9},{9,8},{10,11... | collective-permute-start | bytes 3170312 | tf_op jit(solution)/shard_map/ppermute | solution.py:309
  46.3 27.2 %collective-permute-start.9 = (bf16[2064,256]{1,0:T(8,128)(2,1)S(1)}, bf16[2064,256]{1,0:T(8,128)(2,1)}, u32[]{:S(2)}, u32[]{:S(2)}) collective-permute-start(bf16[2064,256]{1,0:T(8,128)(2,1)S(1)} %constant_dynamic-update-slice_fusion.2.rest_5_), channel_id=1, source_target_pairs={{0,1},{1,0},{2,3},{3,2},{4,5},{5,4},{6,7},{7,6},{8,9},{9,8},{10,11... | collective-permute-start | bytes 3170312 | tf_op jit(solution)/shard_map/ppermute | solution.py:309
  64.2 27.1 %collective-permute-start.16 = (bf16[2064,256]{1,0:T(8,128)(2,1)}, bf16[2064,256]{1,0:T(8,128)(2,1)}, u32[]{:S(2)}, u32[]{:S(2)}) collective-permute-start(bf16[2064,256]{1,0:T(8,128)(2,1)} %collective-permute-done.12.rest_9_), channel_id=1, source_target_pairs={{0,12},{1,13},{2,14},{3,15},{4,0},{5,1},{6,2},{7,3},{8,4},{9,5},{1... | collective-permute-start | bytes 3170312 | tf_op jit(solution)/shard_map/ppermute | solution.py:321
  70.7 25.5 %collective-permute-start.14 = (bf16[2064,256]{1,0:T(8,128)(2,1)}, bf16[2064,256]{1,0:T(8,128)(2,1)}, u32[]{:S(2)}, u32[]{:S(2)}) collective-permute-start(bf16[2064,256]{1,0:T(8,128)(2,1)} %collective-permute-done.12.rest_9_), channel_id=1, source_target_pairs={{0,2},{1,3},{2,0},{3,1},{4,6},{5,7},{6,4},{7,5},{8,10},{9,11},{10,... | collective-permute-start | bytes 3170312 | tf_op jit(solution)/shard_map/ppermute | solution.py:324
  70.8 27.6 %collective-permute-start.11 = (bf16[2064,256]{1,0:T(8,128)(2,1)}, bf16[2064,256]{1,0:T(8,128)(2,1)}, u32[]{:S(2)}, u32[]{:S(2)}) collective-permute-start(bf16[2064,256]{1,0:T(8,128)(2,1)} %collective-permute-done.10.rest_7_), channel_id=1, source_target_pairs={{0,1},{1,0},{2,3},{3,2},{4,5},{5,4},{6,7},{7,6},{8,9},{9,8},{10,11... | collective-permute-start | bytes 3170312 | tf_op jit(solution)/shard_map/ppermute | solution.py:309
  73.5 25.8 %collective-permute-start.20 = (bf16[2048,256]{1,0:T(8,128)(2,1)}, bf16[2048,256]{1,0:T(8,128)(2,1)S(1)}, u32[]{:S(2)}, u32[]{:S(2)}) collective-permute-start(bf16[2048,256]{1,0:T(8,128)(2,1)} %constant_dynamic-slice_fusion.1.rest_1_), channel_id=1, source_target_pairs={{0,1},{1,0},{2,3},{3,2},{4,5},{5,4},{6,7},{7,6},{8,9},{9,8},{10,11... | collective-permute-start | bytes 3145736 | tf_op jit(solution)/shard_map/ppermute | solution.py:309
  91.3 12.2 %collective-permute-start.13 = (bf16[2064,256]{1,0:T(8,128)(2,1)}, bf16[2064,256]{1,0:T(8,128)(2,1)S(1)}, u32[]{:S(2)}, u32[]{:S(2)}) collective-permute-start(bf16[2064,256]{1,0:T(8,128)(2,1)} %collective-permute-done.12.rest_9_), channel_id=1, source_target_pairs={{0,1},{1,0},{2,3},{3,2},{4,5},{5,4},{6,7},{7,6},{8,9},{9,8},{10,11... | collective-permute-start | bytes 3170312 | tf_op jit(solution)/shard_map/ppermute | solution.py:309
  96.1 19.5 %collective-permute-start.19 = (bf16[1040,256]{1,0:T(8,128)(2,1)}, bf16[1040,256]{1,0:T(8,128)(2,1)S(1)}, u32[]{:S(2)}, u32[]{:S(2)}) collective-permute-start(bf16[1040,256]{1,0:T(8,128)(2,1)} %slice.79), channel_id=1, source_target_pairs={{0,2},{1,3},{2,0},{3,1},{4,6},{5,7},{6,4},{7,5},{8,10},{9,11},{10,... | collective-permute-start | bytes 1597448 | tf_op jit(solution)/shard_map/ppermute | solution.py:329
  98.4 17.8 %collective-permute-start.15 = (bf16[2064,256]{1,0:T(8,128)(2,1)}, bf16[2064,256]{1,0:T(8,128)(2,1)}, u32[]{:S(2)}, u32[]{:S(2)}) collective-permute-start(bf16[2064,256]{1,0:T(8,128)(2,1)} %collective-permute-done.14.rest_1_.rest_11_), channel_id=1, source_target_pairs={{0,1},{1,0},{2,3},{3,2},{4,5},{5,4},{6,7},{7,6},{8,9},{9,8},{10,11... | collective-permute-start | bytes 3170312 | tf_op jit(solution)/shard_map/ppermute | solution.py:309
  99.3 16.3 %collective-permute-start.18 = (bf16[1024,256]{1,0:T(8,128)(2,1)}, bf16[1024,256]{1,0:T(8,128)(2,1)}, u32[]{:S(2)}, u32[]{:S(2)}) collective-permute-start(bf16[1024,256]{1,0:T(8,128)(2,1)} %slice.78), channel_id=1, source_target_pairs={{0,12},{1,13},{2,14},{3,15},{4,0},{5,1},{6,2},{7,3},{8,4},{9,5},{1... | collective-permute-start | bytes 1572872 | tf_op jit(solution)/shard_map/ppermute | solution.py:328
  103.6 13.4 %collective-permute-start.17 = (bf16[2064,256]{1,0:T(8,128)(2,1)}, bf16[2064,256]{1,0:T(8,128)(2,1)}, u32[]{:S(2)}, u32[]{:S(2)}) collective-permute-start(bf16[2064,256]{1,0:T(8,128)(2,1)} %collective-permute-done.16.rest_3_.rest_13_), channel_id=1, source_target_pairs={{0,1},{1,0},{2,3},{3,2},{4,5},{5,4},{6,7},{7,6},{8,9},{9,8},{10,11... | collective-permute-start | bytes 3170312 | tf_op jit(solution)/shard_map/ppermute | solution.py:309
  115.6 3.0 %collective-permute-start.22 = (bf16[1040,256]{1,0:T(8,128)(2,1)S(1)}, bf16[1040,256]{1,0:T(8,128)(2,1)}, u32[]{:S(2)}, u32[]{:S(2)}) collective-permute-start(bf16[1040,256]{1,0:T(8,128)(2,1)S(1)} %collective-permute-done.19.rest_6_.rest_16_), channel_id=1, source_target_pairs={{0,1},{1,0},{2,3},{3,2},{4,5},{5,4},{6,7},{7,6},{8,9},{9,8},{10,11... | collective-permute-start | bytes 1597448 | tf_op jit(solution)/shard_map/ppermute | solution.py:309
  115.7 2.9 %collective-permute-start.23 = (bf16[1024,256]{1,0:T(8,128)(2,1)}, bf16[1024,256]{1,0:T(8,128)(2,1)S(1)}, u32[]{:S(2)}, u32[]{:S(2)}) collective-permute-start(bf16[1024,256]{1,0:T(8,128)(2,1)} %collective-permute-done.18.rest_5_.rest_15_), channel_id=1, source_target_pairs={{0,1},{1,0},{2,3},{3,2},{4,5},{5,4},{6,7},{7,6},{8,9},{9,8},{10,11... | collective-permute-start | bytes 1572872 | tf_op jit(solution)/shard_map/ppermute | solution.py:309
  130.2 15.9 %collective-permute-start.24 = (bf16[1056,256]{1,0:T(8,128)(2,1)}, bf16[1056,256]{1,0:T(8,128)(2,1)S(1)}, u32[]{:S(2)}, u32[]{:S(2)}) collective-permute-start(bf16[1056,256]{1,0:T(8,128)(2,1)} %shard_map.106), channel_id=1, source_target_pairs={{0,16},{16,0},{1,17},{17,1},{2,18},{18,2},{3,19},{19,3},{4,20},{20... | collective-permute-start | bytes 1622024 | tf_op jit(solution)/shard_map/ppermute | solution.py:378
  146.6 1.4 collective-permute-start.25
  148.0 5.1 %collective-permute-start.26 = (f32[104,256]{1,0:T(8,128)S(1)}, f32[104,256]{1,0:T(8,128)S(1)}, u32[]{:S(2)}, u32[]{:S(2)}) collective-permute-start(f32[104,256]{1,0:T(8,128)S(1)} %dynamic-slice_add_fusion), channel_id=1, source_target_pairs={{0,16},{16,0},{1,17},{17,1},{2,18},{18,2},{3,19},{19,3},{4,20},{20... | collective-permute-start | bytes 319496 | tf_op jit(solution)/shard_map/ppermute | solution.py:400
  153.1 4.8 %collective-permute-start.27 = (f32[104,256]{1,0:T(8,128)S(1)}, f32[104,256]{1,0:T(8,128)S(1)}, u32[]{:S(2)}, u32[]{:S(2)}) collective-permute-start(f32[104,256]{1,0:T(8,128)S(1)} %add.91), channel_id=1, source_target_pairs={{0,2},{1,3},{2,0},{3,1},{4,6},{5,7},{6,4},{7,5},{8,10},{9,11},{10,... | collective-permute-start | bytes 319496 | tf_op jit(solution)/shard_map/ppermute | solution.py:405
  157.9 4.8 %collective-permute-start.28 = (f32[104,256]{1,0:T(8,128)S(1)}, f32[104,256]{1,0:T(8,128)S(1)}, u32[]{:S(2)}, u32[]{:S(2)}) collective-permute-start(f32[104,256]{1,0:T(8,128)S(1)} %add.92), channel_id=1, source_target_pairs={{0,4},{1,5},{2,6},{3,7},{4,0},{5,1},{6,2},{7,3},{8,12},{9,13},{10,... | collective-permute-start | bytes 319496 | tf_op jit(solution)/shard_map/ppermute | solution.py:405
  162.7 6.8 %collective-permute-start.29 = (f32[104,256]{1,0:T(8,128)S(1)}, f32[104,256]{1,0:T(8,128)S(1)}, u32[]{:S(2)}, u32[]{:S(2)}) collective-permute-start(f32[104,256]{1,0:T(8,128)S(1)} %add.93), channel_id=1, source_target_pairs={{0,8},{1,9},{2,10},{3,11},{4,12},{5,13},{6,14},{7,15},{8,0},{9,1},... | collective-permute-start | bytes 319496 | tf_op jit(solution)/shard_map/ppermute | solution.py:405
  169.5 1.4 collective-permute-start.30
  (13 other events, 109.3 us)

commit v4 on v3

--- a/solution.py
+++ b/solution.py
@@ -141,8 +141,8 @@
 
 def information_sums(own, received, misfit, scale):
     rows, rank = misfit.shape[1], own.shape[1]
-    half = rank // 2
-    packed = half + half // 2 + 16
+    half, part = rank // 2, rank // 4
+    blocks = 2 * part + part // 2
 
     def kernel(own_ref, received_ref, misfit_ref, out_ref):
         jacobian = (own_ref[0:rows] + received_ref[0:rows].astype(jnp.float32)) * scale
@@ -150,45 +150,61 @@
         gram = lax.dot_general(
             jacobian, jacobian, (((0,), (0,)), ((), ())), preferred_element_type=jnp.float32
         )
-        out_ref[0:half, :] = gram[0:half, :]
-        out_ref[half : half + half // 2, 0:half] = gram[half : half + half // 2, half:]
-        out_ref[half : half + half // 2, half:] = gram[half + half // 2 :, half:]
+        out_ref[0:part, :] = gram[0:part, :]
+        out_ref[part:half, part:] = gram[part:half, part:]
+        out_ref[part:half, 0:part] = gram[half + part :, half + part :]
+        out_ref[half:blocks, 0:half] = gram[half : half + part // 2, half:]
+        out_ref[half:blocks, half:] = gram[half + part // 2 : half + part, half:]
         rest = misfit_ref[...]
         parts = []
         for _ in range(3):
-            part = rest.astype(jnp.bfloat16)
-            parts.append(part)
-            rest = rest - part.astype(jnp.float32)
+            piece = rest.astype(jnp.bfloat16)
+            parts.append(piece)
+            rest = rest - piece.astype(jnp.float32)
         lhs = jnp.concatenate(parts + [jnp.zeros((16 - 3, rows), jnp.bfloat16)], axis=0)
         projected = jnp.dot(lhs, jacobian, preferred_element_type=jnp.float32)
         total = projected[0:1] + projected[1:2] + projected[2:3]
-        out_ref[half + half // 2 :, :] = jnp.broadcast_to(total, (16, rank))
+        out_ref[blocks:, :] = jnp.broadcast_to(total, (16, rank))
 
     return pl.pallas_call(
         kernel,
-        out_shape=jax.ShapeDtypeStruct((packed, rank), jnp.float32),
+        out_shape=jax.ShapeDtypeStruct((blocks + 16, rank), jnp.float32),
         compiler_params=pltpu.CompilerParams(vmem_limit_bytes=32 * 2**20),
     )(own, received, misfit)
 
 
-def finish_factor(packed):
-    rank = packed.shape[1]
-    half = rank // 2
-    quarter = half // 2
+def finish_factor(mine, back, last):
+    rank = mine.shape[1]
+    half, strip = rank // 2, rank // 4
     wide = rank + 128
-    strip = 64
-
-    def kernel(in_ref, up_ref, rhs_ref, work, factor):
-        top = in_ref[0:half, :]
-        work[0:half, 0:rank] = top
-        work[half:, 0:half] = top[:, half:].T
-        work[half : half + quarter, half:rank] = in_ref[half : half + quarter, 0:half]
-        work[half + quarter :, half:rank] = in_ref[half : half + quarter, half:]
+    blocks = 2 * strip + strip // 2
+
+    def kernel(last_ref, mine_ref, back_ref, up_ref, rhs_ref, sums, work, factor):
+        own_half = mine_ref.shape[0]
+
+        @pl.when(last_ref[0] == 0)
+        def _():
+            sums[0:own_half, :] = mine_ref[...]
+            sums[own_half:, :] = back_ref[...]
+
+        @pl.when(last_ref[0] != 0)
+        def _():
+            sums[0:own_half, :] = back_ref[...]
+            sums[own_half:, :] = mine_ref[...]
+
+        work[0:strip, 0:rank] = sums[0:strip, :]
+        work[strip:half, 0:rank] = sums[strip:half, :]
+        work[half : half + strip // 2, half:rank] = sums[half:blocks, 0:half]
+        work[half + strip // 2 : half + strip, half:rank] = sums[half:blocks, half:]
+        corner = sums[strip:half, 0:half]
+        work[half + strip :, half:rank] = jnp.concatenate(
+            [jnp.zeros((strip, strip), jnp.float32), corner[:, 0:strip]], axis=1
+        )
         for k in range(0, rank, 128):
             row = lax.broadcasted_iota(jnp.int32, (128, 128), 0)
             col = lax.broadcasted_iota(jnp.int32, (128, 128), 1)
             work[k : k + 128, k : k + 128] += (row == col).astype(jnp.float32)
-        column = in_ref[half + quarter : half + quarter + 8, :].T
+        column = sums[blocks : blocks + 8, :].T
         work[:, rank:] = jnp.broadcast_to(column[:, 0:1], (rank, 128))
 
         sub = lax.broadcasted_iota(jnp.int32, (8, wide), 0)
@@ -258,20 +274,23 @@
                     up_ref[k : k + 128, c : c + 128] = jnp.where(
                         col >= row, factor[k : k + 128, c : c + 128], 0.0
                     )
-            rhs_ref[:, k : k + 128] = factor[k : k + 128, rank:].T[0:8, :]
+            rhs_ref[:, k : k + 128] = factor[k : k + 128, rank:].T[0:1, :]
 
     return pl.pallas_call(
         kernel,
         out_shape=(
             jax.ShapeDtypeStruct((rank, rank), jnp.float32),
-            jax.ShapeDtypeStruct((8, rank), jnp.float32),
+            jax.ShapeDtypeStruct((1, rank), jnp.float32),
         ),
+        in_specs=[pl.BlockSpec(memory_space=pltpu.SMEM)]
+        + [pl.BlockSpec(memory_space=pltpu.VMEM)] * 2,
         scratch_shapes=[
+            pltpu.VMEM((blocks + 16, rank), jnp.float32),
             pltpu.VMEM((rank, wide), jnp.float32),
             pltpu.VMEM((rank, wide), jnp.float32),
         ],
         compiler_params=pltpu.CompilerParams(vmem_limit_bytes=32 * 2**20),
-    )(packed)
+    )(last.astype(jnp.int32).reshape(1), mine, back)
 
 
 def per_device(flux, noise, prior_scale, footprints, soundings, targets, basis):
@@ -405,15 +424,12 @@
         mine = mine + lax.ppermute(mine, "space", pairs)
         shift *= 2
     back = lax.ppermute(mine, "space", over_last)
-    packed = jnp.where(
-        last == 0, jnp.concatenate([mine, back]), jnp.concatenate([back, mine])
-    )
-    factor_up, rhs = finish_factor(packed)
+    factor_up, rhs = finish_factor(mine, back, last)
     return (
         proposal,
         predicted.reshape(1, block_count, obs_count),
         factor_up,
-        rhs[0],
+        rhs.reshape(rank),
     )
 
 

time: 182 us -> 180 us (0.989)
  waiting for transfers between devices: 56.1 us -> 54.1 us
  transfers between devices with their start and end apart: 31 -> 31, of which waited for: 10 -> 10; matrix products, arithmetic and copies ran while one was open for 20% -> 20% of each run, Pallas kernels for 10% -> 11%
where the time goes in v4:
time: 180 us; the launch traced here: 179 us
  waiting for transfers between devices  54.1 us (30%)
  starting transfers between devices  42.8 us (24%)
  Pallas kernels  39.8 us (22%)
  local copies, waits for them, and re-layouts  30.7 us (17%)
  matrix products  5.75 us (3%)
  other arithmetic  4.36 us (2%)
    ppermute x2, waiting for transfers between devices, per_device(): near_array = lax.ppermute(near_array, 'space', over_top)  34.7 us
    pallas_call x3, Pallas kernels, block_products(): pl.pallas_call(kernel, out_shape=jax.ShapeDtypeStruct(((blocks + 1) * row...  27.3 us
    ppermute x4, starting transfers between devices, both(): lax.ppermute(x, 'space', way)  18.5 us
    unnamed x58, local copies, waits for them, and re-layouts  14.6 us
    ppermute x3, waiting for transfers between devices, per_device(): mine = mine + lax.ppermute(mine, 'space', pairs)  10.3 us
    pallas_call x1, Pallas kernels, finish_factor(): pl.pallas_call(kernel, out_shape=(jax.ShapeDtypeStruct((rank, rank), jnp....  9.81 us
    ppermute x2, starting transfers between devices, per_device(): near_array = lax.ppermute(near_array, 'space', over_top)  5.97 us
    dot_general x1, matrix products, per_device(): lax.dot_general(jnp.stack(proposals), own_blocks.reshape(block_count * ob...  5.75 us
  transfers between devices with their start and end apart: 31, of which 10 were waited for; matrix products, arithmetic and copies ran while one was open for 20% of the time, Pallas kernels for 11%

profile of v4, /device:TPU:0, one launch (start us, length us, event | category | flops | bytes accessed | tf_op | source)
XLA Modules:
  0.0 178.6 jit_solution(7608555907877570063)
XLA Ops:
  0.7 1.6 copy-done
  3.3 5.0 %collective-permute-start.8 = (bf16[2048,256]{1,0:T(8,128)(2,1)}, bf16[2048,256]{1,0:T(8,128)(2,1)}, u32[]{:S(2)}, u32[]{:S(2)}) collective-permute-start(bf16[2048,256]{1,0:T(8,128)(2,1)} %constant_dynamic-slice_fusion.1.rest_1_), channel_id=1, source_target_pairs={{0,12},{1,13},{2,14},{3,15},{4,0},{5,1},{6,2},{7,3},{8,4},{9,5},{1... | collective-permute-start | bytes 3145736 | tf_op jit(solution)/shard_map/ppermute | solution.py:332
  8.3 1.5 collective-permute-start.5
  9.8 1.5 collective-permute-start
  11.3 4.8 %dynamic-slice_bitcast_fusion = bf16[32,32,2048]{2,1,0:T(8,128)(2,1)} fusion(bf16[1,32,32,4096]{3,2,1,0:T(8,128)(2,1)} %param.10, s32[]{:T(128)S(6)} %select_n.63), kind=kLoop, calls=%fused_computation | loop fusion | bytes 8388612 | tf_op jit(solution)/shard_map/dynamic_slice | solution.py:317
  16.1 1.3 collective-permute-start.1
  17.4 1.3 collective-permute-start.2
  22.6 1.7 shard_map.102
  25.1 9.7 %collective-permute-start.7 = (bf16[16,256]{1,0:T(8,128)(2,1)S(1)}, bf16[16,256]{1,0:T(8,128)(2,1)S(1)}, u32[]{:S(2)}, u32[]{:S(2)}) collective-permute-start(bf16[16,256]{1,0:T(8,128)(2,1)S(1)} %convert_element_type.57), channel_id=1, source_target_pairs={{0,12},{1,13},{2,14},{3,15},{4,0},{5,1},{6,2},{7,3},{8,4},{9,5},{1... | collective-permute-start | bytes 24584 | tf_op jit(solution)/shard_map/ppermute | solution.py:332
  34.8 1.3 constant_dynamic-update-slice_fusion.3
  36.1 2.1 %collective-permute-done.7 = bf16[16,256]{1,0:T(8,128)(2,1)S(1)} collective-permute-done((bf16[16,256]{1,0:T(8,128)(2,1)S(1)}, bf16[16,256]{1,0:T(8,128)(2,1)S(1)}, u32[]{:S(2)}, u32[]{:S(2)}) %collective-permute-start.7) | collective-permute-done | bytes 8224 | tf_op jit(solution)/shard_map/ppermute | solution.py:332
  38.2 2.0 %collective-permute-start.12 = (bf16[2064,256]{1,0:T(8,128)(2,1)S(1)}, bf16[2064,256]{1,0:T(8,128)(2,1)}, u32[]{:S(2)}, u32[]{:S(2)}) collective-permute-start(bf16[2064,256]{1,0:T(8,128)(2,1)S(1)} %constant_dynamic-update-slice_fusion.2.rest_5_), channel_id=1, source_target_pairs={{0,12},{1,13},{2,14},{3,15},{4,0},{5,1},{6,2},{7,3},{8,4},{9,5},{1... | collective-permute-start | bytes 3170312 | tf_op jit(solution)/shard_map/ppermute | solution.py:340
  40.6 2.2 %collective-permute-start.4 = (bf16[16,256]{1,0:T(8,128)(2,1)S(1)}, bf16[16,256]{1,0:T(8,128)(2,1)S(1)}, u32[]{:S(2)}, u32[]{:S(2)}) collective-permute-start(bf16[16,256]{1,0:T(8,128)(2,1)S(1)} %convert_element_type.57), channel_id=1, source_target_pairs={{0,2},{1,3},{2,0},{3,1},{4,6},{5,7},{6,4},{7,5},{8,10},{9,11},{10,... | collective-permute-start | bytes 24584 | tf_op jit(solution)/shard_map/ppermute | solution.py:332
  43.3 2.3 %constant_dynamic-update-slice_fusion.1 = bf16[2064,256]{1,0:T(8,128)(2,1)} fusion(bf16[2048,256]{1,0:T(8,128)(2,1)} %collective-permute-done.5), kind=kLoop, calls=%fused_computation.15 | loop fusion | bytes 2097152
  46.8 17.4 %collective-permute-done.12.rest_9_ = bf16[2064,256]{1,0:T(8,128)(2,1)} collective-permute-done((bf16[2064,256]{1,0:T(8,128)(2,1)S(1)}, bf16[2064,256]{1,0:T(8,128)(2,1)}, u32[]{:S(2)}, u32[]{:S(2)}) %collective-permute-start.12) | collective-permute-done | bytes 1056800 | tf_op jit(solution)/shard_map/ppermute | solution.py:340
  64.2 3.9 %collective-permute-start.16 = (bf16[2064,256]{1,0:T(8,128)(2,1)}, bf16[2064,256]{1,0:T(8,128)(2,1)}, u32[]{:S(2)}, u32[]{:S(2)}) collective-permute-start(bf16[2064,256]{1,0:T(8,128)(2,1)} %collective-permute-done.12.rest_9_), channel_id=1, source_target_pairs={{0,12},{1,13},{2,14},{3,15},{4,0},{5,1},{6,2},{7,3},{8,4},{9,5},{1... | collective-permute-start | bytes 3170312 | tf_op jit(solution)/shard_map/ppermute | solution.py:340
  74.1 17.3 %collective-permute-done.16.rest_3_.rest_13_ = bf16[2064,256]{1,0:T(8,128)(2,1)} collective-permute-done((bf16[2064,256]{1,0:T(8,128)(2,1)}, bf16[2064,256]{1,0:T(8,128)(2,1)}, u32[]{:S(2)}, u32[]{:S(2)}) %collective-permute-start.16) | collective-permute-done | bytes 1056800 | tf_op jit(solution)/shard_map/ppermute | solution.py:340
  94.2 1.9 %slice.75 = bf16[1040,256]{1,0:T(8,128)(2,1)} slice(bf16[2064,256]{1,0:T(8,128)(2,1)} %collective-permute-done.16.rest_3_.rest_13_), slice={[1024:2064], [0:256]} | slice | bytes 1064960 | tf_op jit(solution)/shard_map/slice | solution.py:348
  96.4 2.0 %slice.74 = bf16[1024,256]{1,0:T(8,128)(2,1)} slice(bf16[2064,256]{1,0:T(8,128)(2,1)} %collective-permute-done.14.rest_1_.rest_11_), slice={[0:1024], [0:256]} | slice | bytes 1048576 | tf_op jit(solution)/shard_map/slice | solution.py:347
  99.3 4.3 %collective-permute-start.18 = (bf16[1024,256]{1,0:T(8,128)(2,1)}, bf16[1024,256]{1,0:T(8,128)(2,1)}, u32[]{:S(2)}, u32[]{:S(2)}) collective-permute-start(bf16[1024,256]{1,0:T(8,128)(2,1)} %slice.74), channel_id=1, source_target_pairs={{0,12},{1,13},{2,14},{3,15},{4,0},{5,1},{6,2},{7,3},{8,4},{9,5},{1... | collective-permute-start | bytes 1572872 | tf_op jit(solution)/shard_map/ppermute | solution.py:347
  104.6 9.0 %shard_map.103.rest_9_ = f32[1056,256]{1,0:T(8,128)} custom-call(s32[56]{0:T(128)} %reshape.236.slots_ref, s32[14]{0:T(128)} %convert_reduce_fusion.2.counts_ref, s32[1]{0:T(128)} %bitcast.18.starts_ref, bf16[32,32,4096]{2,1,0:T(8,128)(2,1)} %bitcast.86, bf16[2048,256]{1,0:T(8,128)(2,1)} %constant_dynamic-slice_fusion.1.rest_1_, ...), custom_call_target="tpu_custom_call" | custom-call | flops 1 | bytes 1 | tf_op jit(solution)/shard_map/pallas_call | solution.py:119
  119.4 10.8 %shard_map.106 = bf16[1056,256]{1,0:T(8,128)(2,1)} custom-call(s32[64]{0:T(128)} %reshape.239.slots_ref, s32[16]{0:T(128)} %get-tuple-element.22.counts_ref, s32[1]{0:T(128)} %bitcast.23.starts_ref, bf16[32,32,2048]{2,1,0:T(8,128)(2,1)} %collective-permute-done.21._.rest_0_, bf16[2048,256]{1,0:T(8,128)(2,1)} %constant_dynamic-slice_fusion.1.rest_1_, ...), custom_call_target="tpu_custom_call" | custom-call | flops 1 | bytes 1 | tf_op jit(solution)/shard_map/pallas_call | solution.py:119
  130.2 1.5 collective-permute-start.24
  132.3 7.5 %shard_map.105.own_ref = f32[1056,256]{1,0:T(8,128)} custom-call(s32[64]{0:T(128)} %reshape.238.slots_ref, s32[16]{0:T(128)} %get-tuple-element.23.counts_ref, s32[1]{0:T(128)} %bitcast.18.starts_ref, bf16[32,32,4096]{2,1,0:T(8,128)(2,1)} %bitcast.87, bf16[2064,256]{1,0:T(8,128)(2,1)} %collective-permute-done.14.rest_1_.rest_11_, ...), custom_call_target="tpu_custom_call" | custom-call | flops 1 | bytes 1 | tf_op jit(solution)/shard_map/pallas_call | solution.py:119
  140.3 5.8 %fusion = f32[1024]{0:T(1024)S(1)} fusion(bf16[16,4096]{1,0:T(8,128)(2,1)S(1)} %stack.97, bf16[1024,4096]{1,0:T(8,128)(2,1)} %bitcast.88, s32[1024]{0:T(1024)S(1)} %eq.127, s32[16]{0:T(128)S(1)} %stack.94), kind=kOutput, calls=%fused_computation.2 | convolution fusion | flops 134265856 | bytes 8527936 | tf_op jit(solution)/shard_map/dot_general | solution.py:376
  148.5 4.1 %collective-permute-done.26 = f32[88,256]{1,0:T(8,128)S(1)} collective-permute-done((f32[88,256]{1,0:T(8,128)S(1)}, f32[88,256]{1,0:T(8,128)S(1)}, u32[]{:S(2)}, u32[]{:S(2)}) %collective-permute-start.26) | collective-permute-done | bytes 90144 | tf_op jit(solution)/shard_map/ppermute | solution.py:419
  152.7 1.8 %collective-permute-start.27 = (f32[88,256]{1,0:T(8,128)S(1)}, f32[88,256]{1,0:T(8,128)S(1)}, u32[]{:S(2)}, u32[]{:S(2)}) collective-permute-start(f32[88,256]{1,0:T(8,128)S(1)} %add.91), channel_id=1, source_target_pairs={{0,2},{1,3},{2,0},{3,1},{4,6},{5,7},{6,4},{7,5},{8,10},{9,11},{10,... | collective-permute-start | bytes 270344 | tf_op jit(solution)/shard_map/ppermute | solution.py:424
  154.5 2.8 %collective-permute-done.27 = f32[88,256]{1,0:T(8,128)S(1)} collective-permute-done((f32[88,256]{1,0:T(8,128)S(1)}, f32[88,256]{1,0:T(8,128)S(1)}, u32[]{:S(2)}, u32[]{:S(2)}) %collective-permute-start.27) | collective-permute-done | bytes 90144 | tf_op jit(solution)/shard_map/ppermute | solution.py:424
  157.4 4.5 %collective-permute-done.28 = f32[88,256]{1,0:T(8,128)S(1)} collective-permute-done((f32[88,256]{1,0:T(8,128)S(1)}, f32[88,256]{1,0:T(8,128)S(1)}, u32[]{:S(2)}, u32[]{:S(2)}) %collective-permute-start.28) | collective-permute-done | bytes 90144 | tf_op jit(solution)/shard_map/ppermute | solution.py:424
  161.9 2.5 %collective-permute-start.29 = (f32[88,256]{1,0:T(8,128)S(1)}, f32[88,256]{1,0:T(8,128)S(1)}, u32[]{:S(2)}, u32[]{:S(2)}) collective-permute-start(f32[88,256]{1,0:T(8,128)S(1)} %add.93), channel_id=1, source_target_pairs={{0,8},{1,9},{2,10},{3,11},{4,12},{5,13},{6,14},{7,15},{8,0},{9,1},... | collective-permute-start | bytes 270344 | tf_op jit(solution)/shard_map/ppermute | solution.py:424
  164.4 3.0 %collective-permute-done.29 = f32[88,256]{1,0:T(8,128)S(1)} collective-permute-done((f32[88,256]{1,0:T(8,128)S(1)}, f32[88,256]{1,0:T(8,128)S(1)}, u32[]{:S(2)}, u32[]{:S(2)}) %collective-permute-start.29) | collective-permute-done | bytes 90144 | tf_op jit(solution)/shard_map/ppermute | solution.py:424
  168.8 9.8 %shard_map.108 = (f32[256,256]{1,0:T(8,128)}, f32[1,256]{1,0:T(1,128)}) custom-call(s32[1]{0:T(128)} %bitcast.22.last_ref, f32[88,256]{1,0:T(8,128)S(1)} %add.94.mine_ref, f32[88,256]{1,0:T(8,128)S(1)} %collective-permute-done.30.back_ref), custom_call_target="tpu_custom_call" | custom-call | tf_op jit(solution)/shard_map/pallas_call | solution.py:279
  (143 shorter events, 29.4 us)
Async XLA Ops:
  3.3 31.5 %collective-permute-start.8 = (bf16[2048,256]{1,0:T(8,128)(2,1)}, bf16[2048,256]{1,0:T(8,128)(2,1)}, u32[]{:S(2)}, u32[]{:S(2)}) collective-permute-start(bf16[2048,256]{1,0:T(8,128)(2,1)} %constant_dynamic-slice_fusion.1.rest_1_), channel_id=1, source_target_pairs={{0,12},{1,13},{2,14},{3,15},{4,0},{5,1},{6,2},{7,3},{8,4},{9,5},{1... | collective-permute-start | bytes 3145736 | tf_op jit(solution)/shard_map/ppermute | solution.py:332
  8.3 34.5 %collective-permute-start.5 = (bf16[2048,256]{1,0:T(8,128)(2,1)}, bf16[2048,256]{1,0:T(8,128)(2,1)}, u32[]{:S(2)}, u32[]{:S(2)}) collective-permute-start(bf16[2048,256]{1,0:T(8,128)(2,1)} %constant_dynamic-slice_fusion.1.rest_1_), channel_id=1, source_target_pairs={{0,2},{1,3},{2,0},{3,1},{4,6},{5,7},{6,4},{7,5},{8,10},{9,11},{10,... | collective-permute-start | bytes 3145736 | tf_op jit(solution)/shard_map/ppermute | solution.py:332
  9.8 6.3 %collective-permute-start = (s32[32]{0:T(128)S(1)}, s32[32]{0:T(128)S(1)}, u32[]{:S(2)}, u32[]{:S(2)}) collective-permute-start(s32[32]{0:T(128)S(1)} %bitcast.108), channel_id=1, source_target_pairs={{0,16},{16,0},{1,17},{17,1},{2,18},{18,2},{3,19},{19,3},{4,20},{20... | collective-permute-start | bytes 392 | tf_op jit(solution)/shard_map/ppermute | solution.py:313
  16.1 5.7 %collective-permute-start.1 = (f32[1,512]{1,0:T(1,128)S(1)}, f32[1,512]{1,0:T(1,128)S(1)}, u32[]{:S(2)}, u32[]{:S(2)}) collective-permute-start(f32[1,512]{1,0:T(1,128)S(1)} %get-tuple-element.24), channel_id=1, source_target_pairs={{0,1},{1,2},{2,3},{3,4},{4,5},{5,6},{6,7},{7,8},{8,9},{9,10},{10,1... | collective-permute-start | bytes 6152 | tf_op jit(solution)/shard_map/ppermute | solution.py:32
  17.4 4.4 %collective-permute-start.2 = (f32[1,512]{1,0:T(1,128)S(1)}, f32[1,512]{1,0:T(1,128)S(1)}, u32[]{:S(2)}, u32[]{:S(2)}) collective-permute-start(f32[1,512]{1,0:T(1,128)S(1)} %get-tuple-element.25), channel_id=1, source_target_pairs={{1,0},{2,1},{3,2},{4,3},{5,4},{6,5},{7,6},{8,7},{9,8},{10,9},{11,1... | collective-permute-start | bytes 6152 | tf_op jit(solution)/shard_map/ppermute | solution.py:33
  21.3 93.8 %collective-permute-start.21 = (bf16[32,32,2048]{2,1,0:T(8,128)(2,1)}, bf16[32,32,2048]{2,1,0:T(8,128)(2,1)}, u32[]{:S(2)}, u32[]{:S(2)}) collective-permute-start(bf16[32,32,2048]{2,1,0:T(8,128)(2,1)} %dynamic-slice_bitcast_fusion), channel_id=1, source_target_pairs={{0,16},{16,0},{1,17},{17,1},{2,18},{18,2},{3,19},{19,3},{4,20},{20... | collective-permute-start | bytes 12582920 | tf_op jit(solution)/shard_map/ppermute | solution.py:319
  25.1 13.1 %collective-permute-start.7 = (bf16[16,256]{1,0:T(8,128)(2,1)S(1)}, bf16[16,256]{1,0:T(8,128)(2,1)S(1)}, u32[]{:S(2)}, u32[]{:S(2)}) collective-permute-start(bf16[16,256]{1,0:T(8,128)(2,1)S(1)} %convert_element_type.57), channel_id=1, source_target_pairs={{0,12},{1,13},{2,14},{3,15},{4,0},{5,1},{6,2},{7,3},{8,4},{9,5},{1... | collective-permute-start | bytes 24584 | tf_op jit(solution)/shard_map/ppermute | solution.py:332
  38.2 26.0 %collective-permute-start.12 = (bf16[2064,256]{1,0:T(8,128)(2,1)S(1)}, bf16[2064,256]{1,0:T(8,128)(2,1)}, u32[]{:S(2)}, u32[]{:S(2)}) collective-permute-start(bf16[2064,256]{1,0:T(8,128)(2,1)S(1)} %constant_dynamic-update-slice_fusion.2.rest_5_), channel_id=1, source_target_pairs={{0,12},{1,13},{2,14},{3,15},{4,0},{5,1},{6,2},{7,3},{8,4},{9,5},{1... | collective-permute-start | bytes 3170312 | tf_op jit(solution)/shard_map/ppermute | solution.py:340
  40.6 32.7 %copy-start.7 = (f32[64,64]{1,0:T(8,128)S(1)}, f32[64,64]{1,0:T(8,128)}, u32[]{:S(2)}) copy-start(f32[64,64]{1,0:T(8,128)} %shard_map.102) | copy-start | bytes 49156
  40.6 5.0 %collective-permute-start.4 = (bf16[16,256]{1,0:T(8,128)(2,1)S(1)}, bf16[16,256]{1,0:T(8,128)(2,1)S(1)}, u32[]{:S(2)}, u32[]{:S(2)}) collective-permute-start(bf16[16,256]{1,0:T(8,128)(2,1)S(1)} %convert_element_type.57), channel_id=1, source_target_pairs={{0,2},{1,3},{2,0},{3,1},{4,6},{5,7},{6,4},{7,5},{8,10},{9,11},{10,... | collective-permute-start | bytes 24584 | tf_op jit(solution)/shard_map/ppermute | solution.py:332
  42.8 3.4 %collective-permute-start.3 = (bf16[16,256]{1,0:T(8,128)(2,1)S(1)}, bf16[16,256]{1,0:T(8,128)(2,1)S(1)}, u32[]{:S(2)}, u32[]{:S(2)}) collective-permute-start(bf16[16,256]{1,0:T(8,128)(2,1)S(1)} %convert_element_type.57), channel_id=1, source_target_pairs={{0,1},{1,0},{2,3},{3,2},{4,5},{5,4},{6,7},{7,6},{8,9},{9,8},{10,11... | collective-permute-start | bytes 24584 | tf_op jit(solution)/shard_map/ppermute | solution.py:328
  42.9 27.8 %collective-permute-start.10 = (bf16[2064,256]{1,0:T(8,128)(2,1)S(1)}, bf16[2064,256]{1,0:T(8,128)(2,1)}, u32[]{:S(2)}, u32[]{:S(2)}) collective-permute-start(bf16[2064,256]{1,0:T(8,128)(2,1)S(1)} %constant_dynamic-update-slice_fusion.2.rest_5_), channel_id=1, source_target_pairs={{0,2},{1,3},{2,0},{3,1},{4,6},{5,7},{6,4},{7,5},{8,10},{9,11},{10,... | collective-permute-start | bytes 3170312 | tf_op jit(solution)/shard_map/ppermute | solution.py:343
  46.2 24.5 %collective-permute-start.6 = (bf16[2064,256]{1,0:T(8,128)(2,1)}, bf16[2064,256]{1,0:T(8,128)(2,1)}, u32[]{:S(2)}, u32[]{:S(2)}) collective-permute-start(bf16[2064,256]{1,0:T(8,128)(2,1)} %constant_dynamic-update-slice_fusion.rest_3_), channel_id=1, source_target_pairs={{0,1},{1,0},{2,3},{3,2},{4,5},{5,4},{6,7},{7,6},{8,9},{9,8},{10,11... | collective-permute-start | bytes 3170312 | tf_op jit(solution)/shard_map/ppermute | solution.py:328
  46.3 27.2 %collective-permute-start.9 = (bf16[2064,256]{1,0:T(8,128)(2,1)S(1)}, bf16[2064,256]{1,0:T(8,128)(2,1)}, u32[]{:S(2)}, u32[]{:S(2)}) collective-permute-start(bf16[2064,256]{1,0:T(8,128)(2,1)S(1)} %constant_dynamic-update-slice_fusion.2.rest_5_), channel_id=1, source_target_pairs={{0,1},{1,0},{2,3},{3,2},{4,5},{5,4},{6,7},{7,6},{8,9},{9,8},{10,11... | collective-permute-start | bytes 3170312 | tf_op jit(solution)/shard_map/ppermute | solution.py:328
  64.2 27.1 %collective-permute-start.16 = (bf16[2064,256]{1,0:T(8,128)(2,1)}, bf16[2064,256]{1,0:T(8,128)(2,1)}, u32[]{:S(2)}, u32[]{:S(2)}) collective-permute-start(bf16[2064,256]{1,0:T(8,128)(2,1)} %collective-permute-done.12.rest_9_), channel_id=1, source_target_pairs={{0,12},{1,13},{2,14},{3,15},{4,0},{5,1},{6,2},{7,3},{8,4},{9,5},{1... | collective-permute-start | bytes 3170312 | tf_op jit(solution)/shard_map/ppermute | solution.py:340
  70.7 25.5 %collective-permute-start.14 = (bf16[2064,256]{1,0:T(8,128)(2,1)}, bf16[2064,256]{1,0:T(8,128)(2,1)}, u32[]{:S(2)}, u32[]{:S(2)}) collective-permute-start(bf16[2064,256]{1,0:T(8,128)(2,1)} %collective-permute-done.12.rest_9_), channel_id=1, source_target_pairs={{0,2},{1,3},{2,0},{3,1},{4,6},{5,7},{6,4},{7,5},{8,10},{9,11},{10,... | collective-permute-start | bytes 3170312 | tf_op jit(solution)/shard_map/ppermute | solution.py:343
  70.8 27.6 %collective-permute-start.11 = (bf16[2064,256]{1,0:T(8,128)(2,1)}, bf16[2064,256]{1,0:T(8,128)(2,1)}, u32[]{:S(2)}, u32[]{:S(2)}) collective-permute-start(bf16[2064,256]{1,0:T(8,128)(2,1)} %collective-permute-done.10.rest_7_), channel_id=1, source_target_pairs={{0,1},{1,0},{2,3},{3,2},{4,5},{5,4},{6,7},{7,6},{8,9},{9,8},{10,11... | collective-permute-start | bytes 3170312 | tf_op jit(solution)/shard_map/ppermute | solution.py:328
  73.5 25.8 %collective-permute-start.20 = (bf16[2048,256]{1,0:T(8,128)(2,1)}, bf16[2048,256]{1,0:T(8,128)(2,1)S(1)}, u32[]{:S(2)}, u32[]{:S(2)}) collective-permute-start(bf16[2048,256]{1,0:T(8,128)(2,1)} %constant_dynamic-slice_fusion.1.rest_1_), channel_id=1, source_target_pairs={{0,1},{1,0},{2,3},{3,2},{4,5},{5,4},{6,7},{7,6},{8,9},{9,8},{10,11... | collective-permute-start | bytes 3145736 | tf_op jit(solution)/shard_map/ppermute | solution.py:328
  91.3 12.2 %collective-permute-start.13 = (bf16[2064,256]{1,0:T(8,128)(2,1)}, bf16[2064,256]{1,0:T(8,128)(2,1)S(1)}, u32[]{:S(2)}, u32[]{:S(2)}) collective-permute-start(bf16[2064,256]{1,0:T(8,128)(2,1)} %collective-permute-done.12.rest_9_), channel_id=1, source_target_pairs={{0,1},{1,0},{2,3},{3,2},{4,5},{5,4},{6,7},{7,6},{8,9},{9,8},{10,11... | collective-permute-start | bytes 3170312 | tf_op jit(solution)/shard_map/ppermute | solution.py:328
  96.1 19.5 %collective-permute-start.19 = (bf16[1040,256]{1,0:T(8,128)(2,1)}, bf16[1040,256]{1,0:T(8,128)(2,1)S(1)}, u32[]{:S(2)}, u32[]{:S(2)}) collective-permute-start(bf16[1040,256]{1,0:T(8,128)(2,1)} %slice.75), channel_id=1, source_target_pairs={{0,2},{1,3},{2,0},{3,1},{4,6},{5,7},{6,4},{7,5},{8,10},{9,11},{10,... | collective-permute-start | bytes 1597448 | tf_op jit(solution)/shard_map/ppermute | solution.py:348
  98.4 17.8 %collective-permute-start.15 = (bf16[2064,256]{1,0:T(8,128)(2,1)}, bf16[2064,256]{1,0:T(8,128)(2,1)}, u32[]{:S(2)}, u32[]{:S(2)}) collective-permute-start(bf16[2064,256]{1,0:T(8,128)(2,1)} %collective-permute-done.14.rest_1_.rest_11_), channel_id=1, source_target_pairs={{0,1},{1,0},{2,3},{3,2},{4,5},{5,4},{6,7},{7,6},{8,9},{9,8},{10,11... | collective-permute-start | bytes 3170312 | tf_op jit(solution)/shard_map/ppermute | solution.py:328
  99.3 16.3 %collective-permute-start.18 = (bf16[1024,256]{1,0:T(8,128)(2,1)}, bf16[1024,256]{1,0:T(8,128)(2,1)}, u32[]{:S(2)}, u32[]{:S(2)}) collective-permute-start(bf16[1024,256]{1,0:T(8,128)(2,1)} %slice.74), channel_id=1, source_target_pairs={{0,12},{1,13},{2,14},{3,15},{4,0},{5,1},{6,2},{7,3},{8,4},{9,5},{1... | collective-permute-start | bytes 1572872 | tf_op jit(solution)/shard_map/ppermute | solution.py:347
  103.6 13.4 %collective-permute-start.17 = (bf16[2064,256]{1,0:T(8,128)(2,1)}, bf16[2064,256]{1,0:T(8,128)(2,1)}, u32[]{:S(2)}, u32[]{:S(2)}) collective-permute-start(bf16[2064,256]{1,0:T(8,128)(2,1)} %collective-permute-done.16.rest_3_.rest_13_), channel_id=1, source_target_pairs={{0,1},{1,0},{2,3},{3,2},{4,5},{5,4},{6,7},{7,6},{8,9},{9,8},{10,11... | collective-permute-start | bytes 3170312 | tf_op jit(solution)/shard_map/ppermute | solution.py:328
  115.6 3.0 %collective-permute-start.22 = (bf16[1040,256]{1,0:T(8,128)(2,1)S(1)}, bf16[1040,256]{1,0:T(8,128)(2,1)}, u32[]{:S(2)}, u32[]{:S(2)}) collective-permute-start(bf16[1040,256]{1,0:T(8,128)(2,1)S(1)} %collective-permute-done.19.rest_6_.rest_16_), channel_id=1, source_target_pairs={{0,1},{1,0},{2,3},{3,2},{4,5},{5,4},{6,7},{7,6},{8,9},{9,8},{10,11... | collective-permute-start | bytes 1597448 | tf_op jit(solution)/shard_map/ppermute | solution.py:328
  115.7 2.9 %collective-permute-start.23 = (bf16[1024,256]{1,0:T(8,128)(2,1)}, bf16[1024,256]{1,0:T(8,128)(2,1)S(1)}, u32[]{:S(2)}, u32[]{:S(2)}) collective-permute-start(bf16[1024,256]{1,0:T(8,128)(2,1)} %collective-permute-done.18.rest_5_.rest_15_), channel_id=1, source_target_pairs={{0,1},{1,0},{2,3},{3,2},{4,5},{5,4},{6,7},{7,6},{8,9},{9,8},{10,11... | collective-permute-start | bytes 1572872 | tf_op jit(solution)/shard_map/ppermute | solution.py:328
  130.2 15.9 %collective-permute-start.24 = (bf16[1056,256]{1,0:T(8,128)(2,1)}, bf16[1056,256]{1,0:T(8,128)(2,1)S(1)}, u32[]{:S(2)}, u32[]{:S(2)}) collective-permute-start(bf16[1056,256]{1,0:T(8,128)(2,1)} %shard_map.106), channel_id=1, source_target_pairs={{0,16},{16,0},{1,17},{17,1},{2,18},{18,2},{3,19},{19,3},{4,20},{20... | collective-permute-start | bytes 1622024 | tf_op jit(solution)/shard_map/ppermute | solution.py:397
  146.6 1.4 collective-permute-start.25
  147.9 4.7 %collective-permute-start.26 = (f32[88,256]{1,0:T(8,128)S(1)}, f32[88,256]{1,0:T(8,128)S(1)}, u32[]{:S(2)}, u32[]{:S(2)}) collective-permute-start(f32[88,256]{1,0:T(8,128)S(1)} %dynamic-slice_add_fusion), channel_id=1, source_target_pairs={{0,16},{16,0},{1,17},{17,1},{2,18},{18,2},{3,19},{19,3},{4,20},{20... | collective-permute-start | bytes 270344 | tf_op jit(solution)/shard_map/ppermute | solution.py:419
  152.7 4.6 %collective-permute-start.27 = (f32[88,256]{1,0:T(8,128)S(1)}, f32[88,256]{1,0:T(8,128)S(1)}, u32[]{:S(2)}, u32[]{:S(2)}) collective-permute-start(f32[88,256]{1,0:T(8,128)S(1)} %add.91), channel_id=1, source_target_pairs={{0,2},{1,3},{2,0},{3,1},{4,6},{5,7},{6,4},{7,5},{8,10},{9,11},{10,... | collective-permute-start | bytes 270344 | tf_op jit(solution)/shard_map/ppermute | solution.py:424
  157.3 4.6 %collective-permute-start.28 = (f32[88,256]{1,0:T(8,128)S(1)}, f32[88,256]{1,0:T(8,128)S(1)}, u32[]{:S(2)}, u32[]{:S(2)}) collective-permute-start(f32[88,256]{1,0:T(8,128)S(1)} %add.92), channel_id=1, source_target_pairs={{0,4},{1,5},{2,6},{3,7},{4,0},{5,1},{6,2},{7,3},{8,12},{9,13},{10,... | collective-permute-start | bytes 270344 | tf_op jit(solution)/shard_map/ppermute | solution.py:424
  161.9 5.5 %collective-permute-start.29 = (f32[88,256]{1,0:T(8,128)S(1)}, f32[88,256]{1,0:T(8,128)S(1)}, u32[]{:S(2)}, u32[]{:S(2)}) collective-permute-start(f32[88,256]{1,0:T(8,128)S(1)} %add.93), channel_id=1, source_target_pairs={{0,8},{1,9},{2,10},{3,11},{4,12},{5,13},{6,14},{7,15},{8,0},{9,1},... | collective-permute-start | bytes 270344 | tf_op jit(solution)/shard_map/ppermute | solution.py:424
  167.4 1.4 collective-permute-start.30
  (13 other events, 109.3 us)
